TPU v7x, 256 devices: a whole 4x4x8 slice. The times are simulated.
256 devices in a mesh: row: 2 (over core), col: 4 (over x), depth: 32 (over z, y).
Axes of the slice: x: 4, y: 4, z: 8, core: 2. Of those that a mesh axis runs over, the one named last changes fastest.
Arguments:
- parent_block: float32 [32, 512, 512], P('depth', 'row', 'col')
- parent_right: float32 [32, 512, 3072], P('depth', 'row', 'col'), may hold values from -5 to 5
- parent_below: float32 [32, 3072, 512], P('depth', 'row', 'col'), may hold values from -5 to 5
- grand_block: float32 [32, 3072, 3072], P('depth', 'row', 'col'), may hold values from -6 to 6
- lower_parent: bfloat16 [32, 512, 512], P('depth', 'row', 'col'), may hold values from -0.75 to 0.75
- lower_grand: bfloat16 [32, 3072, 512], P('depth', 'row', 'col'), may hold values from -2 to 2
- upper_parent: bfloat16 [32, 512, 512], P('depth', 'row', 'col'), may hold values from -0.75 to 0.75
- upper_grand: bfloat16 [32, 512, 3072], P('depth', 'row', 'col'), may hold values from -2 to 2
- lower_inverse: bfloat16 [32, 512, 512], P('depth'), may hold values from -0.25 to 0.25
- upper_inverse: bfloat16 [32, 512, 512], P('depth'), may hold values from -0.25 to 0.25
- pivot_order: int32 [32, 512], P('depth'), may hold values from 0 to 511, each once within a row
- live_width: int32 [32], P('depth'), may hold values from 128 to 512, as said below
- tile_pattern: int32 [32, 24], P('depth'), may hold values 0 or 1
Outputs:
- grand_schur: float32 [32, 3072, 3072], P('depth', 'row', 'col')
Inputs may be any that keep to these rules, and one draw needn't show every extreme that they name: `live_width`: some layer has all 512 columns live and another only 128.
All inputs are finite; a program needn't handle non-finite values. No bound on the sum of `tile_pattern` on one device may be relied on, other than what follows from the above.
Results may differ from a plain program's by a relative error of at most 0.002.
Values may be sent and summed in bfloat16 or wider, within the bound.
No kernel may reach another device: no remote copies, remote signals or barrier semaphores. Data moves between devices by JAX's collectives and lax.ppermute only.
A program may use at most 64 MiB of HBM per device.

v0:
```python
import jax
import jax.numpy as jnp
from jax import lax
from jax.sharding import PartitionSpec as P

W = 512
P_SIZE = 512
TILE = 128
NEWTON = 3


def swapped(block, axis, bit):
    count = lax.axis_size(axis)
    route = []
    for low in range(count):
        high = low | 1 << bit
        if high != low and high < count:
            route += [(low, high), (high, low)]
    return lax.ppermute(block, axis, route)


def newton_inverse(matrix):
    inverse = jnp.eye(P_SIZE, dtype=jnp.float32) / jnp.diagonal(matrix)[None, :]
    for step in range(NEWTON):
        product = jnp.dot(matrix, inverse, precision=lax.Precision.HIGHEST)
        inverse = 2.0 * inverse - jnp.dot(inverse, product, precision=lax.Precision.HIGHEST)
    return inverse


def body(
    parent_block,
    parent_right,
    parent_below,
    grand_block,
    lower_parent,
    lower_grand,
    upper_parent,
    upper_grand,
    lower_inverse,
    upper_inverse,
    pivot_order,
    live_width,
    tile_pattern,
):
    row_count = lax.axis_size("row")
    col_count = lax.axis_size("col")
    row_index = lax.axis_index("row")
    col_index = lax.axis_index("col")
    tile_count = tile_pattern.shape[1]
    row_tiles = tile_count // row_count
    col_tiles = tile_count // col_count
    live = (jnp.arange(W, dtype=jnp.int32) < live_width[0]).astype(jnp.float32)
    row_live = jnp.repeat(
        lax.dynamic_slice_in_dim(tile_pattern[0], row_index * row_tiles, row_tiles), TILE
    ).astype(jnp.float32)
    col_live = jnp.repeat(
        lax.dynamic_slice_in_dim(tile_pattern[0], col_index * col_tiles, col_tiles), TILE
    ).astype(jnp.float32)
    solve_right = upper_inverse[0]
    factor = solve_right
    panel_parent = (
        jnp.dot(
            lax.all_gather(lower_parent[0], "col", axis=1, tiled=True),
            factor,
            preferred_element_type=jnp.float32,
        )
        * live[None, :]
    ).astype(jnp.bfloat16)
    panel_grand = (
        jnp.dot(
            lax.all_gather(lower_grand[0], "col", axis=1, tiled=True),
            factor,
            preferred_element_type=jnp.float32,
        )
        * live[None, :]
        * row_live[:, None]
    ).astype(jnp.bfloat16)
    full_parent, full_grand = (
        lax.all_gather(upper_parent[0], "row", axis=0, tiled=True),
        lax.all_gather(upper_grand[0], "row", axis=0, tiled=True),
    )
    order = pivot_order[0]
    solve_left = lower_inverse[0]
    upper_pivot = (
        jnp.dot(solve_left, full_parent[order], preferred_element_type=jnp.float32) * live[:, None]
    ).astype(jnp.bfloat16)
    upper_far = (
        jnp.dot(solve_left, full_grand[order], preferred_element_type=jnp.float32)
        * live[:, None]
        * col_live[None, :]
    ).astype(jnp.bfloat16)
    pivot_sum = parent_block[0] - jnp.dot(
        panel_parent, upper_pivot, preferred_element_type=jnp.float32
    )
    right_sum = parent_right[0] - jnp.dot(
        panel_parent, upper_far, preferred_element_type=jnp.float32
    )
    below_sum = parent_below[0] - jnp.dot(
        panel_grand, upper_pivot, preferred_element_type=jnp.float32
    )
    corner_sum = grand_block[0] - jnp.dot(
        panel_grand, upper_far, preferred_element_type=jnp.float32
    )
    sibling = swapped((pivot_sum, right_sum, below_sum, corner_sum), "depth", 0)
    corner_pair = corner_sum + sibling[3]
    right_piece = right_sum + sibling[1]
    pivot_pair = pivot_sum + sibling[0]
    below_pair = below_sum + sibling[2]
    pivot_rows = lax.all_gather(pivot_pair, "row", axis=0, tiled=True)
    pivot_whole = lax.all_gather(pivot_rows, "col", axis=1, tiled=True)
    inverse_b = newton_inverse(pivot_whole).astype(jnp.bfloat16)
    factor = inverse_b
    level_lower = jnp.dot(
        lax.all_gather(below_pair.astype(jnp.bfloat16), "col", axis=1, tiled=True),
        factor,
        preferred_element_type=jnp.float32,
    ).astype(jnp.bfloat16)
    update = jnp.dot(
        level_lower,
        lax.all_gather(right_piece.astype(jnp.bfloat16), "row", axis=0, tiled=True),
        preferred_element_type=jnp.float32,
    )
    level_sum = corner_pair - update
    result = level_sum + swapped(level_sum, "depth", 1)
    return result[None]


def solution(mesh):
    return jax.shard_map(
        body,
        mesh=mesh,
        in_specs=(
            P("depth", "row", "col"),
            P("depth", "row", "col"),
            P("depth", "row", "col"),
            P("depth", "row", "col"),
            P("depth", "row", "col"),
            P("depth", "row", "col"),
            P("depth", "row", "col"),
            P("depth", "row", "col"),
            P("depth", None, None),
            P("depth", None, None),
            P("depth", None),
            P("depth"),
            P("depth", None),
        ),
        out_specs=P("depth", "row", "col"),
        check_vma=False,
    )
```

profile of v0, /device:TPU:96, one launch (start us, length us, event | category | flops | bytes accessed | tf_op | source)
XLA Modules:
  0.0 350.0 jit_solution(13589630519883696339)
XLA Ops:
  8.0 2.1 all-gather.2
  12.1 2.4 all-gather.1
  14.5 2.0 gather_fusion
  17.8 26.0 %all-gather.12.cloned.1.call-done = bf16[1,1536,512]{2,1,0:T(8,128)(2,1)} async-done(((bf16[1,1536,128]{2,1,0:T(8,128)(2,1)}), bf16[1,1536,512]{2,1,0:T(8,128)(2,1)}) %all-gather.12.cloned.1.call-update) | async-done | bytes 1572880 | tf_op jit(solution)/shard_map/all_gather | solution.py:71
  43.8 2.4 fusion.1
  46.2 6.0 %bitcast_subtract_fusion = f32[1536,768]{1,0:T(8,128)} fusion(f32[1,1536,768]{2,1,0:T(8,128)} %param.16, bf16[1536,512]{1,0:T(8,128)(2,1)S(1)} %fusion.1, bf16[768,512]{1,0:T(8,128)(2,1)S(1)} %multiply_convert_fusion), kind=kOutput, calls=%fused_computation.3 | convolution fusion | flops 1209139200 | bytes 11796480 | tf_op jit(solution)/shard_map/dot_general | solution.py:101
  53.7 12.3 %all-gather.3 = bf16[1,256,512]{2,1,0:T(8,128)(2,1)S(1)} all-gather(bf16[1,256,128]{2,1,0:T(8,128)(2,1)S(1)} %copy-done.6), channel_id=5, replica_groups=mesh['row'=2,'col'=4,'depth'=32] {'col'}, dimensions={2}, use_global_device_ids=true | all-gather | bytes 327680 | tf_op jit(solution)/shard_map/all_gather | solution.py:63
  67.2 90.7 %collective-permute-done.2 = f32[256,128]{1,0:T(8,128)S(1)} collective-permute-done((f32[256,128]{1,0:T(8,128)S(1)}, f32[256,128]{1,0:T(8,128)S(1)}, u32[]{:S(2)}, u32[]{:S(2)}) %collective-permute-start.2) | collective-permute-done | bytes 131104 | tf_op jit(solution)/shard_map/ppermute | solution.py:19
  157.9 2.1 all_gather.29
  164.5 17.8 %collective-permute-done.1 = f32[1536,128]{1,0:T(8,128)S(1)} collective-permute-done((f32[1536,128]{1,0:T(8,128)S(1)}, f32[1536,128]{1,0:T(8,128)S(1)}, u32[]{:S(2)}, u32[]{:S(2)}) %collective-permute-start.1) | collective-permute-done | bytes 786464 | tf_op jit(solution)/shard_map/ppermute | solution.py:19
  183.2 15.2 %collective-permute-done.3 = f32[256,768]{1,0:T(8,128)S(1)} collective-permute-done((f32[256,768]{1,0:T(8,128)S(1)}, f32[256,768]{1,0:T(8,128)S(1)}, u32[]{:S(2)}, u32[]{:S(2)}) %collective-permute-start.3) | collective-permute-done | bytes 786464 | tf_op jit(solution)/shard_map/ppermute | solution.py:19
  198.5 2.4 all_gather.31
  200.9 8.9 %gather_fusion.2 = f32[512]{0:T(512)S(1)} fusion(f32[512,512]{1,0:T(8,128)} %all-gather.10.cloned.1.call-done, s32[512]{0:T(512)S(1)} %bitcast.66), kind=kCustom, calls=%fused_computation.2 | custom fusion | bytes 8192 | tf_op jit(solution)/shard_map/jit(diagonal)/cond/branch_0_fun/gather | solution.py:23
  209.8 1.8 fusion.7
  211.7 1.8 convolution_subtract_fusion.3
  213.5 1.8 fusion.16
  215.3 1.9 convolution_subtract_fusion.2
  217.2 1.9 fusion.17
  219.1 1.9 fusion.3
  221.0 4.2 %all-gather.8.cloned.1.call-done = bf16[1536,512]{1,0:T(8,128)(2,1)} async-done(((bf16[1536,128]{1,0:T(8,128)(2,1)}), bf16[1536,512]{1,0:T(8,128)(2,1)}) %all-gather.8.cloned.1.call-update) | async-done | bytes 1572880 | tf_op jit(solution)/shard_map/all_gather | solution.py:114
  225.2 8.8 %add_subtract_fusion = f32[1536,768]{1,0:T(8,128)} fusion(f32[1536,768]{1,0:T(8,128)} %bitcast_subtract_fusion, f32[1536,768]{1,0:T(8,128)} %collective-permute-done, bf16[512,768]{1,0:T(8,128)(2,1)S(1)} %all_gather.31, bf16[1536,512]{1,0:T(8,128)(2,1)} %all-gather.8.cloned.1.call-done, bf16[512,512]{1,0:T(8,128)(2,1)S(1)} %fusion.3), kind=kOutput, calls=%fused_computation.5 | convolution fusion | flops 2016411648 | bytes 17039360 | tf_op jit(solution)/shard_map/dot_general | solution.py:118
  234.0 3.0 collective-permute-start.4
  237.0 101.4 %collective-permute-done.4 = f32[1536,768]{1,0:T(8,128)S(1)} collective-permute-done((f32[1536,768]{1,0:T(8,128)}, f32[1536,768]{1,0:T(8,128)S(1)}, u32[]{:S(2)}, u32[]{:S(2)}) %collective-permute-start.4) | collective-permute-done | bytes 4718624 | tf_op jit(solution)/shard_map/ppermute | solution.py:19
  338.3 5.1 %add_bitcast_fusion = f32[1,1536,768]{2,1,0:T(8,128)} fusion(f32[1536,768]{1,0:T(8,128)} %add_subtract_fusion, f32[1536,768]{1,0:T(8,128)S(1)} %collective-permute-done.4), kind=kLoop, calls=%fused_computation.4 | loop fusion | flops 1179648 | bytes 14155776 | tf_op jit(solution)/shard_map/broadcast_in_dim | solution.py:125
  (46 shorter events, 12.1 us)
Async XLA Ops:
  6.5 37.2 %copy-start = (bf16[1,512,512]{2,1,0:T(8,128)(2,1)S(1)}, bf16[1,512,512]{2,1,0:T(8,128)(2,1)}, u32[]{:S(2)}) copy-start(bf16[1,512,512]{2,1,0:T(8,128)(2,1)} %param.22) | copy-start | bytes 1572868
  6.5 5.6 %copy-start.4 = (bf16[1,256,768]{2,1,0:T(8,128)(2,1)S(1)}, bf16[1,256,768]{2,1,0:T(8,128)(2,1)}, u32[]{:S(2)}) copy-start(bf16[1,256,768]{2,1,0:T(8,128)(2,1)} %param.20) | copy-start | bytes 1179652
  6.5 37.2 %all-gather.12.cloned.1.call-start = ((), (), s32[]{:S(2)}) async-start(), calls=%async_computation.2 | async-start | bytes 1966080 | tf_op jit(solution)/shard_map/all_gather | solution.py:71
  7.3 193.6 %all-gather.10.cloned.1.call-start = ((), (), s32[]{:S(2)}) async-start(), calls=%async_computation.1 | async-start | bytes 1310720 | tf_op jit(solution)/shard_map/all_gather | solution.py:110
  14.5 2.0 copy-start.7
  14.5 2.3 copy-start.3
  46.2 7.5 %copy-start.6 = (bf16[1,256,128]{2,1,0:T(8,128)(2,1)S(1)}, bf16[1,256,128]{2,1,0:T(8,128)(2,1)}, u32[]{:S(2)}) copy-start(bf16[1,256,128]{2,1,0:T(8,128)(2,1)} %param.17) | copy-start | bytes 196612
  46.2 20.1 %copy-start.5 = (f32[1,256,128]{2,1,0:T(8,128)S(1)}, f32[1,256,128]{2,1,0:T(8,128)}, u32[]{:S(2)}) copy-start(f32[1,256,128]{2,1,0:T(8,128)} %param.13) | copy-start | bytes 393220
  52.2 173.0 %collective-permute-start = (f32[1536,768]{1,0:T(8,128)}, f32[1536,768]{1,0:T(8,128)}, u32[]{:S(2)}, u32[]{:S(2)}) collective-permute-start(f32[1536,768]{1,0:T(8,128)} %bitcast_subtract_fusion), channel_id=1, source_target_pairs={{0,1},{1,0},{2,3},{3,2},{4,5},{5,4},{6,7},{7,6},{8,9},{9,8},{10,11... | collective-permute-start | bytes 14155784 | tf_op jit(solution)/shard_map/ppermute | solution.py:19
  66.5 91.4 %collective-permute-start.2 = (f32[256,128]{1,0:T(8,128)S(1)}, f32[256,128]{1,0:T(8,128)S(1)}, u32[]{:S(2)}, u32[]{:S(2)}) collective-permute-start(f32[256,128]{1,0:T(8,128)S(1)} %convolution_subtract_fusion.5), channel_id=1, source_target_pairs={{0,1},{1,0},{2,3},{3,2},{4,5},{5,4},{6,7},{7,6},{8,9},{9,8},{10,11... | collective-permute-start | bytes 393224 | tf_op jit(solution)/shard_map/ppermute | solution.py:19
  160.1 65.1 %all-gather.8.cloned.1.call-start = ((), (), s32[]{:S(2)}) async-start(), calls=%async_computation | async-start | bytes 1966080 | tf_op jit(solution)/shard_map/all_gather | solution.py:114
  160.1 3.4 copy-start.2
  161.9 20.5 %collective-permute-start.1 = (f32[1536,128]{1,0:T(8,128)S(1)}, f32[1536,128]{1,0:T(8,128)S(1)}, u32[]{:S(2)}, u32[]{:S(2)}) collective-permute-start(f32[1536,128]{1,0:T(8,128)S(1)} %convolution_subtract_fusion), channel_id=1, source_target_pairs={{0,1},{1,0},{2,3},{3,2},{4,5},{5,4},{6,7},{7,6},{8,9},{9,8},{10,11... | collective-permute-start | bytes 2359304 | tf_op jit(solution)/shard_map/ppermute | solution.py:19
  163.9 34.6 %collective-permute-start.3 = (f32[256,768]{1,0:T(8,128)S(1)}, f32[256,768]{1,0:T(8,128)S(1)}, u32[]{:S(2)}, u32[]{:S(2)}) collective-permute-start(f32[256,768]{1,0:T(8,128)S(1)} %convolution_subtract_fusion.4), channel_id=1, source_target_pairs={{0,1},{1,0},{2,3},{3,2},{4,5},{5,4},{6,7},{7,6},{8,9},{9,8},{10,11... | collective-permute-start | bytes 2359304 | tf_op jit(solution)/shard_map/ppermute | solution.py:19
  200.9 8.9 %copy-start.1 = (f32[512,512]{1,0:T(8,128)S(1)}, f32[512,512]{1,0:T(8,128)}, u32[]{:S(2)}) copy-start(f32[512,512]{1,0:T(8,128)} %all-gather.10.cloned.1.call-done) | copy-start | bytes 3145732
  234.0 104.4 %collective-permute-start.4 = (f32[1536,768]{1,0:T(8,128)}, f32[1536,768]{1,0:T(8,128)S(1)}, u32[]{:S(2)}, u32[]{:S(2)}) collective-permute-start(f32[1536,768]{1,0:T(8,128)} %add_subtract_fusion), channel_id=1, source_target_pairs={{0,2},{2,0},{1,3},{3,1},{4,6},{6,4},{5,7},{7,5},{8,10},{10,8},{9,1... | collective-permute-start | bytes 14155784 | tf_op jit(solution)/shard_map/ppermute | solution.py:19
Sparse Core Ops, SparseCore 0:
  9.2 34.5 all-gather.11
  160.2 29.4 all-gather.9
  191.4 33.7 all-gather.7
where the time goes:
time: 352 us; the launch traced here: 350 us
  waiting for transfers between devices  256 us (73%)
  matrix products  31.8 us (9%)
  blocking collectives  21.3 us (6%)
  between operations  14 us (4%)
  local copies, waits for them, and re-layouts  12.5 us (4%)
  starting transfers between devices  7.44 us (2%)
  other arithmetic  6.91 us (2%)
    ppermute x5, waiting for transfers between devices, swapped(): return lax.ppermute(block, axis, route)  225 us
    all_gather x1, waiting for transfers between devices, body(): lax.all_gather(lower_grand[0], 'col', axis=1, tiled=True)  26 us
    all_gather x1, blocking collectives, body(): lax.all_gather(lower_parent[0], 'col', axis=1, tiled=True)  12.3 us
    gather x1, local copies, waits for them, and re-layouts, newton_inverse(): inverse = jnp.eye(P_SIZE, dtype=jnp.float32) / jnp.diagonal(matrix)[None, :]  8.93 us
    dot_general x1, matrix products, body(): jnp.dot(level_lower, lax.all_gather(right_piece.astype(jnp.bfloat16), 'ro...  8.76 us
    ppermute x5, starting transfers between devices, swapped(): return lax.ppermute(block, axis, route)  7.36 us
  transfers between devices with their start and end apart: 8, of which 6 were waited for; matrix products, arithmetic and copies ran while one was open for 8% of the time, Pallas kernels for 0%

commit v1 on v0

v1 whole, which is shorter than its diff:
```python
import jax
import jax.numpy as jnp
from jax import lax
from jax.experimental import pallas as pl
from jax.experimental.pallas import tpu as pltpu
from jax.sharding import PartitionSpec as P

TILE = 128
NEWTON = 3
COLUMNS = 256
RING = (0, 1, 3, 2)
F32 = jnp.float32
BF16 = jnp.bfloat16
I16 = jnp.int16
SCALARS = pl.BlockSpec(memory_space=pltpu.SMEM)


def swapped(block, axis, mask):
    route = [(low, low ^ mask) for low in range(lax.axis_size(axis))]
    return lax.ppermute(block, axis, route)


def ring_gather(block, axis):
    return [swapped(block, axis, mask) for mask in RING[1:]]


def dot(left, right):
    return jnp.dot(left, right, preferred_element_type=F32)


def call(kernel, outs, args, specs=None, grid=None, out_specs=None, scratch=(), flops=0, aliases=None):
    size = sum(a.size * a.dtype.itemsize for a in list(args) + list(outs))
    more = {}
    if grid is not None:
        more = dict(grid=grid, out_specs=out_specs)
    if specs is not None:
        more["in_specs"] = specs
    if aliases is not None:
        more["input_output_aliases"] = aliases
    return pl.pallas_call(
        kernel,
        out_shape=list(outs),
        scratch_shapes=list(scratch),
        compiler_params=pltpu.CompilerParams(vmem_limit_bytes=40 * 2**20),
        cost_estimate=pl.CostEstimate(flops=flops, bytes_accessed=size, transcendentals=0),
        **more,
    )(*args)


def shape(dims, dtype):
    return jax.ShapeDtypeStruct(dims, dtype)


def start_at(block, size):
    return pl.ds(pl.multiple_of(block * size, size), size)


def iota(dims, axis):
    return lax.broadcasted_iota(jnp.int32, dims, axis)


def encode(block, coded_ref):
    rows = block.shape[0]
    most = jnp.maximum(jnp.max(jnp.abs(block), axis=0, keepdims=True), 1e-30)
    power = jnp.ceil(jnp.log2(most) + 0.01)
    scale = 0.98 * jnp.exp2(15.0 - power)
    coded_ref[:rows, :] = jnp.round(block * scale).astype(jnp.int32).astype(I16)
    coded_ref[rows:, :] = jnp.broadcast_to(power, (16, block.shape[1])).astype(jnp.int32).astype(I16)


def decode(coded_ref):
    rows = coded_ref.shape[0] - 16
    power = coded_ref[rows:, :].astype(jnp.int32).astype(F32)[:1, :]
    scale = jnp.exp2(power - 15.0) * (1.0 / 0.98)
    return coded_ref[:rows, :].astype(jnp.int32).astype(F32) * scale


def leaf_parent_kernel(
    at, live, tiles, order, upper_inverse, lower_inverse, pivot_own, pivot_across, far_own, far_across,
    lower_0, lower_1, lower_3, lower_2, parent_block, parent_right,
    solve_right, strip, give, keep, solve_left, right,
):
    row, col, g = at[0], at[1], at[2]
    width = lower_0.shape[1]
    size = upper_inverse.shape[0]
    half_k = far_own.shape[0]
    wide = far_own.shape[1]
    shown = iota((width, size), 1) < live[0]
    for k, mask in enumerate(RING):
        block = upper_inverse[start_at(col ^ mask, width), :].astype(F32)
        solve_right[k * width : (k + 1) * width, :] = jnp.where(shown, block, 0.0).astype(BF16)
    chosen = jnp.where(iota((size, size), 0) == order[...], 1.0, 0.0).astype(BF16)
    masked = jnp.where(iota((size, size), 0) < live[0], lower_inverse[...].astype(F32), 0.0).astype(BF16)
    solve_left[...] = lax.dot_general(
        masked, chosen, (((1,), (1,)), ((), ())), preferred_element_type=F32
    ).astype(BF16)
    left_own = solve_left[:, start_at(row, half_k)]
    left_across = solve_left[:, start_at(1 - row, half_k)]
    count = wide // TILE
    far = dot(left_own, far_own[...]) + dot(left_across, far_across[...])
    for t in range(count):
        flag = tiles[0, col * count + t].astype(F32)
        strip[:, t * TILE : (t + 1) * TILE] = (far[:, t * TILE : (t + 1) * TILE] * flag).astype(BF16)
    strip[:, wide:] = (dot(left_own, pivot_own[...]) + dot(left_across, pivot_across[...])).astype(BF16)
    lower = jnp.concatenate([lower_0[...], lower_1[...], lower_3[...], lower_2[...]], axis=1)
    panel = dot(lower, solve_right[...]).astype(BF16)
    right[...] = parent_right[...] - dot(panel, strip[:, :wide])
    pivot = parent_block[...] - dot(panel, strip[:, wide:])
    rows = right.shape[0] // 2
    give[:, :wide] = right[start_at(1 - g, rows), :]
    keep[:, :wide] = right[start_at(g, rows), :]
    for ref in (give, keep):
        ref[:, wide : wide + width] = pivot[:rows, :]
        ref[:, wide + width :] = pivot[rows:, :]


def parent_pair_kernel(keep, came, pivot, right):
    rows, wide = right.shape
    total = keep[...] + came[...]
    right[...] = total[:, :wide].astype(BF16)
    pivot[:rows, :] = total[:, wide : wide + TILE]
    pivot[rows:, :] = total[:, wide + TILE :]


def leaf_grand_kernel(part, at, tiles, lower_0, lower_1, lower_3, lower_2, solve_right, strip, parent_below, grand, *rest):
    if part == 0:
        corner, coded, below, panel = rest
    else:
        before, corner, coded, give, keep, panel = rest
    row, g = at[0], at[2]
    j = pl.program_id(0)
    wide = strip.shape[1] - TILE

    @pl.when(j == 0)
    def _():
        lower = jnp.concatenate([lower_0[...], lower_1[...], lower_3[...], lower_2[...]], axis=1)
        whole = dot(lower, solve_right[...])
        count = whole.shape[0] // TILE
        for t in range(count):
            flag = tiles[0, (row * 2 + part) * count + t].astype(F32)
            panel[t * TILE : (t + 1) * TILE, :] = (whole[t * TILE : (t + 1) * TILE, :] * flag).astype(BF16)
        found = parent_below[...] - dot(panel[...], strip[:, wide:])
        if part == 0:
            below[...] = found
        else:
            give[...] = jnp.where(g == 0, found, before[...])
            keep[...] = jnp.where(g == 0, before[...], found)

    block = grand[...] - dot(panel[...], strip[:, pl.ds(pl.multiple_of(j * COLUMNS, COLUMNS), COLUMNS)])
    corner[...] = block
    encode(block, coded)


def corner_pair_kernel(corner, came, total, coded):
    block = corner[...] + decode(came)
    total[...] = block
    encode(block, coded)


def newton_kernel(at, block_0, block_1, block_3, block_2, out, matrix, inverse):
    col = at[1]
    size = matrix.shape[0]
    for mask, block in zip(RING, (block_0, block_1, block_3, block_2)):
        matrix[:, start_at(col ^ mask, block.shape[1])] = block[...]
    where = iota((size, size), 0) == iota((size, size), 1)
    only = jnp.where(where, matrix[...], 0.0)
    by_row = 1.0 / jnp.sum(only, axis=1, keepdims=True)
    by_col = 1.0 / jnp.sum(only, axis=0, keepdims=True)
    inverse[...] = jnp.where(where, 2.0 * by_col, 0.0) - by_row * (matrix[...] * by_col)
    for step in range(NEWTON - 1):
        held = inverse[...]
        product = jnp.dot(matrix[...], held, precision=lax.Precision.HIGHEST, preferred_element_type=F32)
        inverse[...] = 2.0 * held - jnp.dot(held, product, precision=lax.Precision.HIGHEST, preferred_element_type=F32)
    out[...] = inverse[...].astype(BF16)


def level_lower_kernel(which, at, block_0, block_1, block_3, block_2, inverse_own, inverse_came, out, inverse):
    row, col = at[0], at[1]

    @pl.when(pl.program_id(0) == 0)
    def _():
        for k, mask in enumerate(RING):
            here = slice(k * TILE, (k + 1) * TILE)

            @pl.when(row == which)
            def _():
                inverse[here, :] = inverse_own[start_at(col ^ mask, TILE), :]

            @pl.when(row != which)
            def _():
                inverse[here, :] = inverse_came[start_at(col ^ mask, TILE), :]

    whole = jnp.concatenate([block_0[...], block_1[...], block_3[...], block_2[...]], axis=1)
    out[...] = dot(whole, inverse[...]).astype(BF16)


def right_kernel(at, own, across, out):
    row, g = at[0], at[2]
    rows = own.shape[0] // 4
    for ref, core in ((own, row), (across, 1 - row)):
        for k in range(4):
            half = g if k % 2 == 0 else 1 - g
            out[start_at((k // 2) * 4 + core * 2 + half, rows), :] = ref[k * rows : (k + 1) * rows, :]


def final_kernel(at, total, came, lower_mine, lower_other, right, *rest):
    out = rest[-1]
    size = lower_mine.shape[1]
    update = dot(lower_mine[...], right[:size, :]) + dot(lower_other[...], right[size:, :])
    out[...] = total[...] + decode(came) - update


def body(
    parent_block,
    parent_right,
    parent_below,
    grand_block,
    lower_parent,
    lower_grand,
    upper_parent,
    upper_grand,
    lower_inverse,
    upper_inverse,
    pivot_order,
    live_width,
    tile_pattern,
):
    row_index = lax.axis_index("row")
    col_index = lax.axis_index("col")
    depth_index = lax.axis_index("depth")
    h = (depth_index >> 1) & 1
    g = (depth_index ^ (depth_index >> 1)) & 1
    at = jnp.stack([row_index, col_index, g, h])
    size = upper_inverse.shape[2]
    rows, wide = grand_block.shape[1:]
    width = lower_grand.shape[2]
    part_rows = rows // 2
    strips = wide // COLUMNS

    parents = ring_gather(lower_parent[0], "col")
    across_pivot = swapped(upper_parent[0], "row", 1)
    across_far = swapped(upper_grand[0], "row", 1)
    grands = ring_gather(lower_grand[0], "col")
    solve_right, strip, give, keep = call(
        leaf_parent_kernel,
        [
            shape((size, size), BF16),
            shape((size, wide + width), BF16),
            shape((parent_right.shape[1] // 2, wide + 2 * width), F32),
            shape((parent_right.shape[1] // 2, wide + 2 * width), F32),
        ],
        [
            at, live_width, tile_pattern, pivot_order, upper_inverse[0], lower_inverse[0],
            upper_parent[0], across_pivot, upper_grand[0], across_far,
            lower_parent[0], *parents, parent_block[0], parent_right[0],
        ],
        specs=[SCALARS] * 3 + [pl.BlockSpec(memory_space=pltpu.VMEM)] * 13,
        scratch=[pltpu.VMEM((size, size), BF16), pltpu.VMEM(parent_right.shape[1:], F32)],
        flops=2 * size * size * (size + wide + width),
    )

    came = swapped(give, "depth", 1)
    pivot_mine, right_own = call(
        parent_pair_kernel,
        [shape(parent_block.shape[1:], F32), shape((parent_right.shape[1] // 2, wide), BF16)],
        [keep, came],
    )
    pivot_other = swapped(pivot_mine, "depth", 3)
    right_sibling = swapped(right_own, "depth", 1)
    right_pair = jnp.concatenate([right_own, right_sibling], axis=0)
    right_four = jnp.concatenate([right_pair, swapped(right_pair, "depth", 3)], axis=0)

    def leaf_grand(part, before):
        outs = [shape((part_rows, wide), F32), shape((part_rows + 16, wide), I16)]
        below_spec = pl.BlockSpec((part_rows, width), lambda j: (0, 0))
        here_spec = pl.BlockSpec((part_rows, width), lambda j: (part, 0))
        out_specs = [
            pl.BlockSpec((part_rows, COLUMNS), lambda j: (0, j)),
            pl.BlockSpec((part_rows + 16, COLUMNS), lambda j: (0, j)),
        ]
        count = 1 if part == 0 else 2
        return call(
            lambda *refs: leaf_grand_kernel(part, *refs),
            outs + [shape((part_rows, width), F32)] * count,
            [at, tile_pattern, lower_grand[0], *grands, solve_right, strip, parent_below[0], grand_block[0], *before],
            specs=[SCALARS] * 2
            + [here_spec] * 4
            + [
                pl.BlockSpec((size, size), lambda j: (0, 0)),
                pl.BlockSpec((size, wide + width), lambda j: (0, 0)),
                here_spec,
                pl.BlockSpec((part_rows, COLUMNS), lambda j: (part, j)),
            ]
            + [below_spec] * len(before),
            grid=(strips,),
            out_specs=out_specs + [below_spec] * count,
            scratch=[pltpu.VMEM((part_rows, size), BF16)],
            flops=2 * part_rows * size * (size + wide + width),
        )

    corner_0, coded_0, below_0 = leaf_grand(0, [])
    corner_1, coded_1, below_give, below_keep = leaf_grand(1, [below_0])

    def corner_pair(corner, coded):
        return call(
            corner_pair_kernel,
            [shape((part_rows, wide), F32), shape((part_rows + 16, wide), I16)],
            [corner, coded],
            specs=[
                pl.BlockSpec((part_rows, COLUMNS), lambda j: (0, j)),
                pl.BlockSpec((part_rows + 16, COLUMNS), lambda j: (0, j)),
            ],
            grid=(strips,),
            out_specs=[
                pl.BlockSpec((part_rows, COLUMNS), lambda j: (0, j)),
                pl.BlockSpec((part_rows + 16, COLUMNS), lambda j: (0, j)),
            ],
        )

    came_0 = swapped(coded_0, "depth", 3)
    below_came = swapped(below_give, "depth", 1)
    came_1 = swapped(coded_1, "depth", 1)
    below_own = (below_keep + below_came).astype(BF16)
    below_mine = jnp.concatenate([below_own, swapped(below_own, "depth", 1)], axis=0)
    below_other = swapped(below_mine, "depth", 3)
    pair_0, coded_0 = corner_pair(corner_0, came_0)
    pair_1, coded_1 = corner_pair(corner_1, came_1)
    came_0 = swapped(coded_0, "depth", 1)
    came_1 = swapped(coded_1, "depth", 3)

    first = row_index == 0
    traded = swapped(jnp.where(first, pivot_other, pivot_mine), "row", 1)
    kept = jnp.where(first, pivot_mine, pivot_other)
    pivot_rows = jnp.concatenate(
        [jnp.where(first, kept, traded), jnp.where(first, traded, kept)], axis=0
    )
    (inverse_own,) = call(
        newton_kernel,
        [shape((size, size), BF16)],
        [at, pivot_rows, *ring_gather(pivot_rows, "col")],
        specs=[SCALARS] + [pl.BlockSpec(memory_space=pltpu.VMEM)] * 4,
        scratch=[pltpu.VMEM((size, size), F32), pltpu.VMEM((size, size), F32)],
        flops=2 * 24 * size**3,
    )
    inverse_came = swapped(inverse_own, "row", 1)

    def level_lower(which, block):
        spec = pl.BlockSpec((part_rows, width), lambda i: (i, 0))
        whole = pl.BlockSpec((size, size), lambda i: (0, 0))
        return call(
            lambda *refs: level_lower_kernel(which, *refs),
            [shape((rows, size), BF16)],
            [at, block, *ring_gather(block, "col"), inverse_own, inverse_came],
            specs=[SCALARS] + [spec] * 4 + [whole] * 2,
            grid=(2,),
            out_specs=[pl.BlockSpec((part_rows, size), lambda i: (i, 0))],
            scratch=[pltpu.VMEM((size, size), BF16)],
            flops=2 * rows * size * size,
        )[0]

    lower_mine = level_lower(0, below_mine)
    lower_other = level_lower(1, below_other)
    (right_all,) = call(
        right_kernel,
        [shape((2 * size, wide), BF16)],
        [at, right_four, swapped(right_four, "row", 1)],
        specs=[SCALARS] + [pl.BlockSpec(memory_space=pltpu.VMEM)] * 2,
    )

    def final(part, total, came, before):
        lower_spec = pl.BlockSpec((part_rows, size), lambda j, at: (part ^ at[2], 0))
        args = [at, total, came, lower_mine, lower_other, right_all, *before]
        return pl.pallas_call(
            final_kernel,
            out_shape=shape((rows, wide), F32),
            grid_spec=pltpu.PrefetchScalarGridSpec(
                num_scalar_prefetch=1,
                grid=(strips,),
                in_specs=[
                    pl.BlockSpec((part_rows, COLUMNS), lambda j, at: (0, j)),
                    pl.BlockSpec((part_rows + 16, COLUMNS), lambda j, at: (0, j)),
                    lower_spec,
                    lower_spec,
                    pl.BlockSpec((2 * size, COLUMNS), lambda j, at: (0, j)),
                ]
                + [pl.BlockSpec(memory_space=pl.ANY)] * len(before),
                out_specs=pl.BlockSpec((part_rows, COLUMNS), lambda j, at: (part, j)),
            ),
            input_output_aliases={6: 0} if before else {},
            compiler_params=pltpu.CompilerParams(vmem_limit_bytes=40 * 2**20),
            cost_estimate=pl.CostEstimate(
                flops=4 * part_rows * size * wide, bytes_accessed=13 * part_rows * wide, transcendentals=0
            ),
        )(*args)

    result = final(0, pair_0, came_0, [])
    result = final(1, pair_1, came_1, [result])
    return result[None]


def solution(mesh):
    return jax.shard_map(
        body,
        mesh=mesh,
        in_specs=(
            P("depth", "row", "col"),
            P("depth", "row", "col"),
            P("depth", "row", "col"),
            P("depth", "row", "col"),
            P("depth", "row", "col"),
            P("depth", "row", "col"),
            P("depth", "row", "col"),
            P("depth", "row", "col"),
            P("depth", None, None),
            P("depth", None, None),
            P("depth", None),
            P("depth"),
            P("depth", None),
        ),
        out_specs=P("depth", "row", "col"),
        check_vma=False,
    )
```

time: 352 us -> 176 us (0.50)
  waiting for transfers between devices: 256 us -> 82.3 us
  Pallas kernels: 0 us -> 38.1 us
  matrix products: 31.8 us -> 0 us
  starting transfers between devices: 7.44 us -> 38.7 us
  blocking collectives: 21.3 us -> 0 us
  between operations: 14 us -> 0.9 us
  other arithmetic: 6.91 us -> 1.23 us
    ppermute x5 -> x31, waiting for transfers between devices: 225 us -> 82.3 us  [swapped(): return lax.ppermute(block, axis, route)]
    pallas_call x0 -> x12, Pallas kernels: none -> 38.1 us  [the longest x10 30.6 us: call(): pl.pallas_call(kernel, out_shape=list(outs), scratch_shapes=list(scratch)...]
    dot_general x15 -> x0, matrix products: 31.8 us -> none  [the longest x1 8.76 us: body(): jnp.dot(level_lower, lax.all_gather(right_piece.astype(jnp.bfloat16), 'ro...]
    ppermute x5 -> x31, starting transfers between devices: 7.36 us -> 38.7 us  [swapped(): return lax.ppermute(block, axis, route)]
    all_gather x3 -> x0, waiting for transfers between devices: 30.2 us -> none  [the longest x1 26 us: body(): lax.all_gather(lower_grand[0], 'col', axis=1, tiled=True)]
    all_gather x5 -> x0, blocking collectives: 21.3 us -> none  [the longest x1 12.3 us: body(): lax.all_gather(lower_parent[0], 'col', axis=1, tiled=True)]
    unnamed x16 -> x36, local copies, waits for them, and re-layouts: 0.04 us -> 14.5 us
    gather x3 -> x0, local copies, waits for them, and re-layouts: 12.3 us -> none  [the longest x1 8.93 us: newton_inverse(): inverse = jnp.eye(P_SIZE, dtype=jnp.float32) / jnp.diagonal(matrix)[None, :]]
  transfers between devices with their start and end apart: 8 -> 31, of which waited for: 6 -> 14; matrix products, arithmetic and copies ran while one was open for 8% -> 1% of each run, Pallas kernels for 0% -> 20%
where the time goes in v1:
time: 176 us
  waiting for transfers between devices  82.3 us (47%)
  starting transfers between devices  38.7 us (22%)
  Pallas kernels  38.1 us (22%)
  local copies, waits for them, and re-layouts  14.5 us (8%)
    ppermute x31, waiting for transfers between devices, swapped(): return lax.ppermute(block, axis, route)  82.3 us
    ppermute x31, starting transfers between devices, swapped(): return lax.ppermute(block, axis, route)  38.7 us
    pallas_call x10, Pallas kernels, call(): pl.pallas_call(kernel, out_shape=list(outs), scratch_shapes=list(scratch)...  30.6 us
    unnamed x36, local copies, waits for them, and re-layouts  14.5 us
    pallas_call x2, Pallas kernels, final(): pl.pallas_call(final_kernel, out_shape=shape((rows, wide), F32), grid_spe...  7.5 us
  transfers between devices with their start and end apart: 31, of which 14 were waited for; matrix products, arithmetic and copies ran while one was open for 1% of the time, Pallas kernels for 20%

profile of v1, /device:TPU:96, one launch (start us, length us, event | category | flops | bytes accessed | tf_op | source)
XLA Modules:
  0.0 175.7 jit_solution(12289648633969529445)
XLA Ops:
  0.0 3.0 %collective-permute-start.2 = (bf16[1536,128]{1,0:T(8,128)(2,1)}, bf16[1536,128]{1,0:T(8,128)(2,1)S(1)}, u32[]{:S(2)}, u32[]{:S(2)}) collective-permute-start(bf16[1536,128]{1,0:T(8,128)(2,1)} %bitcast.19), channel_id=1, source_target_pairs={{0,64},{32,96},{64,0},{96,32},{1,65},{33,97},{65,1},{97,33},{2,66}... | collective-permute-start | bytes 1179656 | tf_op jit(solution)/shard_map/ppermute | solution.py:20
  4.2 3.6 %collective-permute-start.7 = (bf16[256,128]{1,0:T(8,128)(2,1)}, bf16[256,128]{1,0:T(8,128)(2,1)S(1)}, u32[]{:S(2)}, u32[]{:S(2)}) collective-permute-start(bf16[256,128]{1,0:T(8,128)(2,1)} %bitcast.32), channel_id=1, source_target_pairs={{0,64},{32,96},{64,0},{96,32},{1,65},{33,97},{65,1},{97,33},{2,66}... | collective-permute-start | bytes 196616 | tf_op jit(solution)/shard_map/ppermute | solution.py:20
  7.7 15.4 %collective-permute-done.7.lower_2 = bf16[256,128]{1,0:T(8,128)(2,1)S(1)} collective-permute-done((bf16[256,128]{1,0:T(8,128)(2,1)}, bf16[256,128]{1,0:T(8,128)(2,1)S(1)}, u32[]{:S(2)}, u32[]{:S(2)}) %collective-permute-start.7) | collective-permute-done | bytes 65568 | tf_op jit(solution)/shard_map/ppermute | solution.py:20
  25.9 2.9 %collective-permute-done.6.lower_3 = bf16[256,128]{1,0:T(8,128)(2,1)S(1)} collective-permute-done((bf16[256,128]{1,0:T(8,128)(2,1)}, bf16[256,128]{1,0:T(8,128)(2,1)S(1)}, u32[]{:S(2)}, u32[]{:S(2)}) %collective-permute-start.6) | collective-permute-done | bytes 65568 | tf_op jit(solution)/shard_map/ppermute | solution.py:20
  29.7 3.5 %collective-permute-done.5.lower_1 = bf16[256,128]{1,0:T(8,128)(2,1)S(1)} collective-permute-done((bf16[256,128]{1,0:T(8,128)(2,1)}, bf16[256,128]{1,0:T(8,128)(2,1)S(1)}, u32[]{:S(2)}, u32[]{:S(2)}) %collective-permute-start.5) | collective-permute-done | bytes 65568 | tf_op jit(solution)/shard_map/ppermute | solution.py:20
  42.9 3.1 %shard_map.127 = (bf16[512,512]{1,0:T(8,128)(2,1)S(1)}, bf16[512,896]{1,0:T(8,128)(2,1)S(1)}, f32[128,1024]{1,0:T(8,128)}, f32[128,1024]{1,0:T(8,128)S(1)}) custom-call(s32[4]{0:T(128)S(1)} %pad_add_fusion.at.refs_0_, s32[1]{0:T(128)S(6)} %copy.18.live, s32[1,24]{1,0:T(1,128)S(1)} %copy-done.15, s32[1,512]{1,0:T(1,128)S(1)} %copy-done.16, ...), custom_call_target="tpu_custom_call" | custom-call | flops 738197504 | bytes 5638260 | tf_op jit(solution)/shard_map/pallas_call | solution.py:40
  50.7 4.2 %shard_map.128 = (f32[768,768]{1,0:T(8,128)S(1)}, s16[784,768]{1,0:T(8,128)(2,1)}, f32[768,128]{1,0:T(8,128)S(1)}) custom-call(s32[4]{0:T(128)S(1)} %pad_add_fusion.at.refs_0_, s32[1,24]{1,0:T(1,128)S(1)} %copy-done.15, bf16[1536,128]{1,0:T(8,128)(2,1)S(1)} %bitcast.22, bf16[1536,128]{1,0:T(8,128)(2,1)S(1)} %collective-permute-done.refs_3_, ...), custom_call_target="tpu_custom_call" | custom-call | flops 1107296256 | bytes 12476528 | tf_op jit(solution)/shard_map/pallas_call | solution.py:40
  56.3 4.4 %shard_map.129 = (f32[768,768]{1,0:T(8,128)S(1)}, s16[784,768]{1,0:T(8,128)(2,1)}, f32[768,128]{1,0:T(8,128)}, f32[768,128]{1,0:T(8,128)S(1)}) custom-call(s32[4]{0:T(128)S(1)} %pad_add_fusion.at.refs_0_, s32[1,24]{1,0:T(1,128)S(1)} %copy-done.15, bf16[1536,128]{1,0:T(8,128)(2,1)S(1)} %bitcast.23, bf16[1536,128]{1,0:T(8,128)(2,1)S(1)} %collective-permute-done.refs_3_, ...), custom_call_target="tpu_custom_call" | custom-call | flops 1107296256 | bytes 13262960 | tf_op jit(solution)/shard_map/pallas_call | solution.py:40
  61.9 3.0 %collective-permute-start.29 = (s16[784,768]{1,0:T(8,128)(2,1)}, s16[784,768]{1,0:T(8,128)(2,1)}, u32[]{:S(2)}, u32[]{:S(2)}) collective-permute-start(s16[784,768]{1,0:T(8,128)(2,1)} %get-tuple-element.36), channel_id=1, source_target_pairs={{0,3},{1,2},{2,1},{3,0},{4,7},{5,6},{6,5},{7,4},{8,11},{9,10},{10,... | collective-permute-start | bytes 3612680 | tf_op jit(solution)/shard_map/ppermute | solution.py:20
  68.3 5.3 %collective-permute-done.10 = f32[768,128]{1,0:T(8,128)S(1)} collective-permute-done((f32[768,128]{1,0:T(8,128)}, f32[768,128]{1,0:T(8,128)S(1)}, u32[]{:S(2)}, u32[]{:S(2)}) %collective-permute-start.10) | collective-permute-done | bytes 393248 | tf_op jit(solution)/shard_map/ppermute | solution.py:20
  76.8 17.4 %collective-permute-done.16 = f32[256,128]{1,0:T(8,128)S(1)} collective-permute-done((f32[256,128]{1,0:T(8,128)S(1)}, f32[256,128]{1,0:T(8,128)S(1)}, u32[]{:S(2)}, u32[]{:S(2)}) %collective-permute-start.16) | collective-permute-done | bytes 131104 | tf_op jit(solution)/shard_map/ppermute | solution.py:20
  94.3 9.4 %collective-permute-done.11 = bf16[768,128]{1,0:T(8,128)(2,1)S(1)} collective-permute-done((bf16[768,128]{1,0:T(8,128)(2,1)S(1)}, bf16[768,128]{1,0:T(8,128)(2,1)S(1)}, u32[]{:S(2)}, u32[]{:S(2)}) %collective-permute-start.11) | collective-permute-done | bytes 196640 | tf_op jit(solution)/shard_map/ppermute | solution.py:20
  109.6 2.8 %collective-permute-start.19 = (f32[512,128]{1,0:T(8,128)S(1)}, f32[512,128]{1,0:T(8,128)S(1)}, u32[]{:S(2)}, u32[]{:S(2)}) collective-permute-start(f32[512,128]{1,0:T(8,128)S(1)} %pad_maximum_fusion.2.block_0), channel_id=1, source_target_pairs={{0,96},{32,64},{64,32},{96,0},{1,97},{33,65},{65,33},{97,1},{2,98}... | collective-permute-start | bytes 786440 | tf_op jit(solution)/shard_map/ppermute | solution.py:20
  112.5 2.8 %shard_map.136 = (f32[768,768]{1,0:T(8,128)S(1)}, s16[784,768]{1,0:T(8,128)(2,1)S(1)}) custom-call(f32[768,768]{1,0:T(8,128)S(1)} %copy-done.3, s16[784,768]{1,0:T(8,128)(2,1)} %collective-permute-done.29.came), custom_call_target="tpu_custom_call" | custom-call | bytes 7127040 | tf_op jit(solution)/shard_map/pallas_call | solution.py:40
  121.8 3.5 %collective-permute-done.20.block_2 = f32[512,128]{1,0:T(8,128)S(1)} collective-permute-done((f32[512,128]{1,0:T(8,128)S(1)}, f32[512,128]{1,0:T(8,128)S(1)}, u32[]{:S(2)}, u32[]{:S(2)}) %collective-permute-start.20) | collective-permute-done | bytes 262176 | tf_op jit(solution)/shard_map/ppermute | solution.py:20
  125.2 2.8 %collective-permute-start.24 = (bf16[1536,128]{1,0:T(8,128)(2,1)S(1)}, bf16[1536,128]{1,0:T(8,128)(2,1)S(1)}, u32[]{:S(2)}, u32[]{:S(2)}) collective-permute-start(bf16[1536,128]{1,0:T(8,128)(2,1)S(1)} %collective-permute-done.22.refs_1_), channel_id=1, source_target_pairs={{0,96},{32,64},{64,32},{96,0},{1,97},{33,65},{65,33},{97,1},{2,98}... | collective-permute-start | bytes 1179656 | tf_op jit(solution)/shard_map/ppermute | solution.py:20
  128.0 3.3 %collective-permute-done.19.block_3 = f32[512,128]{1,0:T(8,128)S(1)} collective-permute-done((f32[512,128]{1,0:T(8,128)S(1)}, f32[512,128]{1,0:T(8,128)S(1)}, u32[]{:S(2)}, u32[]{:S(2)}) %collective-permute-start.19) | collective-permute-done | bytes 262176 | tf_op jit(solution)/shard_map/ppermute | solution.py:20
  132.7 8.1 %shard_map.132.refs_5_ = bf16[512,512]{1,0:T(8,128)(2,1)S(1)} custom-call(s32[4]{0:T(128)S(1)} %pad_add_fusion.at.refs_0_, f32[512,128]{1,0:T(8,128)S(1)} %pad_maximum_fusion.2.block_0, f32[512,128]{1,0:T(8,128)S(1)} %collective-permute-done.18.block_1, f32[512,128]{1,0:T(8,128)S(1)} %collective-permute-done.19.block_3, ...), custom_call_target="tpu_custom_call" | custom-call | flops 6442450944 | bytes 1572880 | tf_op jit(solution)/shard_map/pallas_call | solution.py:40
  141.4 2.8 %collective-permute-done.24.refs_3_ = bf16[1536,128]{1,0:T(8,128)(2,1)S(1)} collective-permute-done((bf16[1536,128]{1,0:T(8,128)(2,1)S(1)}, bf16[1536,128]{1,0:T(8,128)(2,1)S(1)}, u32[]{:S(2)}, u32[]{:S(2)}) %collective-permute-start.24) | collective-permute-done | bytes 393248 | tf_op jit(solution)/shard_map/ppermute | solution.py:20
  144.2 8.3 %collective-permute-done.23.refs_2_ = bf16[1536,128]{1,0:T(8,128)(2,1)S(1)} collective-permute-done((bf16[1536,128]{1,0:T(8,128)(2,1)S(1)}, bf16[1536,128]{1,0:T(8,128)(2,1)S(1)}, u32[]{:S(2)}, u32[]{:S(2)}) %collective-permute-start.23) | collective-permute-done | bytes 393248 | tf_op jit(solution)/shard_map/ppermute | solution.py:20
  152.5 2.8 %collective-permute-start.13 = (bf16[1536,128]{1,0:T(8,128)(2,1)S(1)}, bf16[1536,128]{1,0:T(8,128)(2,1)S(1)}, u32[]{:S(2)}, u32[]{:S(2)}) collective-permute-start(bf16[1536,128]{1,0:T(8,128)(2,1)S(1)} %pad_maximum_fusion.refs_1_), channel_id=1, source_target_pairs={{0,96},{32,64},{64,32},{96,0},{1,97},{33,65},{65,33},{97,1},{2,98}... | collective-permute-start | bytes 1179656 | tf_op jit(solution)/shard_map/ppermute | solution.py:20
  157.1 7.4 %collective-permute-done.13.refs_3_ = bf16[1536,128]{1,0:T(8,128)(2,1)S(1)} collective-permute-done((bf16[1536,128]{1,0:T(8,128)(2,1)S(1)}, bf16[1536,128]{1,0:T(8,128)(2,1)S(1)}, u32[]{:S(2)}, u32[]{:S(2)}) %collective-permute-start.13) | collective-permute-done | bytes 393248 | tf_op jit(solution)/shard_map/ppermute | solution.py:20
  168.2 3.8 %shard_map.137.rest_0_ = f32[1536,768]{1,0:T(8,128)} custom-call(s32[4]{0:T(128)S(1)} %pad_add_fusion.at.refs_0_, f32[768,768]{1,0:T(8,128)S(1)} %get-tuple-element.37.total, s16[784,768]{1,0:T(8,128)(2,1)S(1)} %collective-permute-done.30.came, bf16[1536,512]{1,0:T(8,128)(2,1)S(1)} %shard_map.133.lower_mine, bf16[1536,512]{1,0:T(8,128)(2,1)S(1)} %shard_map.134.lower_other, ...), custom_call_target="tpu_custom_call" | custom-call | flops 1207959552 | bytes 7667712 | tf_op jit(solution)/shard_map/pallas_call | solution.py:373
  172.0 3.7 %shard_map.138 = f32[1536,768]{1,0:T(8,128)} custom-call(s32[4]{0:T(128)S(1)} %pad_add_fusion.at.refs_0_, f32[768,768]{1,0:T(8,128)S(1)} %get-tuple-element.27.total, s16[784,768]{1,0:T(8,128)(2,1)S(1)} %collective-permute-done.9.came, bf16[1536,512]{1,0:T(8,128)(2,1)S(1)} %shard_map.133.lower_mine, ...), custom_call_target="tpu_custom_call", output_to_operand_aliasing={{}: (6, {})} | custom-call | flops 1207959552 | bytes 7667712 | tf_op jit(solution)/shard_map/pallas_call | solution.py:373
  (94 shorter events, 47.7 us)
Async XLA Ops:
  0.0 34.8 %collective-permute-start.4 = (bf16[256,768]{1,0:T(8,128)(2,1)}, bf16[256,768]{1,0:T(8,128)(2,1)S(1)}, u32[]{:S(2)}, u32[]{:S(2)}) collective-permute-start(bf16[256,768]{1,0:T(8,128)(2,1)} %bitcast.27), channel_id=1, source_target_pairs={{0,128},{128,0},{1,129},{129,1},{2,130},{130,2},{3,131},{131,3},{4... | collective-permute-start | bytes 1179656 | tf_op jit(solution)/shard_map/ppermute | solution.py:20
  0.0 48.3 %collective-permute-start.2 = (bf16[1536,128]{1,0:T(8,128)(2,1)}, bf16[1536,128]{1,0:T(8,128)(2,1)S(1)}, u32[]{:S(2)}, u32[]{:S(2)}) collective-permute-start(bf16[1536,128]{1,0:T(8,128)(2,1)} %bitcast.19), channel_id=1, source_target_pairs={{0,64},{32,96},{64,0},{96,32},{1,65},{33,97},{65,1},{97,33},{2,66}... | collective-permute-start | bytes 1179656 | tf_op jit(solution)/shard_map/ppermute | solution.py:20
  3.0 45.3 %collective-permute-start.1 = (bf16[1536,128]{1,0:T(8,128)(2,1)}, bf16[1536,128]{1,0:T(8,128)(2,1)S(1)}, u32[]{:S(2)}, u32[]{:S(2)}) collective-permute-start(bf16[1536,128]{1,0:T(8,128)(2,1)} %bitcast.20), channel_id=1, source_target_pairs={{0,96},{32,64},{64,32},{96,0},{1,97},{33,65},{65,33},{97,1},{2,98}... | collective-permute-start | bytes 1179656 | tf_op jit(solution)/shard_map/ppermute | solution.py:20
  4.2 44.2 %collective-permute-start = (bf16[1536,128]{1,0:T(8,128)(2,1)}, bf16[1536,128]{1,0:T(8,128)(2,1)S(1)}, u32[]{:S(2)}, u32[]{:S(2)}) collective-permute-start(bf16[1536,128]{1,0:T(8,128)(2,1)} %bitcast.21), channel_id=1, source_target_pairs={{0,32},{32,0},{64,96},{96,64},{1,33},{33,1},{65,97},{97,65},{2,34}... | collective-permute-start | bytes 1179656 | tf_op jit(solution)/shard_map/ppermute | solution.py:20
  4.2 18.9 %collective-permute-start.7 = (bf16[256,128]{1,0:T(8,128)(2,1)}, bf16[256,128]{1,0:T(8,128)(2,1)S(1)}, u32[]{:S(2)}, u32[]{:S(2)}) collective-permute-start(bf16[256,128]{1,0:T(8,128)(2,1)} %bitcast.32), channel_id=1, source_target_pairs={{0,64},{32,96},{64,0},{96,32},{1,65},{33,97},{65,1},{97,33},{2,66}... | collective-permute-start | bytes 196616 | tf_op jit(solution)/shard_map/ppermute | solution.py:20
  46.8 18.3 %collective-permute-start.15 = (f32[128,1024]{1,0:T(8,128)}, f32[128,1024]{1,0:T(8,128)}, u32[]{:S(2)}, u32[]{:S(2)}) collective-permute-start(f32[128,1024]{1,0:T(8,128)} %get-tuple-element.32), channel_id=1, source_target_pairs={{0,1},{1,0},{2,3},{3,2},{4,5},{5,4},{6,7},{7,6},{8,9},{9,8},{10,11... | collective-permute-start | bytes 1572872 | tf_op jit(solution)/shard_map/ppermute | solution.py:20
  61.4 12.2 %collective-permute-start.10 = (f32[768,128]{1,0:T(8,128)}, f32[768,128]{1,0:T(8,128)S(1)}, u32[]{:S(2)}, u32[]{:S(2)}) collective-permute-start(f32[768,128]{1,0:T(8,128)} %get-tuple-element.30), channel_id=1, source_target_pairs={{0,1},{1,0},{2,3},{3,2},{4,5},{5,4},{6,7},{7,6},{8,9},{9,8},{10,11... | collective-permute-start | bytes 1179656 | tf_op jit(solution)/shard_map/ppermute | solution.py:20
  61.9 47.8 %collective-permute-start.29 = (s16[784,768]{1,0:T(8,128)(2,1)}, s16[784,768]{1,0:T(8,128)(2,1)}, u32[]{:S(2)}, u32[]{:S(2)}) collective-permute-start(s16[784,768]{1,0:T(8,128)(2,1)} %get-tuple-element.36), channel_id=1, source_target_pairs={{0,3},{1,2},{2,1},{3,0},{4,7},{5,6},{6,5},{7,4},{8,11},{9,10},{10,... | collective-permute-start | bytes 3612680 | tf_op jit(solution)/shard_map/ppermute | solution.py:20
  64.9 47.5 %collective-permute-start.8 = (s16[784,768]{1,0:T(8,128)(2,1)}, s16[784,768]{1,0:T(8,128)(2,1)}, u32[]{:S(2)}, u32[]{:S(2)}) collective-permute-start(s16[784,768]{1,0:T(8,128)(2,1)} %get-tuple-element.26), channel_id=1, source_target_pairs={{0,1},{1,0},{2,3},{3,2},{4,5},{5,4},{6,7},{7,6},{8,9},{9,8},{10,11... | collective-permute-start | bytes 3612680 | tf_op jit(solution)/shard_map/ppermute | solution.py:20
  67.2 27.0 %collective-permute-start.16 = (f32[256,128]{1,0:T(8,128)S(1)}, f32[256,128]{1,0:T(8,128)S(1)}, u32[]{:S(2)}, u32[]{:S(2)}) collective-permute-start(f32[256,128]{1,0:T(8,128)S(1)} %get-tuple-element.33), channel_id=1, source_target_pairs={{0,3},{1,2},{2,1},{3,0},{4,7},{5,6},{6,5},{7,4},{8,11},{9,10},{10,... | collective-permute-start | bytes 393224 | tf_op jit(solution)/shard_map/ppermute | solution.py:20
  74.7 29.0 %collective-permute-start.11 = (bf16[768,128]{1,0:T(8,128)(2,1)S(1)}, bf16[768,128]{1,0:T(8,128)(2,1)S(1)}, u32[]{:S(2)}, u32[]{:S(2)}) collective-permute-start(bf16[768,128]{1,0:T(8,128)(2,1)S(1)} %add_convert_fusion), channel_id=1, source_target_pairs={{0,1},{1,0},{2,3},{3,2},{4,5},{5,4},{6,7},{7,6},{8,9},{9,8},{10,11... | collective-permute-start | bytes 589832 | tf_op jit(solution)/shard_map/ppermute | solution.py:20
  75.2 33.0 %collective-permute-start.26 = (bf16[128,768]{1,0:T(8,128)(2,1)S(1)}, bf16[128,768]{1,0:T(8,128)(2,1)S(1)}, u32[]{:S(2)}, u32[]{:S(2)}) collective-permute-start(bf16[128,768]{1,0:T(8,128)(2,1)S(1)} %get-tuple-element.34), channel_id=1, source_target_pairs={{0,1},{1,0},{2,3},{3,2},{4,5},{5,4},{6,7},{7,6},{8,9},{9,8},{10,11... | collective-permute-start | bytes 589832 | tf_op jit(solution)/shard_map/ppermute | solution.py:20
  103.7 14.3 %collective-permute-start.22 = (bf16[1536,128]{1,0:T(8,128)(2,1)S(1)}, bf16[1536,128]{1,0:T(8,128)(2,1)S(1)}, u32[]{:S(2)}, u32[]{:S(2)}) collective-permute-start(bf16[1536,128]{1,0:T(8,128)(2,1)S(1)} %pad_maximum_fusion.refs_1_), channel_id=1, source_target_pairs={{0,3},{1,2},{2,1},{3,0},{4,7},{5,6},{6,5},{7,4},{8,11},{9,10},{10,... | collective-permute-start | bytes 1179656 | tf_op jit(solution)/shard_map/ppermute | solution.py:20
  105.9 13.6 %collective-permute-start.14 = (bf16[1536,128]{1,0:T(8,128)(2,1)S(1)}, bf16[1536,128]{1,0:T(8,128)(2,1)S(1)}, u32[]{:S(2)}, u32[]{:S(2)}) collective-permute-start(bf16[1536,128]{1,0:T(8,128)(2,1)S(1)} %pad_maximum_fusion.refs_1_), channel_id=1, source_target_pairs={{0,64},{32,96},{64,0},{96,32},{1,65},{33,97},{65,1},{97,33},{2,66}... | collective-permute-start | bytes 1179656 | tf_op jit(solution)/shard_map/ppermute | solution.py:20
  108.2 17.0 %collective-permute-start.20 = (f32[512,128]{1,0:T(8,128)S(1)}, f32[512,128]{1,0:T(8,128)S(1)}, u32[]{:S(2)}, u32[]{:S(2)}) collective-permute-start(f32[512,128]{1,0:T(8,128)S(1)} %pad_maximum_fusion.2.block_0), channel_id=1, source_target_pairs={{0,64},{32,96},{64,0},{96,32},{1,65},{33,97},{65,1},{97,33},{2,66}... | collective-permute-start | bytes 786440 | tf_op jit(solution)/shard_map/ppermute | solution.py:20
  109.6 21.6 %collective-permute-start.19 = (f32[512,128]{1,0:T(8,128)S(1)}, f32[512,128]{1,0:T(8,128)S(1)}, u32[]{:S(2)}, u32[]{:S(2)}) collective-permute-start(f32[512,128]{1,0:T(8,128)S(1)} %pad_maximum_fusion.2.block_0), channel_id=1, source_target_pairs={{0,96},{32,64},{64,32},{96,0},{1,97},{33,65},{65,33},{97,1},{2,98}... | collective-permute-start | bytes 786440 | tf_op jit(solution)/shard_map/ppermute | solution.py:20
  112.4 19.5 %collective-permute-start.18 = (f32[512,128]{1,0:T(8,128)S(1)}, f32[512,128]{1,0:T(8,128)S(1)}, u32[]{:S(2)}, u32[]{:S(2)}) collective-permute-start(f32[512,128]{1,0:T(8,128)S(1)} %pad_maximum_fusion.2.block_0), channel_id=1, source_target_pairs={{0,32},{32,0},{64,96},{96,64},{1,33},{33,1},{65,97},{97,65},{2,34}... | collective-permute-start | bytes 786440 | tf_op jit(solution)/shard_map/ppermute | solution.py:20
  118.0 22.8 %collective-permute-start.27 = (bf16[256,768]{1,0:T(8,128)(2,1)S(1)}, bf16[256,768]{1,0:T(8,128)(2,1)S(1)}, u32[]{:S(2)}, u32[]{:S(2)}) collective-permute-start(bf16[256,768]{1,0:T(8,128)(2,1)S(1)} %pad_maximum_fusion.1), channel_id=1, source_target_pairs={{0,3},{1,2},{2,1},{3,0},{4,7},{5,6},{6,5},{7,4},{8,11},{9,10},{10,... | collective-permute-start | bytes 1179656 | tf_op jit(solution)/shard_map/ppermute | solution.py:20
  119.5 21.4 %collective-permute-start.25 = (bf16[1536,128]{1,0:T(8,128)(2,1)S(1)}, bf16[1536,128]{1,0:T(8,128)(2,1)S(1)}, u32[]{:S(2)}, u32[]{:S(2)}) collective-permute-start(bf16[1536,128]{1,0:T(8,128)(2,1)S(1)} %collective-permute-done.22.refs_1_), channel_id=1, source_target_pairs={{0,64},{32,96},{64,0},{96,32},{1,65},{33,97},{65,1},{97,33},{2,66}... | collective-permute-start | bytes 1179656 | tf_op jit(solution)/shard_map/ppermute | solution.py:20
  125.2 19.0 %collective-permute-start.24 = (bf16[1536,128]{1,0:T(8,128)(2,1)S(1)}, bf16[1536,128]{1,0:T(8,128)(2,1)S(1)}, u32[]{:S(2)}, u32[]{:S(2)}) collective-permute-start(bf16[1536,128]{1,0:T(8,128)(2,1)S(1)} %collective-permute-done.22.refs_1_), channel_id=1, source_target_pairs={{0,96},{32,64},{64,32},{96,0},{1,97},{33,65},{65,33},{97,1},{2,98}... | collective-permute-start | bytes 1179656 | tf_op jit(solution)/shard_map/ppermute | solution.py:20
  131.3 36.9 %collective-permute-start.30 = (s16[784,768]{1,0:T(8,128)(2,1)S(1)}, s16[784,768]{1,0:T(8,128)(2,1)S(1)}, u32[]{:S(2)}, u32[]{:S(2)}) collective-permute-start(s16[784,768]{1,0:T(8,128)(2,1)S(1)} %get-tuple-element.38), channel_id=1, source_target_pairs={{0,1},{1,0},{2,3},{3,2},{4,5},{5,4},{6,7},{7,6},{8,9},{9,8},{10,11... | collective-permute-start | bytes 3612680 | tf_op jit(solution)/shard_map/ppermute | solution.py:20
  132.0 40.0 %collective-permute-start.9 = (s16[784,768]{1,0:T(8,128)(2,1)S(1)}, s16[784,768]{1,0:T(8,128)(2,1)S(1)}, u32[]{:S(2)}, u32[]{:S(2)}) collective-permute-start(s16[784,768]{1,0:T(8,128)(2,1)S(1)} %get-tuple-element.28), channel_id=1, source_target_pairs={{0,3},{1,2},{2,1},{3,0},{4,7},{5,6},{6,5},{7,4},{8,11},{9,10},{10,... | collective-permute-start | bytes 3612680 | tf_op jit(solution)/shard_map/ppermute | solution.py:20
  140.8 14.5 %collective-permute-start.21 = (bf16[512,512]{1,0:T(8,128)(2,1)S(1)}, bf16[512,512]{1,0:T(8,128)(2,1)S(1)}, u32[]{:S(2)}, u32[]{:S(2)}) collective-permute-start(bf16[512,512]{1,0:T(8,128)(2,1)S(1)} %shard_map.132.refs_5_), channel_id=1, source_target_pairs={{0,128},{128,0},{1,129},{129,1},{2,130},{130,2},{3,131},{131,3},{4... | collective-permute-start | bytes 1572872 | tf_op jit(solution)/shard_map/ppermute | solution.py:20
  144.2 23.4 %collective-permute-start.28 = (bf16[512,768]{1,0:T(8,128)(2,1)S(1)}, bf16[512,768]{1,0:T(8,128)(2,1)S(1)}, u32[]{:S(2)}, u32[]{:S(2)}) collective-permute-start(bf16[512,768]{1,0:T(8,128)(2,1)S(1)} %constant_dynamic-update-slice_fusion.own), channel_id=1, source_target_pairs={{0,128},{128,0},{1,129},{129,1},{2,130},{130,2},{3,131},{131,3},{4... | collective-permute-start | bytes 2359304 | tf_op jit(solution)/shard_map/ppermute | solution.py:20
  (24 other events, 101.1 us)

commit v2 on v1

v2 whole, which is shorter than its diff:
```python
import math

import jax
import jax.numpy as jnp
from jax import lax
from jax.experimental import pallas as pl
from jax.experimental.pallas import tpu as pltpu
from jax.sharding import PartitionSpec as P

TILE = 128
NEWTON = 3
COLUMNS = 256
VMEM = 32 * 2**20
RING = (0, 1, 3, 2)
F32 = jnp.float32
BF16 = jnp.bfloat16
I16 = jnp.int16
SCALARS = pl.BlockSpec(memory_space=pltpu.SMEM)


def swapped(block, axis, mask):
    route = [(low, low ^ mask) for low in range(lax.axis_size(axis))]
    return lax.ppermute(block, axis, route)


def ring_gather(block, axis):
    return [swapped(block, axis, mask) for mask in RING[1:]]


def dot(left, right):
    return jnp.dot(left, right, preferred_element_type=F32)


def in_hbm(*arrays):
    return [pltpu.with_memory_space_constraint(array, pltpu.HBM) for array in arrays]


def call(kernel, outs, args, specs=None, grid=None, out_specs=None, scratch=(), flops=0, aliases=None):
    size = sum(math.prod(a.shape) * jnp.dtype(a.dtype).itemsize for a in list(args) + list(outs))
    more = {}
    if grid is not None:
        more = dict(grid=grid, out_specs=out_specs)
    if specs is not None:
        more["in_specs"] = specs
    if aliases is not None:
        more["input_output_aliases"] = aliases
    return pl.pallas_call(
        kernel,
        out_shape=list(outs),
        scratch_shapes=list(scratch),
        compiler_params=pltpu.CompilerParams(vmem_limit_bytes=VMEM),
        cost_estimate=pl.CostEstimate(flops=flops, bytes_accessed=size, transcendentals=0),
        **more,
    )(*args)


def shape(dims, dtype):
    return jax.ShapeDtypeStruct(dims, dtype)


def start_at(block, size):
    return pl.ds(pl.multiple_of(block * size, size), size)


def iota(dims, axis):
    return lax.broadcasted_iota(jnp.int32, dims, axis)


def encode(block, coded_ref):
    rows = block.shape[0]
    most = jnp.maximum(jnp.max(jnp.abs(block), axis=0, keepdims=True), 1e-30)
    power = jnp.ceil(jnp.log2(most) + 0.01)
    scale = 0.98 * jnp.exp2(15.0 - power)
    coded_ref[:rows, :] = jnp.round(block * scale).astype(jnp.int32).astype(I16)
    coded_ref[rows:, :] = jnp.broadcast_to(power, (16, block.shape[1])).astype(jnp.int32).astype(I16)


def decode(coded_ref):
    rows = coded_ref.shape[0] - 16
    power = coded_ref[rows:, :].astype(jnp.int32).astype(F32)[:1, :]
    scale = jnp.exp2(power - 15.0) * (1.0 / 0.98)
    return coded_ref[:rows, :].astype(jnp.int32).astype(F32) * scale


def encode_twice(block, high_ref, low_ref):
    rows = block.shape[0]
    most = jnp.maximum(jnp.max(jnp.abs(block), axis=0, keepdims=True), 1e-30)
    power = jnp.ceil(jnp.log2(most) + 0.01)
    scaled = block * (0.98 * jnp.exp2(15.0 - power))
    high = jnp.round(scaled)
    high_ref[:rows, :] = high.astype(jnp.int32).astype(I16)
    low_ref[:rows, :] = jnp.round((scaled - high) * 2.0**15).astype(jnp.int32).astype(I16)
    for ref in (high_ref, low_ref):
        ref[rows:, :] = jnp.broadcast_to(power, (16, block.shape[1])).astype(jnp.int32).astype(I16)


def decode_twice(high_ref, low_ref):
    rows = high_ref.shape[0] - 16
    power = high_ref[rows:, :].astype(jnp.int32).astype(F32)[:1, :]
    scale = jnp.exp2(power - 15.0) * (1.0 / 0.98)
    high = high_ref[:rows, :].astype(jnp.int32).astype(F32)
    low = low_ref[:rows, :].astype(jnp.int32).astype(F32)
    return (high + low * 2.0**-15) * scale


def prepare_kernel(
    at, live, tiles, order, upper_inverse, lower_inverse, pivot_all, far_all, solve_right, strip, solve_left,
):
    col = at[1]
    size = upper_inverse.shape[0]
    width = size // len(RING)
    wide = far_all.shape[1]
    shown = iota((width, size), 1) < live[0]
    for k, mask in enumerate(RING):
        block = upper_inverse[start_at(col ^ mask, width), :].astype(F32)
        solve_right[k * width : (k + 1) * width, :] = jnp.where(shown, block, 0.0).astype(BF16)
    chosen = jnp.where(iota((size, size), 0) == order[...], 1.0, 0.0).astype(BF16)
    masked = jnp.where(iota((size, size), 0) < live[0], lower_inverse[...].astype(F32), 0.0).astype(BF16)
    solve_left[...] = lax.dot_general(
        masked, chosen, (((1,), (1,)), ((), ())), preferred_element_type=F32
    ).astype(BF16)
    count = wide // TILE
    far = dot(solve_left[...], far_all[...])
    for t in range(count):
        flag = tiles[0, col * count + t].astype(F32)
        strip[:, t * TILE : (t + 1) * TILE] = (far[:, t * TILE : (t + 1) * TILE] * flag).astype(BF16)
    strip[:, wide:] = dot(solve_left[...], pivot_all[...]).astype(BF16)


def leaf_panel_kernel(tile_count, at, tiles, *refs):
    blocks, (solve_right, strip, parent_block, parent_right, parent_below) = refs[:8], refs[8:13]
    panel, right, pivot, below, coded = refs[13:]
    row = at[0]
    height, wide = parent_right.shape
    rows = parent_below.shape[0]
    cut = blocks[0].shape[0]
    for part in (0, 1):
        lower = jnp.concatenate([ref[...] for ref in blocks[4 * part : 4 * part + 4]], axis=1)
        whole = dot(lower, solve_right[...])
        for t in range((rows - cut if part else cut) // TILE):
            flag = tiles[0, row * tile_count + part * (cut // TILE) + t].astype(F32)
            panel[part * cut + t * TILE : part * cut + (t + 1) * TILE, :] = (
                whole[t * TILE : (t + 1) * TILE, :] * flag
            ).astype(BF16)
    parent = whole[rows - cut :, :].astype(BF16)
    here = 0
    found = parent_right[...] - dot(parent, strip[:, :wide])
    right[...] = found
    for k in range(wide // TILE):
        encode(found[:, k * TILE : (k + 1) * TILE], coded.at[here : here + height + 16, :])
        here += height + 16
    found = parent_block[...] - dot(parent, strip[:, wide:])
    pivot[...] = found
    middle = here + height + 16
    encode_twice(found, coded.at[here:middle, :], coded.at[middle : middle + height + 16, :])
    here = middle + height + 16
    found = parent_below[...] - dot(panel[...], strip[:, wide:])
    below[...] = found
    encode(found, coded.at[here:, :])


def leaf_pair_kernel(right, pivot, below, coded, both, below_pair, pivot_pair):
    height, wide = right.shape
    rows = below.shape[0]
    here = 0
    for k in range(wide // TILE):
        came = decode(coded.at[here : here + height + 16, :])
        both[rows + k * height : rows + (k + 1) * height, :] = (
            right[:, k * TILE : (k + 1) * TILE] + came
        ).astype(BF16)
        here += height + 16
    middle = here + height + 16
    pivot_pair[...] = pivot[...] + decode_twice(coded.at[here:middle, :], coded.at[middle : middle + height + 16, :])
    here = middle + height + 16
    total = (below[...] + decode(coded.at[here:, :])).astype(BF16)
    below_pair[...] = total
    both[:rows, :] = total


def leaf_corner_kernel(panel, far, grand, corner, coded):
    block = grand[...] - dot(panel[...], far[...])
    corner[...] = block
    encode(block, coded)


def corner_pair_kernel(corner, came, total, coded):
    block = corner[...] + decode(came)
    total[...] = block
    encode(block, coded)


def newton_kernel(at, block_0, block_1, block_3, block_2, across, out, half, matrix, inverse):
    row, col = at[0], at[1]
    size = matrix.shape[0]
    height, width = block_0.shape
    for k, (mask, block) in enumerate(zip(RING, (block_0, block_1, block_3, block_2))):
        matrix[start_at(row, height), start_at(col ^ mask, width)] = block[...]
        matrix[start_at(1 - row, height), start_at(col ^ mask, width)] = across[k * height : (k + 1) * height, :]
    where = iota((size, size), 0) == iota((size, size), 1)
    only = jnp.where(where, matrix[...], 0.0)
    by_row = 1.0 / jnp.sum(only, axis=1, keepdims=True)
    by_col = 1.0 / jnp.sum(only, axis=0, keepdims=True)
    inverse[...] = jnp.where(where, 2.0 * by_col, 0.0) - by_row * (matrix[...] * by_col)
    for step in range(NEWTON - 1):
        held = inverse[...]
        product = jnp.dot(matrix[...], held, precision=lax.Precision.HIGHEST, preferred_element_type=F32)
        inverse[...] = 2.0 * held - jnp.dot(held, product, precision=lax.Precision.HIGHEST, preferred_element_type=F32)
    out[...] = inverse[...].astype(BF16)
    half[...] = inverse[start_at(row, half.shape[0]), :].astype(BF16)


def level_lower_kernel(at, block_0, block_1, block_3, block_2, inverse, out, ordered):
    col = at[1]

    @pl.when(pl.program_id(0) == 0)
    def _():
        for k, mask in enumerate(RING):
            ordered[k * TILE : (k + 1) * TILE, :] = inverse[start_at(col ^ mask, TILE), :]

    whole = jnp.concatenate([block_0[...], block_1[...], block_3[...], block_2[...]], axis=1)
    out[...] = dot(whole, ordered[...]).astype(BF16)


def right_kernel(at, mine, other, across, out):
    row = at[0]
    height = across.shape[0] // (2 * (out.shape[1] // TILE))
    for k in range(out.shape[1] // TILE):
        strip = slice(k * TILE, (k + 1) * TILE)
        own = mine.shape[0] // 2 + k * height
        out[start_at(row, height), strip] = mine[own : own + height, :]
        out[start_at(2 + row, height), strip] = other[own : own + height, :]
        own = k * height
        out[start_at(1 - row, height), strip] = across[own : own + height, :]
        own += across.shape[0] // 2
        out[start_at(3 - row, height), strip] = across[own : own + height, :]


def update_kernel(total_0, total_1, lower_mine, lower_other, right, out):
    size = lower_mine.shape[1]
    cut = total_0.shape[0]
    update = dot(lower_mine[...], right[:size, :]) + dot(lower_other[...], right[size:, :])
    out[:cut, :] = total_0[...] - update[:cut, :]
    out[cut:, :] = total_1[...] - update[cut:, :]


def final_kernel(part, came_0, came_1, out):
    cut = came_0.shape[0] - 16
    out[:cut, :] = part[:cut, :] + decode(came_0)
    out[cut:, :] = part[cut:, :] + decode(came_1)


def body(
    parent_block,
    parent_right,
    parent_below,
    grand_block,
    lower_parent,
    lower_grand,
    upper_parent,
    upper_grand,
    lower_inverse,
    upper_inverse,
    pivot_order,
    live_width,
    tile_pattern,
):
    row_index = lax.axis_index("row")
    col_index = lax.axis_index("col")
    at = jnp.stack([row_index, col_index])
    size = upper_inverse.shape[2]
    rows, wide = grand_block.shape[1:]
    width = lower_grand.shape[2]
    strips = wide // COLUMNS

    height = parent_right.shape[1]
    cut = (rows + height) // 2
    halves = [lower_grand[0][:cut], jnp.concatenate([lower_grand[0][cut:], lower_parent[0]], axis=0)]
    steps = [swapped(half, "col", mask) for half in halves for mask in (1, 3)]
    blocks = [halves[0], steps[0], steps[1], swapped(steps[0], "col", 3)]
    blocks += [halves[1], steps[2], steps[3], swapped(steps[3], "col", 1)]
    pivot_all = lax.all_gather(upper_parent[0], "row", axis=0, tiled=True)
    far_all = lax.all_gather(upper_grand[0], "row", axis=0, tiled=True)
    solve_right, strip = call(
        prepare_kernel,
        [shape((size, size), BF16), shape((size, wide + width), BF16)],
        [
            at, live_width, tile_pattern, pivot_order, *in_hbm(upper_inverse[0], lower_inverse[0]),
            pivot_all, far_all,
        ],
        specs=[SCALARS] * 3 + [pl.BlockSpec(memory_space=pltpu.VMEM)] * 5,
        scratch=[pltpu.VMEM((size, size), BF16)],
        flops=2 * size * size * (size + wide + width),
    )
    panel, right, pivot, below, coded = call(
        lambda *refs: leaf_panel_kernel(rows // TILE, *refs),
        [
            shape((rows, size), BF16),
            shape((height, wide), F32),
            shape((height, width), F32),
            shape((rows, width), F32),
            shape(((wide // TILE + 2) * (height + 16) + rows + 16, width), I16),
        ],
        [
            at, tile_pattern, *blocks, solve_right, strip,
            *in_hbm(parent_block[0], parent_right[0], parent_below[0]),
        ],
        specs=[SCALARS] * 2 + [pl.BlockSpec(memory_space=pltpu.VMEM)] * 13,
        flops=2 * (rows + height) * size * (size + width),
    )

    def leaf_corner(start, count, panel):
        return call(
            leaf_corner_kernel,
            [pltpu.HBM((count, wide), F32), shape((count + 16, wide), I16)],
            [panel, strip, *in_hbm(grand_block[0])],
            specs=[
                pl.BlockSpec((pl.Element(count), pl.Element(size)), lambda j: (start, 0)),
                pl.BlockSpec((size, COLUMNS), lambda j: (0, j)),
                pl.BlockSpec((pl.Element(count), pl.Element(COLUMNS)), lambda j: (start, j * COLUMNS)),
            ],
            grid=(strips,),
            out_specs=[
                pl.BlockSpec((count, COLUMNS), lambda j: (0, j)),
                pl.BlockSpec((count + 16, COLUMNS), lambda j: (0, j)),
            ],
            flops=2 * count * size * wide,
        )

    corner_0, coded_0 = leaf_corner(0, cut, panel)
    corner_1, coded_1 = leaf_corner(cut, rows - cut, panel)

    right, _ = lax.optimization_barrier((right, coded_1))
    coded = swapped(coded, "depth", 1)
    both_mine, below_mine, pivot_pair = call(
        leaf_pair_kernel,
        [shape((2 * rows, width), BF16), shape((rows, width), BF16), shape((height, width), F32)],
        [right, pivot, below, coded],
    )
    both_other = swapped(both_mine, "depth", 3)
    below_other = both_other[:rows]

    def corner_pair(corner, coded):
        count = corner.shape[0]
        specs = [
            pl.BlockSpec((count, COLUMNS), lambda j: (0, j)),
            pl.BlockSpec((count + 16, COLUMNS), lambda j: (0, j)),
        ]
        return call(
            corner_pair_kernel,
            [pltpu.HBM((count, wide), F32), shape((count + 16, wide), I16)],
            [corner, coded],
            specs=specs,
            grid=(strips,),
            out_specs=specs,
        )

    came_0 = swapped(coded_0, "depth", 3)
    came_1 = swapped(coded_1, "depth", 1)
    pair_0, coded_0 = corner_pair(corner_0, came_0)
    pair_1, coded_1 = corner_pair(corner_1, came_1)
    came_0 = swapped(coded_0, "depth", 1)
    came_1 = swapped(coded_1, "depth", 3)

    first = row_index == 0

    def in_row_order(own, traded):
        return jnp.concatenate([jnp.where(first, own, traded), jnp.where(first, traded, own)], axis=0)

    pivots = [pivot_pair, *ring_gather(pivot_pair, "col")]
    inverse_mine, inverse_half = call(
        newton_kernel,
        [shape((size, size), BF16), shape((height, size), BF16)],
        [at, *pivots, swapped(jnp.concatenate(pivots, axis=0), "row", 1)],
        specs=[SCALARS] + [pl.BlockSpec(memory_space=pltpu.VMEM)] * 5,
        scratch=[pltpu.VMEM((size, size), F32), pltpu.VMEM((size, size), F32)],
        flops=2 * 24 * size**3,
    )
    inverse_half = swapped(inverse_half, "depth", 3)
    inverse_other = in_row_order(inverse_half, swapped(inverse_half, "row", 1))

    def level_lower(block, inverse):
        spec = pl.BlockSpec((rows // 2, width), lambda i: (i, 0))
        whole = pl.BlockSpec((size, size), lambda i: (0, 0))
        return call(
            level_lower_kernel,
            [shape((rows, size), BF16)],
            [at, block, *ring_gather(block, "col"), inverse],
            specs=[SCALARS] + [spec] * 4 + [whole],
            grid=(2,),
            out_specs=[pl.BlockSpec((rows // 2, size), lambda i: (i, 0))],
            scratch=[pltpu.VMEM((size, size), BF16)],
            flops=2 * rows * size * size,
        )[0]

    lower_mine = level_lower(below_mine, inverse_mine)
    lower_other = level_lower(below_other, inverse_other)
    right_across = swapped(jnp.concatenate([both_mine[rows:], both_other[rows:]], axis=0), "row", 1)
    (right_all,) = call(
        right_kernel,
        [shape((2 * size, wide), BF16)],
        [at, both_mine, both_other, right_across],
        specs=[SCALARS] + [pl.BlockSpec(memory_space=pltpu.VMEM)] * 3,
    )
    strip_spec = lambda dims: pl.BlockSpec(dims, lambda j: (0, j))
    (update,) = call(
        update_kernel,
        [shape((rows, wide), F32)],
        [pair_0, pair_1, lower_mine, lower_other, right_all],
        specs=[
            strip_spec((cut, COLUMNS)),
            strip_spec((rows - cut, COLUMNS)),
            pl.BlockSpec((rows, size), lambda j: (0, 0)),
            pl.BlockSpec((rows, size), lambda j: (0, 0)),
            strip_spec((2 * size, COLUMNS)),
        ],
        grid=(strips,),
        out_specs=[strip_spec((rows, COLUMNS))],
        flops=4 * rows * size * wide,
    )
    (result,) = call(
        final_kernel,
        [shape((rows, wide), F32)],
        [update, came_0, came_1],
        specs=[
            strip_spec((rows, COLUMNS)),
            strip_spec((cut + 16, COLUMNS)),
            strip_spec((rows - cut + 16, COLUMNS)),
        ],
        grid=(strips,),
        out_specs=[strip_spec((rows, COLUMNS))],
    )
    return result[None]


def solution(mesh):
    return jax.shard_map(
        body,
        mesh=mesh,
        in_specs=(
            P("depth", "row", "col"),
            P("depth", "row", "col"),
            P("depth", "row", "col"),
            P("depth", "row", "col"),
            P("depth", "row", "col"),
            P("depth", "row", "col"),
            P("depth", "row", "col"),
            P("depth", "row", "col"),
            P("depth", None, None),
            P("depth", None, None),
            P("depth", None),
            P("depth"),
            P("depth", None),
        ),
        out_specs=P("depth", "row", "col"),
        check_vma=False,
    )
```

time: 176 us -> 127 us (0.72)
  waiting for transfers between devices: 82.3 us -> 34.5 us
  starting transfers between devices: 38.7 us -> 33.1 us
  local copies, waits for them, and re-layouts: 14.5 us -> 9.01 us
  blocking collectives: 0 us -> 4.47 us
  Pallas kernels: 38.1 us -> 41.4 us
  other arithmetic: 1.23 us -> 3.01 us
    ppermute x31 -> x25, waiting for transfers between devices: 82.3 us -> 34.5 us  [swapped(): return lax.ppermute(block, axis, route)]
    pallas_call x10 -> x13, Pallas kernels: 30.6 us -> 41.4 us  [call(): pl.pallas_call(kernel, out_shape=list(outs), scratch_shapes=list(scratch)...]
    unnamed x36 -> x34, local copies, waits for them, and re-layouts: 14.5 us -> 7 us
    pallas_call x2 -> x0, Pallas kernels: 7.5 us -> none  [final(): pl.pallas_call(final_kernel, out_shape=shape((rows, wide), F32), grid_spe...]
    ppermute x31 -> x25, starting transfers between devices: 38.7 us -> 33.1 us  [swapped(): return lax.ppermute(block, axis, route)]
    all_gather x0 -> x2, blocking collectives: none -> 4.47 us  [the longest x1 2.36 us: body(): far_all = lax.all_gather(upper_grand[0], 'row', axis=0, tiled=True)]
    slice x0 -> x4, local copies, waits for them, and re-layouts: none -> 2.01 us  [the longest x1 1.01 us: body(): lower_grand[0][:cut]]
    concatenate x3 -> x4, other arithmetic: 0.08 us -> 1.86 us  [the longest x1 0.93 us: body(): jnp.concatenate([both_mine[rows:], both_other[rows:]], axis=0)]
  transfers between devices with their start and end apart: 31 -> 25, of which waited for: 14 -> 12; matrix products, arithmetic and copies ran while one was open for 1% -> 3% of each run, Pallas kernels for 20% -> 27%
where the time goes in v2:
time: 127 us; the launch traced here: 126 us
  Pallas kernels  41.4 us (33%)
  waiting for transfers between devices  34.5 us (27%)
  starting transfers between devices  33.1 us (26%)
  local copies, waits for them, and re-layouts  9.01 us (7%)
  blocking collectives  4.47 us (4%)
  other arithmetic  3.01 us (2%)
    pallas_call x13, Pallas kernels, call(): pl.pallas_call(kernel, out_shape=list(outs), scratch_shapes=list(scratch)...  41.4 us
    ppermute x25, waiting for transfers between devices, swapped(): return lax.ppermute(block, axis, route)  34.5 us
    ppermute x25, starting transfers between devices, swapped(): return lax.ppermute(block, axis, route)  33.1 us
    unnamed x34, local copies, waits for them, and re-layouts  7 us
  transfers between devices with their start and end apart: 25, of which 12 were waited for; matrix products, arithmetic and copies ran while one was open for 3% of the time, Pallas kernels for 27%

profile of v2, /device:TPU:96, one launch (start us, length us, event | category | flops | bytes accessed | tf_op | source)
XLA Modules:
  0.0 126.3 jit_solution(6153087930494979704)
XLA Ops:
  4.4 2.2 %collective-permute-start.4 = (bf16[896,128]{1,0:T(8,128)(2,1)S(1)}, bf16[896,128]{1,0:T(8,128)(2,1)S(1)}, u32[]{:S(2)}, u32[]{:S(2)}) collective-permute-start(bf16[896,128]{1,0:T(8,128)(2,1)S(1)} %pad_maximum_fusion.3.refs_6_), channel_id=1, source_target_pairs={{0,96},{32,64},{64,32},{96,0},{1,97},{33,65},{65,33},{97,1},{2,98}... | collective-permute-start | bytes 688136 | tf_op jit(solution)/shard_map/ppermute | solution.py:23
  14.2 2.4 %all-gather.1 = bf16[1,512,768]{2,1,0:T(8,128)(2,1)S(1)} all-gather(bf16[1,256,768]{2,1,0:T(8,128)(2,1)S(1)} %copy-done.16), channel_id=3, replica_groups=mesh['row'=2,'col'=4,'depth'=32] {'row'}, dimensions={1}, use_global_device_ids=true | all-gather | bytes 1179648 | tf_op jit(solution)/shard_map/all_gather | solution.py:282
  16.6 2.3 %shard_map.127 = (bf16[512,512]{1,0:T(8,128)(2,1)S(1)}, bf16[512,896]{1,0:T(8,128)(2,1)S(1)}) custom-call(s32[2]{0:T(128)S(1)} %pad_add_fusion.at.refs_0_, s32[1]{0:T(128)S(6)} %copy.14.live, s32[1,24]{1,0:T(1,128)S(1)} %copy-done.14, s32[1,512]{1,0:T(1,128)S(1)} %copy-done.15, bf16[512,512]{1,0:T(8,128)(2,1)} %bitcast.24, bf16[512,512]{1,0:T(8,128)(2,1)} %bitcast.25, ...), custom_call_target="tpu_custom_call" | custom-call | flops 738197504 | bytes 3410028 | tf_op jit(solution)/shard_map/pallas_call | solution.py:47
  19.1 3.4 %collective-permute-done.2.refs_5_ = bf16[896,128]{1,0:T(8,128)(2,1)S(1)} collective-permute-done((bf16[896,128]{1,0:T(8,128)(2,1)S(1)}, bf16[896,128]{1,0:T(8,128)(2,1)S(1)}, u32[]{:S(2)}, u32[]{:S(2)}) %collective-permute-start.2) | collective-permute-done | bytes 229408 | tf_op jit(solution)/shard_map/ppermute | solution.py:23
  22.6 3.5 %shard_map.128 = (bf16[1536,512]{1,0:T(8,128)(2,1)S(1)}, f32[256,768]{1,0:T(8,128)S(1)}, f32[256,128]{1,0:T(8,128)S(1)}, f32[1536,128]{1,0:T(8,128)S(1)}, s16[3728,128]{1,0:T(8,128)(2,1)S(1)}) custom-call(s32[2]{0:T(128)S(1)} %pad_add_fusion.at.refs_0_, s32[1,24]{1,0:T(1,128)S(1)} %copy-done.14, bf16[896,128]{1,0:T(8,128)(2,1)S(1)} %slice_bitcast_fusion.refs_2_, ...), custom_call_target="tpu_custom_call" | custom-call | flops 1174405120 | bytes 9212008 | tf_op jit(solution)/shard_map/pallas_call | solution.py:47
  27.8 4.5 %shard_map.129 = (f32[896,768]{1,0:T(8,128)}, s16[912,768]{1,0:T(8,128)(2,1)S(1)}) custom-call(bf16[1536,512]{1,0:T(8,128)(2,1)S(1)} %get-tuple-element.28.panel, bf16[512,896]{1,0:T(8,128)(2,1)S(1)} %get-tuple-element.27.refs_11_.far, f32[1536,768]{1,0:T(8,128)} %bitcast.18), custom_call_target="tpu_custom_call" | custom-call | flops 704643072 | bytes 11362304 | tf_op jit(solution)/shard_map/pallas_call | solution.py:47
  32.2 2.2 %collective-permute-start.6 = (s16[912,768]{1,0:T(8,128)(2,1)S(1)}, s16[912,768]{1,0:T(8,128)(2,1)S(1)}, u32[]{:S(2)}, u32[]{:S(2)}) collective-permute-start(s16[912,768]{1,0:T(8,128)(2,1)S(1)} %get-tuple-element.30), channel_id=1, source_target_pairs={{0,3},{1,2},{2,1},{3,0},{4,7},{5,6},{6,5},{7,4},{8,11},{9,10},{10,... | collective-permute-start | bytes 4202504 | tf_op jit(solution)/shard_map/ppermute | solution.py:23
  34.4 4.1 %shard_map.131 = (f32[640,768]{1,0:T(8,128)}, s16[656,768]{1,0:T(8,128)(2,1)S(1)}) custom-call(bf16[1536,512]{1,0:T(8,128)(2,1)S(1)} %get-tuple-element.28.panel, bf16[512,896]{1,0:T(8,128)(2,1)S(1)} %get-tuple-element.27.refs_11_.far, f32[1536,768]{1,0:T(8,128)} %bitcast.19), custom_call_target="tpu_custom_call" | custom-call | flops 503316480 | bytes 10182656 | tf_op jit(solution)/shard_map/pallas_call | solution.py:47
  38.5 9.4 %collective-permute-done.8.coded = s16[3728,128]{1,0:T(8,128)(2,1)S(1)} collective-permute-done((s16[3728,128]{1,0:T(8,128)(2,1)S(1)}, s16[3728,128]{1,0:T(8,128)(2,1)S(1)}, u32[]{:S(2)}, u32[]{:S(2)}) %collective-permute-start.8) | collective-permute-done | bytes 954400 | tf_op jit(solution)/shard_map/ppermute | solution.py:23
  51.7 3.3 %collective-permute-done.14.block_2 = f32[256,128]{1,0:T(8,128)S(1)} collective-permute-done((f32[256,128]{1,0:T(8,128)S(1)}, f32[256,128]{1,0:T(8,128)S(1)}, u32[]{:S(2)}, u32[]{:S(2)}) %collective-permute-start.14) | collective-permute-done | bytes 131104 | tf_op jit(solution)/shard_map/ppermute | solution.py:23
  58.2 2.2 %collective-permute-start.16 = (bf16[3072,128]{1,0:T(8,128)(2,1)S(1)}, bf16[3072,128]{1,0:T(8,128)(2,1)S(1)}, u32[]{:S(2)}, u32[]{:S(2)}) collective-permute-start(bf16[3072,128]{1,0:T(8,128)(2,1)S(1)} %get-tuple-element.43.mine), channel_id=1, source_target_pairs={{0,3},{1,2},{2,1},{3,0},{4,7},{5,6},{6,5},{7,4},{8,11},{9,10},{10,... | collective-permute-start | bytes 2359304 | tf_op jit(solution)/shard_map/ppermute | solution.py:23
  62.5 4.1 %collective-permute-done.6.came = s16[912,768]{1,0:T(8,128)(2,1)S(1)} collective-permute-done((s16[912,768]{1,0:T(8,128)(2,1)S(1)}, s16[912,768]{1,0:T(8,128)(2,1)S(1)}, u32[]{:S(2)}, u32[]{:S(2)}) %collective-permute-start.6) | collective-permute-done | bytes 1400864 | tf_op jit(solution)/shard_map/ppermute | solution.py:23
  66.6 2.4 %collective-permute-start.10 = (bf16[1536,128]{1,0:T(8,128)(2,1)S(1)}, bf16[1536,128]{1,0:T(8,128)(2,1)S(1)}, u32[]{:S(2)}, u32[]{:S(2)}) collective-permute-start(bf16[1536,128]{1,0:T(8,128)(2,1)S(1)} %get-tuple-element.40.block_0), channel_id=1, source_target_pairs={{0,96},{32,64},{64,32},{96,0},{1,97},{33,65},{65,33},{97,1},{2,98}... | collective-permute-start | bytes 1179656 | tf_op jit(solution)/shard_map/ppermute | solution.py:23
  69.0 2.7 %shard_map.130 = (f32[896,768]{1,0:T(8,128)}, s16[912,768]{1,0:T(8,128)(2,1)}) custom-call(f32[896,768]{1,0:T(8,128)S(1)} %copy-done.1, s16[912,768]{1,0:T(8,128)(2,1)S(1)} %collective-permute-done.6.came), custom_call_target="tpu_custom_call" | custom-call | bytes 8306688 | tf_op jit(solution)/shard_map/pallas_call | solution.py:47
  71.7 8.1 %shard_map.134 = (bf16[512,512]{1,0:T(8,128)(2,1)S(1)}, bf16[256,512]{1,0:T(8,128)(2,1)S(1)}) custom-call(s32[2]{0:T(128)S(1)} %pad_add_fusion.at.refs_0_, f32[256,128]{1,0:T(8,128)S(1)} %get-tuple-element.41.block_0, f32[256,128]{1,0:T(8,128)S(1)} %collective-permute-done.12.block_1, f32[256,128]{1,0:T(8,128)S(1)} %collective-permute-done.13.block_3, ...), custom_call_target="tpu_custom_call" | custom-call | flops 6442450944 | bytes 1835016 | tf_op jit(solution)/shard_map/pallas_call | solution.py:47
  82.8 2.2 %collective-permute-start.20 = (bf16[256,512]{1,0:T(8,128)(2,1)S(1)}, bf16[256,512]{1,0:T(8,128)(2,1)}, u32[]{:S(2)}, u32[]{:S(2)}) collective-permute-start(bf16[256,512]{1,0:T(8,128)(2,1)S(1)} %get-tuple-element.44), channel_id=1, source_target_pairs={{0,3},{1,2},{2,1},{3,0},{4,7},{5,6},{6,5},{7,4},{8,11},{9,10},{10,... | collective-permute-start | bytes 786440 | tf_op jit(solution)/shard_map/ppermute | solution.py:23
  87.0 4.7 %collective-permute-done.20 = bf16[256,512]{1,0:T(8,128)(2,1)} collective-permute-done((bf16[256,512]{1,0:T(8,128)(2,1)S(1)}, bf16[256,512]{1,0:T(8,128)(2,1)}, u32[]{:S(2)}, u32[]{:S(2)}) %collective-permute-start.20) | collective-permute-done | bytes 262176 | tf_op jit(solution)/shard_map/ppermute | solution.py:23
  93.2 2.5 %shard_map.132 = (f32[640,768]{1,0:T(8,128)}, s16[656,768]{1,0:T(8,128)(2,1)}) custom-call(f32[640,768]{1,0:T(8,128)S(1)} %copy-done.3, s16[656,768]{1,0:T(8,128)(2,1)S(1)} %collective-permute-done.7.came), custom_call_target="tpu_custom_call" | custom-call | bytes 5947392 | tf_op jit(solution)/shard_map/pallas_call | solution.py:47
  96.5 2.2 %collective-permute-start.24 = (s16[656,768]{1,0:T(8,128)(2,1)}, s16[656,768]{1,0:T(8,128)(2,1)}, u32[]{:S(2)}, u32[]{:S(2)}) collective-permute-start(s16[656,768]{1,0:T(8,128)(2,1)} %get-tuple-element.46), channel_id=1, source_target_pairs={{0,3},{1,2},{2,1},{3,0},{4,7},{5,6},{6,5},{7,4},{8,11},{9,10},{10,... | collective-permute-start | bytes 3022856 | tf_op jit(solution)/shard_map/ppermute | solution.py:23
  108.4 2.3 %collective-permute-done.18.block_3 = bf16[1536,128]{1,0:T(8,128)(2,1)S(1)} collective-permute-done((bf16[1536,128]{1,0:T(8,128)(2,1)S(1)}, bf16[1536,128]{1,0:T(8,128)(2,1)S(1)}, u32[]{:S(2)}, u32[]{:S(2)}) %collective-permute-start.18) | collective-permute-done | bytes 393248 | tf_op jit(solution)/shard_map/ppermute | solution.py:23
  111.0 2.3 %shard_map.136.lower_other = bf16[1536,512]{1,0:T(8,128)(2,1)S(1)} custom-call(s32[2]{0:T(128)S(1)} %pad_add_fusion.at.refs_0_, bf16[1536,128]{1,0:T(8,128)(2,1)S(1)} %get-tuple-element.48.block_0, bf16[1536,128]{1,0:T(8,128)(2,1)S(1)} %collective-permute-done.17.block_1, bf16[1536,128]{1,0:T(8,128)(2,1)S(1)} %collective-permute-done.18.block_3, ...), custom_call_target="tpu_custom_call" | custom-call | flops 805306368 | bytes 3670024 | tf_op jit(solution)/shard_map/pallas_call | solution.py:47
  115.3 3.7 %shard_map.138.part = f32[1536,768]{1,0:T(8,128)S(1)} custom-call(f32[896,768]{1,0:T(8,128)S(1)} %copy-done, f32[640,768]{1,0:T(8,128)S(1)} %copy-done.2, bf16[1536,512]{1,0:T(8,128)(2,1)S(1)} %shard_map.135.lower_mine, bf16[1536,512]{1,0:T(8,128)(2,1)S(1)} %shard_map.136.lower_other, bf16[1024,768]{1,0:T(8,128)(2,1)S(1)} %shard_map.137.right), custom_call_target="tpu_custom_call" | custom-call | flops 2415919104 | bytes 14155776 | tf_op jit(solution)/shard_map/pallas_call | solution.py:47
  119.0 3.2 %collective-permute-done.24.came_1 = s16[656,768]{1,0:T(8,128)(2,1)} collective-permute-done((s16[656,768]{1,0:T(8,128)(2,1)}, s16[656,768]{1,0:T(8,128)(2,1)}, u32[]{:S(2)}, u32[]{:S(2)}) %collective-permute-start.24) | collective-permute-done | bytes 1007648 | tf_op jit(solution)/shard_map/ppermute | solution.py:23
  122.2 4.1 %shard_map.139 = f32[1536,768]{1,0:T(8,128)} custom-call(f32[1536,768]{1,0:T(8,128)S(1)} %shard_map.138.part, s16[912,768]{1,0:T(8,128)(2,1)S(1)} %collective-permute-done.23.came_0, s16[656,768]{1,0:T(8,128)(2,1)} %collective-permute-done.24.came_1), custom_call_target="tpu_custom_call" | custom-call | bytes 11845632 | tf_op jit(solution)/shard_map/pallas_call | solution.py:47
  (85 shorter events, 41.6 us)
Async XLA Ops:
  1.0 9.5 %collective-permute-start = (bf16[896,128]{1,0:T(8,128)(2,1)S(1)}, bf16[896,128]{1,0:T(8,128)(2,1)S(1)}, u32[]{:S(2)}, u32[]{:S(2)}) collective-permute-start(bf16[896,128]{1,0:T(8,128)(2,1)S(1)} %slice_bitcast_fusion.refs_2_), channel_id=1, source_target_pairs={{0,32},{32,0},{64,96},{96,64},{1,33},{33,1},{65,97},{97,65},{2,34}... | collective-permute-start | bytes 688136 | tf_op jit(solution)/shard_map/ppermute | solution.py:23
  4.4 9.8 %collective-permute-start.4 = (bf16[896,128]{1,0:T(8,128)(2,1)S(1)}, bf16[896,128]{1,0:T(8,128)(2,1)S(1)}, u32[]{:S(2)}, u32[]{:S(2)}) collective-permute-start(bf16[896,128]{1,0:T(8,128)(2,1)S(1)} %pad_maximum_fusion.3.refs_6_), channel_id=1, source_target_pairs={{0,96},{32,64},{64,32},{96,0},{1,97},{33,65},{65,33},{97,1},{2,98}... | collective-permute-start | bytes 688136 | tf_op jit(solution)/shard_map/ppermute | solution.py:23
  6.6 12.6 %collective-permute-start.1 = (bf16[896,128]{1,0:T(8,128)(2,1)S(1)}, bf16[896,128]{1,0:T(8,128)(2,1)S(1)}, u32[]{:S(2)}, u32[]{:S(2)}) collective-permute-start(bf16[896,128]{1,0:T(8,128)(2,1)S(1)} %slice_bitcast_fusion.refs_2_), channel_id=1, source_target_pairs={{0,96},{32,64},{64,32},{96,0},{1,97},{33,65},{65,33},{97,1},{2,98}... | collective-permute-start | bytes 688136 | tf_op jit(solution)/shard_map/ppermute | solution.py:23
  7.7 11.4 %collective-permute-start.3 = (bf16[896,128]{1,0:T(8,128)(2,1)S(1)}, bf16[896,128]{1,0:T(8,128)(2,1)S(1)}, u32[]{:S(2)}, u32[]{:S(2)}) collective-permute-start(bf16[896,128]{1,0:T(8,128)(2,1)S(1)} %pad_maximum_fusion.3.refs_6_), channel_id=1, source_target_pairs={{0,32},{32,0},{64,96},{96,64},{1,33},{33,1},{65,97},{97,65},{2,34}... | collective-permute-start | bytes 688136 | tf_op jit(solution)/shard_map/ppermute | solution.py:23
  10.6 12.0 %collective-permute-start.2 = (bf16[896,128]{1,0:T(8,128)(2,1)S(1)}, bf16[896,128]{1,0:T(8,128)(2,1)S(1)}, u32[]{:S(2)}, u32[]{:S(2)}) collective-permute-start(bf16[896,128]{1,0:T(8,128)(2,1)S(1)} %collective-permute-done.refs_3_), channel_id=1, source_target_pairs={{0,96},{32,64},{64,32},{96,0},{1,97},{33,65},{65,33},{97,1},{2,98}... | collective-permute-start | bytes 688136 | tf_op jit(solution)/shard_map/ppermute | solution.py:23
  14.2 8.4 %collective-permute-start.5 = (bf16[896,128]{1,0:T(8,128)(2,1)S(1)}, bf16[896,128]{1,0:T(8,128)(2,1)S(1)}, u32[]{:S(2)}, u32[]{:S(2)}) collective-permute-start(bf16[896,128]{1,0:T(8,128)(2,1)S(1)} %collective-permute-done.4.refs_8_), channel_id=1, source_target_pairs={{0,32},{32,0},{64,96},{96,64},{1,33},{33,1},{65,97},{97,65},{2,34}... | collective-permute-start | bytes 688136 | tf_op jit(solution)/shard_map/ppermute | solution.py:23
  26.1 21.8 %collective-permute-start.8 = (s16[3728,128]{1,0:T(8,128)(2,1)S(1)}, s16[3728,128]{1,0:T(8,128)(2,1)S(1)}, u32[]{:S(2)}, u32[]{:S(2)}) collective-permute-start(s16[3728,128]{1,0:T(8,128)(2,1)S(1)} %get-tuple-element.39), channel_id=1, source_target_pairs={{0,1},{1,0},{2,3},{3,2},{4,5},{5,4},{6,7},{7,6},{8,9},{9,8},{10,11... | collective-permute-start | bytes 2863112 | tf_op jit(solution)/shard_map/ppermute | solution.py:23
  32.2 34.4 %collective-permute-start.6 = (s16[912,768]{1,0:T(8,128)(2,1)S(1)}, s16[912,768]{1,0:T(8,128)(2,1)S(1)}, u32[]{:S(2)}, u32[]{:S(2)}) collective-permute-start(s16[912,768]{1,0:T(8,128)(2,1)S(1)} %get-tuple-element.30), channel_id=1, source_target_pairs={{0,3},{1,2},{2,1},{3,0},{4,7},{5,6},{6,5},{7,4},{8,11},{9,10},{10,... | collective-permute-start | bytes 4202504 | tf_op jit(solution)/shard_map/ppermute | solution.py:23
  48.2 6.9 %collective-permute-start.14 = (f32[256,128]{1,0:T(8,128)S(1)}, f32[256,128]{1,0:T(8,128)S(1)}, u32[]{:S(2)}, u32[]{:S(2)}) collective-permute-start(f32[256,128]{1,0:T(8,128)S(1)} %get-tuple-element.41.block_0), channel_id=1, source_target_pairs={{0,64},{32,96},{64,0},{96,32},{1,65},{33,97},{65,1},{97,33},{2,66}... | collective-permute-start | bytes 393224 | tf_op jit(solution)/shard_map/ppermute | solution.py:23
  49.8 6.6 %collective-permute-start.13 = (f32[256,128]{1,0:T(8,128)S(1)}, f32[256,128]{1,0:T(8,128)S(1)}, u32[]{:S(2)}, u32[]{:S(2)}) collective-permute-start(f32[256,128]{1,0:T(8,128)S(1)} %get-tuple-element.41.block_0), channel_id=1, source_target_pairs={{0,96},{32,64},{64,32},{96,0},{1,97},{33,65},{65,33},{97,1},{2,98}... | collective-permute-start | bytes 393224 | tf_op jit(solution)/shard_map/ppermute | solution.py:23
  56.4 15.2 %collective-permute-start.15 = (f32[1024,128]{1,0:T(8,128)S(1)}, f32[1024,128]{1,0:T(8,128)S(1)}, u32[]{:S(2)}, u32[]{:S(2)}) collective-permute-start(f32[1024,128]{1,0:T(8,128)S(1)} %pad_maximum_fusion.1), channel_id=1, source_target_pairs={{0,128},{128,0},{1,129},{129,1},{2,130},{130,2},{3,131},{131,3},{4... | collective-permute-start | bytes 1572872 | tf_op jit(solution)/shard_map/ppermute | solution.py:23
  56.5 24.7 %collective-permute-start.7 = (s16[656,768]{1,0:T(8,128)(2,1)S(1)}, s16[656,768]{1,0:T(8,128)(2,1)S(1)}, u32[]{:S(2)}, u32[]{:S(2)}) collective-permute-start(s16[656,768]{1,0:T(8,128)(2,1)S(1)} %get-tuple-element.33), channel_id=1, source_target_pairs={{0,1},{1,0},{2,3},{3,2},{4,5},{5,4},{6,7},{7,6},{8,9},{9,8},{10,11... | collective-permute-start | bytes 3022856 | tf_op jit(solution)/shard_map/ppermute | solution.py:23
  58.2 24.6 %collective-permute-start.16 = (bf16[3072,128]{1,0:T(8,128)(2,1)S(1)}, bf16[3072,128]{1,0:T(8,128)(2,1)S(1)}, u32[]{:S(2)}, u32[]{:S(2)}) collective-permute-start(bf16[3072,128]{1,0:T(8,128)(2,1)S(1)} %get-tuple-element.43.mine), channel_id=1, source_target_pairs={{0,3},{1,2},{2,1},{3,0},{4,7},{5,6},{6,5},{7,4},{8,11},{9,10},{10,... | collective-permute-start | bytes 2359304 | tf_op jit(solution)/shard_map/ppermute | solution.py:23
  60.4 24.6 %collective-permute-start.11 = (bf16[1536,128]{1,0:T(8,128)(2,1)S(1)}, bf16[1536,128]{1,0:T(8,128)(2,1)S(1)}, u32[]{:S(2)}, u32[]{:S(2)}) collective-permute-start(bf16[1536,128]{1,0:T(8,128)(2,1)S(1)} %get-tuple-element.40.block_0), channel_id=1, source_target_pairs={{0,64},{32,96},{64,0},{96,32},{1,65},{33,97},{65,1},{97,33},{2,66}... | collective-permute-start | bytes 1179656 | tf_op jit(solution)/shard_map/ppermute | solution.py:23
  66.6 26.1 %collective-permute-start.10 = (bf16[1536,128]{1,0:T(8,128)(2,1)S(1)}, bf16[1536,128]{1,0:T(8,128)(2,1)S(1)}, u32[]{:S(2)}, u32[]{:S(2)}) collective-permute-start(bf16[1536,128]{1,0:T(8,128)(2,1)S(1)} %get-tuple-element.40.block_0), channel_id=1, source_target_pairs={{0,96},{32,64},{64,32},{96,0},{1,97},{33,65},{65,33},{97,1},{2,98}... | collective-permute-start | bytes 1179656 | tf_op jit(solution)/shard_map/ppermute | solution.py:23
  71.7 24.1 %collective-permute-start.9 = (bf16[1536,128]{1,0:T(8,128)(2,1)S(1)}, bf16[1536,128]{1,0:T(8,128)(2,1)S(1)}, u32[]{:S(2)}, u32[]{:S(2)}) collective-permute-start(bf16[1536,128]{1,0:T(8,128)(2,1)S(1)} %get-tuple-element.40.block_0), channel_id=1, source_target_pairs={{0,32},{32,0},{64,96},{96,64},{1,33},{33,1},{65,97},{97,65},{2,34}... | collective-permute-start | bytes 1179656 | tf_op jit(solution)/shard_map/ppermute | solution.py:23
  81.3 41.0 %collective-permute-start.23 = (s16[912,768]{1,0:T(8,128)(2,1)}, s16[912,768]{1,0:T(8,128)(2,1)S(1)}, u32[]{:S(2)}, u32[]{:S(2)}) collective-permute-start(s16[912,768]{1,0:T(8,128)(2,1)} %get-tuple-element.45), channel_id=1, source_target_pairs={{0,1},{1,0},{2,3},{3,2},{4,5},{5,4},{6,7},{7,6},{8,9},{9,8},{10,11... | collective-permute-start | bytes 4202504 | tf_op jit(solution)/shard_map/ppermute | solution.py:23
  82.8 8.9 %collective-permute-start.20 = (bf16[256,512]{1,0:T(8,128)(2,1)S(1)}, bf16[256,512]{1,0:T(8,128)(2,1)}, u32[]{:S(2)}, u32[]{:S(2)}) collective-permute-start(bf16[256,512]{1,0:T(8,128)(2,1)S(1)} %get-tuple-element.44), channel_id=1, source_target_pairs={{0,3},{1,2},{2,1},{3,0},{4,7},{5,6},{6,5},{7,4},{8,11},{9,10},{10,... | collective-permute-start | bytes 786440 | tf_op jit(solution)/shard_map/ppermute | solution.py:23
  85.1 15.4 %collective-permute-start.19 = (bf16[1536,128]{1,0:T(8,128)(2,1)S(1)}, bf16[1536,128]{1,0:T(8,128)(2,1)}, u32[]{:S(2)}, u32[]{:S(2)}) collective-permute-start(bf16[1536,128]{1,0:T(8,128)(2,1)S(1)} %get-tuple-element.48.block_0), channel_id=1, source_target_pairs={{0,64},{32,96},{64,0},{96,32},{1,65},{33,97},{65,1},{97,33},{2,66}... | collective-permute-start | bytes 1179656 | tf_op jit(solution)/shard_map/ppermute | solution.py:23
  91.7 6.9 %collective-permute-start.21 = (bf16[256,512]{1,0:T(8,128)(2,1)}, bf16[256,512]{1,0:T(8,128)(2,1)}, u32[]{:S(2)}, u32[]{:S(2)}) collective-permute-start(bf16[256,512]{1,0:T(8,128)(2,1)} %collective-permute-done.20), channel_id=1, source_target_pairs={{0,128},{128,0},{1,129},{129,1},{2,130},{130,2},{3,131},{131,3},{4... | collective-permute-start | bytes 786440 | tf_op jit(solution)/shard_map/ppermute | solution.py:23
  92.7 20.6 %collective-permute-start.22 = (bf16[3072,128]{1,0:T(8,128)(2,1)}, bf16[3072,128]{1,0:T(8,128)(2,1)}, u32[]{:S(2)}, u32[]{:S(2)}) collective-permute-start(bf16[3072,128]{1,0:T(8,128)(2,1)} %pad_maximum_fusion), channel_id=1, source_target_pairs={{0,128},{128,0},{1,129},{129,1},{2,130},{130,2},{3,131},{131,3},{4... | collective-permute-start | bytes 2359304 | tf_op jit(solution)/shard_map/ppermute | solution.py:23
  96.5 25.7 %collective-permute-start.24 = (s16[656,768]{1,0:T(8,128)(2,1)}, s16[656,768]{1,0:T(8,128)(2,1)}, u32[]{:S(2)}, u32[]{:S(2)}) collective-permute-start(s16[656,768]{1,0:T(8,128)(2,1)} %get-tuple-element.46), channel_id=1, source_target_pairs={{0,3},{1,2},{2,1},{3,0},{4,7},{5,6},{6,5},{7,4},{8,11},{9,10},{10,... | collective-permute-start | bytes 3022856 | tf_op jit(solution)/shard_map/ppermute | solution.py:23
  98.7 12.0 %collective-permute-start.18 = (bf16[1536,128]{1,0:T(8,128)(2,1)S(1)}, bf16[1536,128]{1,0:T(8,128)(2,1)S(1)}, u32[]{:S(2)}, u32[]{:S(2)}) collective-permute-start(bf16[1536,128]{1,0:T(8,128)(2,1)S(1)} %get-tuple-element.48.block_0), channel_id=1, source_target_pairs={{0,96},{32,64},{64,32},{96,0},{1,97},{33,65},{65,33},{97,1},{2,98}... | collective-permute-start | bytes 1179656 | tf_op jit(solution)/shard_map/ppermute | solution.py:23
  100.5 10.5 %collective-permute-start.17 = (bf16[1536,128]{1,0:T(8,128)(2,1)S(1)}, bf16[1536,128]{1,0:T(8,128)(2,1)S(1)}, u32[]{:S(2)}, u32[]{:S(2)}) collective-permute-start(bf16[1536,128]{1,0:T(8,128)(2,1)S(1)} %get-tuple-element.48.block_0), channel_id=1, source_target_pairs={{0,32},{32,0},{64,96},{96,64},{1,33},{33,1},{65,97},{97,65},{2,34}... | collective-permute-start | bytes 1179656 | tf_op jit(solution)/shard_map/ppermute | solution.py:23
  (18 other events, 133.9 us)

commit v3 on v2

v3 whole, which is shorter than its diff:
```python
import math

import jax
import jax.numpy as jnp
from jax import lax
from jax.experimental import pallas as pl
from jax.experimental.pallas import tpu as pltpu
from jax.sharding import PartitionSpec as P

TILE = 128
NEWTON = 3
COLUMNS = 256
VMEM = 32 * 2**20
RING = (0, 1, 3, 2)
F32 = jnp.float32
BF16 = jnp.bfloat16
I16 = jnp.int16
SCALARS = pl.BlockSpec(memory_space=pltpu.SMEM)


def swapped(block, axis, mask):
    route = [(low, low ^ mask) for low in range(lax.axis_size(axis))]
    return lax.ppermute(block, axis, route)


def after(value, *others):
    return lax.optimization_barrier((value, *others))[0]


def ring_gather(block, axis):
    return [swapped(block, axis, mask) for mask in RING[1:]]


def dot(left, right):
    return jnp.dot(left, right, preferred_element_type=F32)


def in_hbm(*arrays):
    return [pltpu.with_memory_space_constraint(array, pltpu.HBM) for array in arrays]


def call(kernel, outs, args, specs=None, grid=None, out_specs=None, scratch=(), flops=0, aliases=None, ahead=0):
    size = sum(math.prod(a.shape) * jnp.dtype(a.dtype).itemsize for a in list(args) + list(outs))
    more = {}
    if ahead:
        more["grid_spec"] = pltpu.PrefetchScalarGridSpec(
            num_scalar_prefetch=ahead, grid=grid, in_specs=specs, out_specs=out_specs, scratch_shapes=list(scratch)
        )
    else:
        more["scratch_shapes"] = list(scratch)
        if grid is not None:
            more.update(grid=grid, out_specs=out_specs)
        if specs is not None:
            more["in_specs"] = specs
    if aliases is not None:
        more["input_output_aliases"] = aliases
    return pl.pallas_call(
        kernel,
        out_shape=list(outs),
        compiler_params=pltpu.CompilerParams(vmem_limit_bytes=VMEM),
        cost_estimate=pl.CostEstimate(
            flops=flops, bytes_accessed=size, transcendentals=0
        ),
        **more,
    )(*args)


def shape(dims, dtype):
    return jax.ShapeDtypeStruct(dims, dtype)


def start_at(block, size):
    return pl.ds(pl.multiple_of(block * size, size), size)


def iota(dims, axis):
    return lax.broadcasted_iota(jnp.int32, dims, axis)


def encode(block, coded_ref):
    rows = block.shape[0]
    most = jnp.maximum(jnp.max(jnp.abs(block), axis=0, keepdims=True), 1e-30)
    power = jnp.ceil(jnp.log2(most) + 0.01)
    scale = 0.98 * jnp.exp2(15.0 - power)
    coded_ref[:rows, :] = jnp.round(block * scale).astype(jnp.int32).astype(I16)
    coded_ref[rows:, :] = jnp.broadcast_to(power, (16, block.shape[1])).astype(jnp.int32).astype(I16)


def decode(coded_ref):
    rows = coded_ref.shape[0] - 16
    power = coded_ref[rows:, :].astype(jnp.int32).astype(F32)[:1, :]
    scale = jnp.exp2(power - 15.0) * (1.0 / 0.98)
    return coded_ref[:rows, :].astype(jnp.int32).astype(F32) * scale


def prepare_kernel(
    at, live, tiles, order, upper_inverse, lower_inverse, pivot_all, far_all, solve_right, strip, solve_left,
):
    col = at[1]
    size = upper_inverse.shape[0]
    width = size // len(RING)
    wide = far_all.shape[1]
    shown = iota((width, size), 1) < live[0]
    for k, mask in enumerate(RING):
        block = upper_inverse[start_at(col ^ mask, width), :].astype(F32)
        solve_right[k * width : (k + 1) * width, :] = jnp.where(shown, block, 0.0).astype(BF16)
    chosen = jnp.where(iota((size, size), 0) == order[...], 1.0, 0.0).astype(BF16)
    masked = jnp.where(iota((size, size), 0) < live[0], lower_inverse[...].astype(F32), 0.0).astype(BF16)
    solve_left[...] = lax.dot_general(
        masked, chosen, (((1,), (1,)), ((), ())), preferred_element_type=F32
    ).astype(BF16)
    count = wide // TILE
    far = dot(solve_left[...], far_all[...])
    for t in range(count):
        flag = tiles[0, col * count + t].astype(F32)
        strip[:, t * TILE : (t + 1) * TILE] = (far[:, t * TILE : (t + 1) * TILE] * flag).astype(BF16)
    strip[:, wide:] = dot(solve_left[...], pivot_all[...]).astype(BF16)


def leaf_panel_kernel(tile_count, at, tiles, *refs):
    blocks, (solve_right, strip, parent_block, parent_right, parent_below) = refs[:8], refs[8:13]
    panel, right, pivot, below, coded = refs[13:]
    row = at[0]
    height, wide = parent_right.shape
    rows = parent_below.shape[0]
    cut = blocks[0].shape[0]
    for part in (0, 1):
        lower = jnp.concatenate([ref[...] for ref in blocks[4 * part : 4 * part + 4]], axis=1)
        whole = dot(lower, solve_right[...])
        for t in range((rows - cut if part else cut) // TILE):
            flag = tiles[0, row * tile_count + part * (cut // TILE) + t].astype(F32)
            panel[part * cut + t * TILE : part * cut + (t + 1) * TILE, :] = (
                whole[t * TILE : (t + 1) * TILE, :] * flag
            ).astype(BF16)
    parent = whole[rows - cut :, :].astype(BF16)
    here = 0
    found = parent_right[...] - dot(parent, strip[:, :wide])
    right[...] = found
    for k in range(wide // TILE):
        encode(found[:, k * TILE : (k + 1) * TILE], coded.at[here : here + height + 16, :])
        here += height + 16
    found = parent_block[...] - dot(parent, strip[:, wide:])
    pivot[...] = found
    found = parent_below[...] - dot(panel[...], strip[:, wide:])
    below[...] = found
    encode(found, coded.at[here:, :])


def leaf_pair_kernel(right, below, coded, both, below_pair):
    height, wide = right.shape
    rows = below.shape[0]
    here = 0
    for k in range(wide // TILE):
        came = decode(coded.at[here : here + height + 16, :])
        both[rows + k * height : rows + (k + 1) * height, :] = (
            right[:, k * TILE : (k + 1) * TILE] + came
        ).astype(BF16)
        here += height + 16
    total = (below[...] + decode(coded.at[here:, :])).astype(BF16)
    below_pair[...] = total
    both[:rows, :] = total


def split_kernel(mine, other, below_other, rights):
    rows = mine.shape[0] // 2
    below_other[...] = other[:rows, :]
    rights[:rows, :] = mine[rows:, :]
    rights[rows:, :] = other[rows:, :]


def corner_give_kernel(at, panel, far, grand, coded):
    encode(grand[...] - dot(panel[...], far[...]), coded)


def corner_pair_kernel(at, panel, far, grand, came, total, coded):
    block = grand[...] - dot(panel[...], far[...]) + decode(came)
    total[...] = block
    encode(block, coded)


def corner_quad_kernel(pair, came, total, coded):
    block = pair[...] + decode(came)
    total[...] = block
    encode(block, coded)


def parts_of(block):
    high = block.astype(BF16)
    return high, (block - high.astype(F32)).astype(BF16)


def dot_wide(left, right):
    left_high, left_low = left
    right_high, right_low = right
    return dot(left_high, right_high) + (dot(left_high, right_low) + dot(left_low, right_high))


def newton_kernel(at, block_0, block_1, block_3, block_2, across, out, half, matrix, inverse):
    row, col = at[0], at[1]
    size = matrix.shape[0]
    height, width = block_0.shape
    for k, (mask, block) in enumerate(zip(RING, (block_0, block_1, block_3, block_2))):
        matrix[start_at(row, height), start_at(col ^ mask, width)] = block[...]
        matrix[start_at(1 - row, height), start_at(col ^ mask, width)] = across[k * height : (k + 1) * height, :]
    where = iota((size, size), 0) == iota((size, size), 1)
    only = jnp.where(where, matrix[...], 0.0)
    by_row = 1.0 / jnp.sum(only, axis=1, keepdims=True)
    by_col = 1.0 / jnp.sum(only, axis=0, keepdims=True)
    inverse[...] = jnp.where(where, 2.0 * by_col, 0.0) - by_row * (matrix[...] * by_col)
    whole = parts_of(matrix[...])
    for step in range(NEWTON - 1):
        held = parts_of(inverse[...])
        inverse[...] = 2.0 * inverse[...] - dot_wide(held, parts_of(dot_wide(whole, held)))
    out[...] = inverse[...].astype(BF16)
    half[...] = inverse[start_at(row, half.shape[0]), :].astype(BF16)


def lower_kernel(at, own, near, far, across_0, across_1, *rest):
    *inverses, out, ordered, whole = rest
    row, col = at[0], at[1]
    size = ordered.shape[0]

    @pl.when(pl.program_id(0) == 0)
    def _():
        if len(inverses) == 1:
            whole[...] = inverses[0][...]
        else:
            whole[start_at(row, size // 2), :] = inverses[0][...]
            whole[start_at(1 - row, size // 2), :] = inverses[1][...]
        for k, mask in enumerate(RING):
            ordered[k * TILE : (k + 1) * TILE, :] = whole[start_at(col ^ mask, TILE), :]

    for part, across in ((0, across_0), (1, across_1)):

        @pl.when(pl.program_id(0) == part)
        def _():
            lower = jnp.concatenate([own[...], near[...], far[...], across[...]], axis=1)
            out[...] = dot(lower, ordered[...]).astype(BF16)


def halves_kernel(near, far, first, second):
    rows = first.shape[0]
    first[...] = near[:rows, :]
    second[...] = far[rows:, :]


def right_kernel(at, rights, across, out):
    row = at[0]
    count = out.shape[1] // TILE
    height = rights.shape[0] // (2 * count)
    for pair in (0, 1):
        for k in range(count):
            strip = slice(k * TILE, (k + 1) * TILE)
            here = slice((pair * count + k) * height, (pair * count + k + 1) * height)
            out[start_at(2 * pair + row, height), strip] = rights[here, :]
            out[start_at(2 * pair + 1 - row, height), strip] = across[here, :]


def final_kernel(at, own_0, came_0, own_1, came_1, lower_mine, lower_other, right, out):
    size = lower_mine.shape[1]
    update = dot(lower_mine[...], right[:size, :]) + dot(lower_other[...], right[size:, :])
    for k, ref in enumerate((own_0, came_0, own_1, came_1)):

        @pl.when(pl.program_id(0) == k)
        def _():
            out[...] = (decode(ref) if k % 2 else ref[...]) - update


def body(
    parent_block,
    parent_right,
    parent_below,
    grand_block,
    lower_parent,
    lower_grand,
    upper_parent,
    upper_grand,
    lower_inverse,
    upper_inverse,
    pivot_order,
    live_width,
    tile_pattern,
):
    row_index = lax.axis_index("row")
    col_index = lax.axis_index("col")
    depth_index = lax.axis_index("depth")
    h = (depth_index >> 1) & 1
    g = (depth_index ^ (depth_index >> 1)) & 1
    at = jnp.stack([row_index, col_index, g, h])
    size = upper_inverse.shape[2]
    rows, wide = grand_block.shape[1:]
    width = lower_grand.shape[2]
    strips = wide // COLUMNS

    height = parent_right.shape[1]
    cut = (rows + height) // 2
    halves = [lower_grand[0][:cut], jnp.concatenate([lower_grand[0][cut:], lower_parent[0]], axis=0)]
    steps = [swapped(half, "col", mask) for half in halves for mask in (1, 3)]
    blocks = [halves[0], steps[0], steps[1], swapped(steps[0], "col", 3)]
    blocks += [halves[1], steps[2], steps[3], swapped(steps[3], "col", 1)]
    pivot_all = lax.all_gather(upper_parent[0], "row", axis=0, tiled=True)
    far_all = lax.all_gather(upper_grand[0], "row", axis=0, tiled=True)
    solve_right, strip = call(
        prepare_kernel,
        [shape((size, size), BF16), shape((size, wide + width), BF16)],
        [
            at, live_width, tile_pattern, pivot_order, *in_hbm(upper_inverse[0], lower_inverse[0]),
            pivot_all, far_all,
        ],
        specs=[SCALARS] * 3 + [pl.BlockSpec(memory_space=pltpu.VMEM)] * 5,
        scratch=[pltpu.VMEM((size, size), BF16)],
        flops=2 * size * size * (size + wide + width),
    )
    panel, right, pivot, below, coded = call(
        lambda *refs: leaf_panel_kernel(rows // TILE, *refs),
        [
            shape((rows, size), BF16),
            shape((height, wide), F32),
            shape((height, width), F32),
            shape((rows, width), F32),
            shape((wide // TILE * (height + 16) + rows + 16, width), I16),
        ],
        [
            at, tile_pattern, *blocks, solve_right, strip,
            *in_hbm(parent_block[0], parent_right[0], parent_below[0]),
        ],
        specs=[SCALARS] * 2 + [pl.BlockSpec(memory_space=pltpu.VMEM)] * 13,
        flops=2 * (rows + height) * size * (size + width),
    )

    half = rows // 4
    coded_spec = pl.BlockSpec((half + 16, COLUMNS), lambda j, at: (0, j))
    total_spec = pl.BlockSpec((half, COLUMNS), lambda j, at: (0, j))

    def corner(kernel, place, came, panel):
        return call(
            kernel,
            [shape((half, wide), F32)] * len(came) + [shape((half + 16, wide), I16)],
            [at, panel, strip, *in_hbm(grand_block[0]), *came],
            specs=[
                pl.BlockSpec((half, size), lambda j, at: (place(at), 0)),
                pl.BlockSpec((size, COLUMNS), lambda j, at: (0, j)),
                pl.BlockSpec((half, COLUMNS), lambda j, at: (place(at), j)),
            ]
            + [coded_spec] * len(came),
            grid=(strips,),
            out_specs=[total_spec] * len(came) + [coded_spec],
            flops=2 * half * size * wide,
            ahead=1,
        )

    def corner_quad(pair, came):
        specs = [pl.BlockSpec((half, COLUMNS), lambda j: (0, j)), pl.BlockSpec((half + 16, COLUMNS), lambda j: (0, j))]
        return call(
            corner_quad_kernel,
            [shape((half, wide), F32), shape((half + 16, wide), I16)],
            [pair, came],
            specs=specs,
            grid=(strips,),
            out_specs=specs,
        )

    (give_1,) = corner(corner_give_kernel, lambda at: 3 - at[3], [], panel)
    (give_0,) = corner(corner_give_kernel, lambda at: 1 - at[2], [], after(panel, give_1))
    step_1 = swapped(give_1, "depth", 3)
    step_0 = swapped(give_0, "depth", 1)

    pivot_pair = pivot + after(swapped(pivot, "depth", 1), give_0)
    pivots = [pivot_pair, *ring_gather(pivot_pair, "col")]
    pivots_across = swapped(jnp.concatenate(pivots, axis=0), "row", 1)

    both_mine, below_mine = call(
        leaf_pair_kernel,
        [shape((2 * rows, width), BF16), shape((rows, width), BF16)],
        [after(right, step_1, pivots_across), below, swapped(coded, "depth", 1)],
    )
    both_other = swapped(both_mine, "depth", 3)

    def near_blocks(block):
        return swapped(block, "col", 1), swapped(block, "col", 3)

    def across_blocks(near, far):
        piece = shape((rows // 2, width), BF16)
        first, second = call(halves_kernel, [piece, piece], [near, far])
        return first, [swapped(first, "col", 3), swapped(second, "col", 1)]

    near_mine = near_blocks(below_mine)
    inverse_mine, inverse_half = call(
        newton_kernel,
        [shape((size, size), BF16), shape((height, size), BF16)],
        [at, *pivots, after(pivots_across, below_mine)],
        specs=[SCALARS] + [pl.BlockSpec(memory_space=pltpu.VMEM)] * 5,
        scratch=[pltpu.VMEM((size, size), F32), pltpu.VMEM((size, size), F32)],
        flops=2 * 12 * size**3,
    )
    inverse_half = swapped(inverse_half, "depth", 3)
    pair_1, coded_1 = corner(
        corner_pair_kernel, lambda at: 2 + at[3], [step_1], after(panel, inverse_mine)
    )
    came_1 = swapped(coded_1, "depth", 1)
    sent_mine, across_mine = across_blocks(near_mine[0], after(near_mine[1], coded_1))
    pair_0, coded_0 = corner(
        corner_pair_kernel, lambda at: at[2], [step_0], after(panel, sent_mine)
    )
    came_0 = swapped(coded_0, "depth", 3)

    def level_lower(block, near, across, inverses):
        block_spec = pl.BlockSpec((rows // 2, width), lambda i: (i, 0))
        across_spec = pl.BlockSpec((rows // 2, width), lambda i: (0, 0))
        return call(
            lower_kernel,
            [shape((rows, size), BF16)],
            [at, block, *near, *across, *inverses],
            specs=[SCALARS]
            + [block_spec] * 3
            + [across_spec] * 2
            + [pl.BlockSpec(one.shape, lambda i: (0, 0)) for one in inverses],
            grid=(2,),
            out_specs=[pl.BlockSpec((rows // 2, size), lambda i: (i, 0))],
            scratch=[pltpu.VMEM((size, size), BF16)] * 2,
            flops=2 * rows * size * size,
        )[0]

    lower_mine = level_lower(below_mine, near_mine, across_mine, [after(inverse_mine, coded_0)])
    below_other, rights = call(
        split_kernel,
        [shape((rows, width), BF16), shape((2 * rows, width), BF16)],
        [both_mine, after(both_other, inverse_half, lower_mine)],
    )
    near_other = near_blocks(below_other)
    inverse_across = swapped(after(inverse_half, rights), "row", 1)
    own_1, coded_1 = corner_quad(after(pair_1, rights), came_1)
    came_1 = swapped(coded_1, "depth", 3)
    sent_other, across_other = across_blocks(near_other[0], after(near_other[1], coded_1, inverse_across))
    own_0, coded_0 = corner_quad(after(pair_0, sent_other), came_0)
    came_0 = swapped(coded_0, "depth", 1)
    (right_all,) = call(
        right_kernel,
        [shape((2 * size, wide), BF16)],
        [at, rights, after(swapped(rights, "row", 1), coded_0)],
        specs=[SCALARS] + [pl.BlockSpec(memory_space=pltpu.VMEM)] * 2,
    )
    lower_other = level_lower(
        below_other, near_other, across_other, [inverse_half, after(inverse_across, right_all)]
    )

    place = lambda k, at: jnp.where(k == 0, at[2], jnp.where(k == 1, 1 - at[2], jnp.where(k == 2, 2 + at[3], 3 - at[3])))
    own_spec = pl.BlockSpec((half, wide), lambda k, at: (0, 0))
    came_spec = pl.BlockSpec((half + 16, wide), lambda k, at: (0, 0))
    lower_spec = pl.BlockSpec((half, size), lambda k, at: (place(k, at), 0))
    (result,) = call(
        final_kernel,
        [shape((rows, wide), F32)],
        [at, own_0, came_0, own_1, came_1, lower_mine, lower_other, right_all],
        specs=[own_spec, came_spec] * 2
        + [lower_spec] * 2
        + [pl.BlockSpec((2 * size, wide), lambda k, at: (0, 0))],
        grid=(4,),
        out_specs=[pl.BlockSpec((half, wide), lambda k, at: (place(k, at), 0))],
        flops=4 * rows * size * wide,
        ahead=1,
    )
    return result[None]


def solution(mesh):
    return jax.shard_map(
        body,
        mesh=mesh,
        in_specs=(
            P("depth", "row", "col"),
            P("depth", "row", "col"),
            P("depth", "row", "col"),
            P("depth", "row", "col"),
            P("depth", "row", "col"),
            P("depth", "row", "col"),
            P("depth", "row", "col"),
            P("depth", "row", "col"),
            P("depth", None, None),
            P("depth", None, None),
            P("depth", None),
            P("depth"),
            P("depth", None),
        ),
        out_specs=P("depth", "row", "col"),
        check_vma=False,
    )
```

time: 127 us -> 112 us (0.88)
  local copies, waits for them, and re-layouts: 9.01 us -> 1.94 us
  starting transfers between devices: 33.1 us -> 39.5 us
  Pallas kernels: 41.4 us -> 35.4 us
  waiting for transfers between devices: 34.5 us -> 28.6 us
  other arithmetic: 3.01 us -> 0.99 us
    unnamed x34 -> x6, local copies, waits for them, and re-layouts: 7 us -> 0.01 us
    ppermute x25 -> x30, starting transfers between devices: 33.1 us -> 39.5 us  [swapped(): return lax.ppermute(block, axis, route)]
    pallas_call x13 -> x17, Pallas kernels: 41.4 us -> 35.4 us  [call(): pl.pallas_call(kernel, out_shape=list(outs), compiler_params=pltpu.Compil...]
    ppermute x25 -> x30, waiting for transfers between devices: 34.5 us -> 28.6 us  [swapped(): return lax.ppermute(block, axis, route)]
  transfers between devices with their start and end apart: 25 -> 30, of which waited for: 12 -> 13; matrix products, arithmetic and copies ran while one was open for 3% -> 2% of each run, Pallas kernels for 27% -> 24%
where the time goes in v3:
time: 112 us
  starting transfers between devices  39.5 us (35%)
  Pallas kernels  35.4 us (32%)
  waiting for transfers between devices  28.6 us (26%)
  blocking collectives  4.47 us (4%)
  local copies, waits for them, and re-layouts  1.94 us (2%)
    ppermute x30, starting transfers between devices, swapped(): return lax.ppermute(block, axis, route)  39.5 us
    pallas_call x17, Pallas kernels, call(): pl.pallas_call(kernel, out_shape=list(outs), compiler_params=pltpu.Compil...  35.4 us
    ppermute x30, waiting for transfers between devices, swapped(): return lax.ppermute(block, axis, route)  28.6 us
    all_gather x1, blocking collectives, body(): far_all = lax.all_gather(upper_grand[0], 'row', axis=0, tiled=True)  2.36 us
  transfers between devices with their start and end apart: 30, of which 13 were waited for; matrix products, arithmetic and copies ran while one was open for 2% of the time, Pallas kernels for 24%

profile of v3, /device:TPU:96, one launch (start us, length us, event | category | flops | bytes accessed | tf_op | source)
XLA Modules:
  0.0 111.8 jit_solution(16042538056137586779)
XLA Ops:
  4.4 2.2 %collective-permute-start.4 = (bf16[896,128]{1,0:T(8,128)(2,1)S(1)}, bf16[896,128]{1,0:T(8,128)(2,1)S(1)}, u32[]{:S(2)}, u32[]{:S(2)}) collective-permute-start(bf16[896,128]{1,0:T(8,128)(2,1)S(1)} %pad_maximum_fusion.1.refs_6_), channel_id=1, source_target_pairs={{0,96},{32,64},{64,32},{96,0},{1,97},{33,65},{65,33},{97,1},{2,98}... | collective-permute-start | bytes 688136 | tf_op jit(solution)/shard_map/ppermute | solution.py:23
  8.4 2.1 %all-gather = bf16[1,512,128]{2,1,0:T(8,128)(2,1)S(1)} all-gather(bf16[1,256,128]{2,1,0:T(8,128)(2,1)} %param.19), channel_id=2, replica_groups=mesh['row'=2,'col'=4,'depth'=32] {'row'}, dimensions={1}, use_global_device_ids=true | all-gather | bytes 196608 | tf_op jit(solution)/shard_map/all_gather | solution.py:301
  10.6 2.1 %collective-permute-start.2 = (bf16[896,128]{1,0:T(8,128)(2,1)S(1)}, bf16[896,128]{1,0:T(8,128)(2,1)S(1)}, u32[]{:S(2)}, u32[]{:S(2)}) collective-permute-start(bf16[896,128]{1,0:T(8,128)(2,1)S(1)} %collective-permute-done.refs_3_), channel_id=1, source_target_pairs={{0,96},{32,64},{64,32},{96,0},{1,97},{33,65},{65,33},{97,1},{2,98}... | collective-permute-start | bytes 688136 | tf_op jit(solution)/shard_map/ppermute | solution.py:23
  14.2 2.4 %all-gather.1 = bf16[1,512,768]{2,1,0:T(8,128)(2,1)S(1)} all-gather(bf16[1,256,768]{2,1,0:T(8,128)(2,1)S(1)} %copy-done.2), channel_id=3, replica_groups=mesh['row'=2,'col'=4,'depth'=32] {'row'}, dimensions={1}, use_global_device_ids=true | all-gather | bytes 1179648 | tf_op jit(solution)/shard_map/all_gather | solution.py:302
  16.6 2.3 %shard_map.127 = (bf16[512,512]{1,0:T(8,128)(2,1)S(1)}, bf16[512,896]{1,0:T(8,128)(2,1)S(1)}) custom-call(s32[4]{0:T(128)S(1)} %pad_add_fusion.at.refs_0_, s32[1]{0:T(128)S(6)} %copy.14.live, s32[1,24]{1,0:T(1,128)S(1)} %copy-done, s32[1,512]{1,0:T(1,128)S(1)} %copy-done.1, bf16[512,512]{1,0:T(8,128)(2,1)} %bitcast.28, bf16[512,512]{1,0:T(8,128)(2,1)} %bitcast.29, ...), custom_call_target="tpu_custom_call" | custom-call | flops 738197504 | bytes 3410036 | tf_op jit(solution)/shard_map/pallas_call | solution.py:57
  19.1 3.4 %collective-permute-done.2.refs_5_ = bf16[896,128]{1,0:T(8,128)(2,1)S(1)} collective-permute-done((bf16[896,128]{1,0:T(8,128)(2,1)S(1)}, bf16[896,128]{1,0:T(8,128)(2,1)S(1)}, u32[]{:S(2)}, u32[]{:S(2)}) %collective-permute-start.2) | collective-permute-done | bytes 229408 | tf_op jit(solution)/shard_map/ppermute | solution.py:23
  22.6 3.5 %shard_map.128 = (bf16[1536,512]{1,0:T(8,128)(2,1)S(1)}, f32[256,768]{1,0:T(8,128)S(1)}, f32[256,128]{1,0:T(8,128)S(1)}, f32[1536,128]{1,0:T(8,128)S(1)}, s16[3184,128]{1,0:T(8,128)(2,1)S(1)}) custom-call(s32[4]{0:T(128)S(1)} %pad_add_fusion.at.refs_0_, s32[1,24]{1,0:T(1,128)S(1)} %copy-done, bf16[896,128]{1,0:T(8,128)(2,1)S(1)} %slice_bitcast_fusion.refs_2_, ...), custom_call_target="tpu_custom_call" | custom-call | flops 1174405120 | bytes 9072752 | tf_op jit(solution)/shard_map/pallas_call | solution.py:57
  28.2 3.3 %shard_map.129 = s16[400,768]{1,0:T(8,128)(2,1)S(1)} custom-call(s32[4]{0:T(128)S(1)} %pad_add_fusion.at.refs_0_, bf16[1536,512]{1,0:T(8,128)(2,1)S(1)} %get-tuple-element.62.panel, bf16[512,896]{1,0:T(8,128)(2,1)S(1)} %get-tuple-element.46.refs_11_.far, f32[1536,768]{1,0:T(8,128)} %bitcast.20), custom_call_target="tpu_custom_call" | custom-call | flops 301989888 | bytes 7823376 | tf_op jit(solution)/shard_map/pallas_call | solution.py:57
  31.5 3.3 %shard_map.130 = s16[400,768]{1,0:T(8,128)(2,1)S(1)} custom-call(s32[4]{0:T(128)S(1)} %pad_add_fusion.at.refs_0_, bf16[1536,512]{1,0:T(8,128)(2,1)S(1)} %get-tuple-element.62.panel, bf16[512,896]{1,0:T(8,128)(2,1)S(1)} %get-tuple-element.46.refs_11_.far, f32[1536,768]{1,0:T(8,128)} %bitcast.21), custom_call_target="tpu_custom_call" | custom-call | flops 301989888 | bytes 7823376 | tf_op jit(solution)/shard_map/pallas_call | solution.py:57
  38.5 3.0 %collective-permute-start.6 = (s16[400,768]{1,0:T(8,128)(2,1)S(1)}, s16[400,768]{1,0:T(8,128)(2,1)S(1)}, u32[]{:S(2)}, u32[]{:S(2)}) collective-permute-start(s16[400,768]{1,0:T(8,128)(2,1)S(1)} %shard_map.129), channel_id=1, source_target_pairs={{0,3},{1,2},{2,1},{3,0},{4,7},{5,6},{6,5},{7,4},{8,11},{9,10},{10,... | collective-permute-start | bytes 1843208 | tf_op jit(solution)/shard_map/ppermute | solution.py:23
  45.3 7.5 %collective-permute-done.6.came = s16[400,768]{1,0:T(8,128)(2,1)S(1)} collective-permute-done((s16[400,768]{1,0:T(8,128)(2,1)S(1)}, s16[400,768]{1,0:T(8,128)(2,1)S(1)}, u32[]{:S(2)}, u32[]{:S(2)}) %collective-permute-start.6) | collective-permute-done | bytes 614432 | tf_op jit(solution)/shard_map/ppermute | solution.py:23
  53.0 2.4 %collective-permute-start.14 = (bf16[1536,128]{1,0:T(8,128)(2,1)S(1)}, bf16[1536,128]{1,0:T(8,128)(2,1)S(1)}, u32[]{:S(2)}, u32[]{:S(2)}) collective-permute-start(bf16[1536,128]{1,0:T(8,128)(2,1)S(1)} %get-tuple-element.55.own), channel_id=1, source_target_pairs={{0,96},{32,64},{64,32},{96,0},{1,97},{33,65},{65,33},{97,1},{2,98}... | collective-permute-start | bytes 1179656 | tf_op jit(solution)/shard_map/ppermute | solution.py:23
  56.0 3.0 %collective-permute-start.16 = (bf16[3072,128]{1,0:T(8,128)(2,1)S(1)}, bf16[3072,128]{1,0:T(8,128)(2,1)S(1)}, u32[]{:S(2)}, u32[]{:S(2)}) collective-permute-start(bf16[3072,128]{1,0:T(8,128)(2,1)S(1)} %get-tuple-element.64.mine), channel_id=1, source_target_pairs={{0,3},{1,2},{2,1},{3,0},{4,7},{5,6},{6,5},{7,4},{8,11},{9,10},{10,... | collective-permute-start | bytes 2359304 | tf_op jit(solution)/shard_map/ppermute | solution.py:23
  58.9 4.5 %shard_map.132 = (bf16[512,512]{1,0:T(8,128)(2,1)S(1)}, bf16[256,512]{1,0:T(8,128)(2,1)S(1)}) custom-call(s32[4]{0:T(128)S(1)} %pad_add_fusion.at.refs_0_, f32[256,128]{1,0:T(8,128)S(1)} %add.3.block_0, f32[256,128]{1,0:T(8,128)S(1)} %collective-permute-done.8.block_1, f32[256,128]{1,0:T(8,128)S(1)} %collective-permute-done.9.block_3, ...), custom_call_target="tpu_custom_call" | custom-call | flops 3221225472 | bytes 1835024 | tf_op jit(solution)/shard_map/pallas_call | solution.py:57
  63.5 3.4 %shard_map.133 = (f32[384,768]{1,0:T(8,128)S(1)}, s16[400,768]{1,0:T(8,128)(2,1)S(1)}) custom-call(s32[4]{0:T(128)S(1)} %pad_add_fusion.at.refs_0_, bf16[1536,512]{1,0:T(8,128)(2,1)S(1)} %get-tuple-element.62.panel, bf16[512,896]{1,0:T(8,128)(2,1)S(1)} %get-tuple-element.46.refs_11_.far, f32[1536,768]{1,0:T(8,128)} %bitcast.22, ...), custom_call_target="tpu_custom_call" | custom-call | flops 301989888 | bytes 9617424 | tf_op jit(solution)/shard_map/pallas_call | solution.py:57
  70.0 3.4 %shard_map.135 = (f32[384,768]{1,0:T(8,128)S(1)}, s16[400,768]{1,0:T(8,128)(2,1)S(1)}) custom-call(s32[4]{0:T(128)S(1)} %pad_add_fusion.at.refs_0_, bf16[1536,512]{1,0:T(8,128)(2,1)S(1)} %get-tuple-element.62.panel, bf16[512,896]{1,0:T(8,128)(2,1)S(1)} %get-tuple-element.46.refs_11_.far, f32[1536,768]{1,0:T(8,128)} %bitcast.23, ...), custom_call_target="tpu_custom_call" | custom-call | flops 301989888 | bytes 9617424 | tf_op jit(solution)/shard_map/pallas_call | solution.py:57
  73.4 3.0 %collective-permute-start.24 = (s16[400,768]{1,0:T(8,128)(2,1)S(1)}, s16[400,768]{1,0:T(8,128)(2,1)S(1)}, u32[]{:S(2)}, u32[]{:S(2)}) collective-permute-start(s16[400,768]{1,0:T(8,128)(2,1)S(1)} %get-tuple-element.67), channel_id=1, source_target_pairs={{0,3},{1,2},{2,1},{3,0},{4,7},{5,6},{6,5},{7,4},{8,11},{9,10},{10,... | collective-permute-start | bytes 1843208 | tf_op jit(solution)/shard_map/ppermute | solution.py:23
  78.3 4.3 %collective-permute-done.17.rest_0_ = bf16[256,512]{1,0:T(8,128)(2,1)S(1)} collective-permute-done((bf16[256,512]{1,0:T(8,128)(2,1)S(1)}, bf16[256,512]{1,0:T(8,128)(2,1)S(1)}, u32[]{:S(2)}, u32[]{:S(2)}) %collective-permute-start.17) | collective-permute-done | bytes 262176 | tf_op jit(solution)/shard_map/ppermute | solution.py:23
  86.3 3.6 %collective-permute-start.26 = (s16[400,768]{1,0:T(8,128)(2,1)S(1)}, s16[400,768]{1,0:T(8,128)(2,1)S(1)}, u32[]{:S(2)}, u32[]{:S(2)}) collective-permute-start(s16[400,768]{1,0:T(8,128)(2,1)S(1)} %get-tuple-element.74), channel_id=1, source_target_pairs={{0,3},{1,2},{2,1},{3,0},{4,7},{5,6},{6,5},{7,4},{8,11},{9,10},{10,... | collective-permute-start | bytes 1843208 | tf_op jit(solution)/shard_map/ppermute | solution.py:23
  89.9 1.8 %collective-permute-done.21.far = bf16[1536,128]{1,0:T(8,128)(2,1)S(1)} collective-permute-done((bf16[1536,128]{1,0:T(8,128)(2,1)S(1)}, bf16[1536,128]{1,0:T(8,128)(2,1)S(1)}, u32[]{:S(2)}, u32[]{:S(2)}) %collective-permute-start.21) | collective-permute-done | bytes 393248 | tf_op jit(solution)/shard_map/ppermute | solution.py:23
  97.0 2.1 %collective-permute-done.28.across_1 = bf16[768,128]{1,0:T(8,128)(2,1)S(1)} collective-permute-done((bf16[768,128]{1,0:T(8,128)(2,1)S(1)}, bf16[768,128]{1,0:T(8,128)(2,1)S(1)}, u32[]{:S(2)}, u32[]{:S(2)}) %collective-permute-start.28) | collective-permute-done | bytes 196640 | tf_op jit(solution)/shard_map/ppermute | solution.py:23
  99.2 2.7 %collective-permute-done.27.across_0 = bf16[768,128]{1,0:T(8,128)(2,1)S(1)} collective-permute-done((bf16[768,128]{1,0:T(8,128)(2,1)S(1)}, bf16[768,128]{1,0:T(8,128)(2,1)S(1)}, u32[]{:S(2)}, u32[]{:S(2)}) %collective-permute-start.27) | collective-permute-done | bytes 196640 | tf_op jit(solution)/shard_map/ppermute | solution.py:23
  104.4 2.0 %collective-permute-done.25.came_0 = s16[400,768]{1,0:T(8,128)(2,1)S(1)} collective-permute-done((s16[400,768]{1,0:T(8,128)(2,1)S(1)}, s16[400,768]{1,0:T(8,128)(2,1)S(1)}, u32[]{:S(2)}, u32[]{:S(2)}) %collective-permute-start.25) | collective-permute-done | bytes 614432 | tf_op jit(solution)/shard_map/ppermute | solution.py:23
  106.4 5.5 %shard_map.143 = f32[1536,768]{1,0:T(8,128)} custom-call(s32[4]{0:T(128)S(1)} %pad_add_fusion.at.refs_0_, f32[384,768]{1,0:T(8,128)S(1)} %get-tuple-element.79.own_0, s16[400,768]{1,0:T(8,128)(2,1)S(1)} %collective-permute-done.25.came_0, f32[384,768]{1,0:T(8,128)S(1)} %get-tuple-element.81.own_1, s16[400,768]{1,0:T(8,128)(2,1)S(1)} %collective-permute-done.26.came_1, ...), custom_call_target="tpu_custom_call" | custom-call | flops 2415919104 | bytes 13025296 | tf_op jit(solution)/shard_map/pallas_call | solution.py:57
  (67 shorter events, 34.1 us)
Async XLA Ops:
  1.0 9.5 %collective-permute-start = (bf16[896,128]{1,0:T(8,128)(2,1)S(1)}, bf16[896,128]{1,0:T(8,128)(2,1)S(1)}, u32[]{:S(2)}, u32[]{:S(2)}) collective-permute-start(bf16[896,128]{1,0:T(8,128)(2,1)S(1)} %slice_bitcast_fusion.refs_2_), channel_id=1, source_target_pairs={{0,32},{32,0},{64,96},{96,64},{1,33},{33,1},{65,97},{97,65},{2,34}... | collective-permute-start | bytes 688136 | tf_op jit(solution)/shard_map/ppermute | solution.py:23
  4.4 9.8 %collective-permute-start.4 = (bf16[896,128]{1,0:T(8,128)(2,1)S(1)}, bf16[896,128]{1,0:T(8,128)(2,1)S(1)}, u32[]{:S(2)}, u32[]{:S(2)}) collective-permute-start(bf16[896,128]{1,0:T(8,128)(2,1)S(1)} %pad_maximum_fusion.1.refs_6_), channel_id=1, source_target_pairs={{0,96},{32,64},{64,32},{96,0},{1,97},{33,65},{65,33},{97,1},{2,98}... | collective-permute-start | bytes 688136 | tf_op jit(solution)/shard_map/ppermute | solution.py:23
  6.6 12.6 %collective-permute-start.1 = (bf16[896,128]{1,0:T(8,128)(2,1)S(1)}, bf16[896,128]{1,0:T(8,128)(2,1)S(1)}, u32[]{:S(2)}, u32[]{:S(2)}) collective-permute-start(bf16[896,128]{1,0:T(8,128)(2,1)S(1)} %slice_bitcast_fusion.refs_2_), channel_id=1, source_target_pairs={{0,96},{32,64},{64,32},{96,0},{1,97},{33,65},{65,33},{97,1},{2,98}... | collective-permute-start | bytes 688136 | tf_op jit(solution)/shard_map/ppermute | solution.py:23
  7.7 11.4 %collective-permute-start.3 = (bf16[896,128]{1,0:T(8,128)(2,1)S(1)}, bf16[896,128]{1,0:T(8,128)(2,1)S(1)}, u32[]{:S(2)}, u32[]{:S(2)}) collective-permute-start(bf16[896,128]{1,0:T(8,128)(2,1)S(1)} %pad_maximum_fusion.1.refs_6_), channel_id=1, source_target_pairs={{0,32},{32,0},{64,96},{96,64},{1,33},{33,1},{65,97},{97,65},{2,34}... | collective-permute-start | bytes 688136 | tf_op jit(solution)/shard_map/ppermute | solution.py:23
  10.6 12.0 %collective-permute-start.2 = (bf16[896,128]{1,0:T(8,128)(2,1)S(1)}, bf16[896,128]{1,0:T(8,128)(2,1)S(1)}, u32[]{:S(2)}, u32[]{:S(2)}) collective-permute-start(bf16[896,128]{1,0:T(8,128)(2,1)S(1)} %collective-permute-done.refs_3_), channel_id=1, source_target_pairs={{0,96},{32,64},{64,32},{96,0},{1,97},{33,65},{65,33},{97,1},{2,98}... | collective-permute-start | bytes 688136 | tf_op jit(solution)/shard_map/ppermute | solution.py:23
  14.2 8.4 %collective-permute-start.5 = (bf16[896,128]{1,0:T(8,128)(2,1)S(1)}, bf16[896,128]{1,0:T(8,128)(2,1)S(1)}, u32[]{:S(2)}, u32[]{:S(2)}) collective-permute-start(bf16[896,128]{1,0:T(8,128)(2,1)S(1)} %collective-permute-done.4.refs_8_), channel_id=1, source_target_pairs={{0,32},{32,0},{64,96},{96,64},{1,33},{33,1},{65,97},{97,65},{2,34}... | collective-permute-start | bytes 688136 | tf_op jit(solution)/shard_map/ppermute | solution.py:23
  26.1 8.8 %collective-permute-start.7 = (f32[256,128]{1,0:T(8,128)S(1)}, f32[256,128]{1,0:T(8,128)S(1)}, u32[]{:S(2)}, u32[]{:S(2)}) collective-permute-start(f32[256,128]{1,0:T(8,128)S(1)} %get-tuple-element.49), channel_id=1, source_target_pairs={{0,1},{1,0},{2,3},{3,2},{4,5},{5,4},{6,7},{7,6},{8,9},{9,8},{10,11... | collective-permute-start | bytes 393224 | tf_op jit(solution)/shard_map/ppermute | solution.py:23
  27.7 25.0 %collective-permute-start.12 = (s16[3184,128]{1,0:T(8,128)(2,1)S(1)}, s16[3184,128]{1,0:T(8,128)(2,1)S(1)}, u32[]{:S(2)}, u32[]{:S(2)}) collective-permute-start(s16[3184,128]{1,0:T(8,128)(2,1)S(1)} %get-tuple-element.54), channel_id=1, source_target_pairs={{0,1},{1,0},{2,3},{3,2},{4,5},{5,4},{6,7},{7,6},{8,9},{9,8},{10,11... | collective-permute-start | bytes 2445320 | tf_op jit(solution)/shard_map/ppermute | solution.py:23
  34.9 7.3 %collective-permute-start.10 = (f32[256,128]{1,0:T(8,128)S(1)}, f32[256,128]{1,0:T(8,128)S(1)}, u32[]{:S(2)}, u32[]{:S(2)}) collective-permute-start(f32[256,128]{1,0:T(8,128)S(1)} %add.3.block_0), channel_id=1, source_target_pairs={{0,64},{32,96},{64,0},{96,32},{1,65},{33,97},{65,1},{97,33},{2,66}... | collective-permute-start | bytes 393224 | tf_op jit(solution)/shard_map/ppermute | solution.py:23
  38.5 14.3 %collective-permute-start.6 = (s16[400,768]{1,0:T(8,128)(2,1)S(1)}, s16[400,768]{1,0:T(8,128)(2,1)S(1)}, u32[]{:S(2)}, u32[]{:S(2)}) collective-permute-start(s16[400,768]{1,0:T(8,128)(2,1)S(1)} %shard_map.129), channel_id=1, source_target_pairs={{0,3},{1,2},{2,1},{3,0},{4,7},{5,6},{6,5},{7,4},{8,11},{9,10},{10,... | collective-permute-start | bytes 1843208 | tf_op jit(solution)/shard_map/ppermute | solution.py:23
  43.5 9.3 %collective-permute-start.11 = (f32[1024,128]{1,0:T(8,128)S(1)}, f32[1024,128]{1,0:T(8,128)S(1)}, u32[]{:S(2)}, u32[]{:S(2)}) collective-permute-start(f32[1024,128]{1,0:T(8,128)S(1)} %pad_maximum_fusion), channel_id=1, source_target_pairs={{0,128},{128,0},{1,129},{129,1},{2,130},{130,2},{3,131},{131,3},{4... | collective-permute-start | bytes 1572872 | tf_op jit(solution)/shard_map/ppermute | solution.py:23
  43.6 26.1 %collective-permute-start.15 = (s16[400,768]{1,0:T(8,128)(2,1)S(1)}, s16[400,768]{1,0:T(8,128)(2,1)S(1)}, u32[]{:S(2)}, u32[]{:S(2)}) collective-permute-start(s16[400,768]{1,0:T(8,128)(2,1)S(1)} %shard_map.130), channel_id=1, source_target_pairs={{0,1},{1,0},{2,3},{3,2},{4,5},{5,4},{6,7},{7,6},{8,9},{9,8},{10,11... | collective-permute-start | bytes 1843208 | tf_op jit(solution)/shard_map/ppermute | solution.py:23
  53.0 14.0 %collective-permute-start.14 = (bf16[1536,128]{1,0:T(8,128)(2,1)S(1)}, bf16[1536,128]{1,0:T(8,128)(2,1)S(1)}, u32[]{:S(2)}, u32[]{:S(2)}) collective-permute-start(bf16[1536,128]{1,0:T(8,128)(2,1)S(1)} %get-tuple-element.55.own), channel_id=1, source_target_pairs={{0,96},{32,64},{64,32},{96,0},{1,97},{33,65},{65,33},{97,1},{2,98}... | collective-permute-start | bytes 1179656 | tf_op jit(solution)/shard_map/ppermute | solution.py:23
  55.4 11.6 %collective-permute-start.13 = (bf16[1536,128]{1,0:T(8,128)(2,1)S(1)}, bf16[1536,128]{1,0:T(8,128)(2,1)S(1)}, u32[]{:S(2)}, u32[]{:S(2)}) collective-permute-start(bf16[1536,128]{1,0:T(8,128)(2,1)S(1)} %get-tuple-element.55.own), channel_id=1, source_target_pairs={{0,32},{32,0},{64,96},{96,64},{1,33},{33,1},{65,97},{97,65},{2,34}... | collective-permute-start | bytes 1179656 | tf_op jit(solution)/shard_map/ppermute | solution.py:23
  56.0 26.6 %collective-permute-start.16 = (bf16[3072,128]{1,0:T(8,128)(2,1)S(1)}, bf16[3072,128]{1,0:T(8,128)(2,1)S(1)}, u32[]{:S(2)}, u32[]{:S(2)}) collective-permute-start(bf16[3072,128]{1,0:T(8,128)(2,1)S(1)} %get-tuple-element.64.mine), channel_id=1, source_target_pairs={{0,3},{1,2},{2,1},{3,0},{4,7},{5,6},{6,5},{7,4},{8,11},{9,10},{10,... | collective-permute-start | bytes 2359304 | tf_op jit(solution)/shard_map/ppermute | solution.py:23
  66.9 17.9 %collective-permute-start.22 = (s16[400,768]{1,0:T(8,128)(2,1)S(1)}, s16[400,768]{1,0:T(8,128)(2,1)S(1)}, u32[]{:S(2)}, u32[]{:S(2)}) collective-permute-start(s16[400,768]{1,0:T(8,128)(2,1)S(1)} %get-tuple-element.59), channel_id=1, source_target_pairs={{0,1},{1,0},{2,3},{3,2},{4,5},{5,4},{6,7},{7,6},{8,9},{9,8},{10,11... | collective-permute-start | bytes 1843208 | tf_op jit(solution)/shard_map/ppermute | solution.py:23
  68.6 7.9 %collective-permute-start.18 = (bf16[768,128]{1,0:T(8,128)(2,1)S(1)}, bf16[768,128]{1,0:T(8,128)(2,1)S(1)}, u32[]{:S(2)}, u32[]{:S(2)}) collective-permute-start(bf16[768,128]{1,0:T(8,128)(2,1)S(1)} %get-tuple-element.61), channel_id=1, source_target_pairs={{0,96},{32,64},{64,32},{96,0},{1,97},{33,65},{65,33},{97,1},{2,98}... | collective-permute-start | bytes 589832 | tf_op jit(solution)/shard_map/ppermute | solution.py:23
  69.7 12.8 %collective-permute-start.17 = (bf16[256,512]{1,0:T(8,128)(2,1)S(1)}, bf16[256,512]{1,0:T(8,128)(2,1)S(1)}, u32[]{:S(2)}, u32[]{:S(2)}) collective-permute-start(bf16[256,512]{1,0:T(8,128)(2,1)S(1)} %get-tuple-element.65), channel_id=1, source_target_pairs={{0,3},{1,2},{2,1},{3,0},{4,7},{5,6},{6,5},{7,4},{8,11},{9,10},{10,... | collective-permute-start | bytes 786440 | tf_op jit(solution)/shard_map/ppermute | solution.py:23
  73.4 18.3 %collective-permute-start.24 = (s16[400,768]{1,0:T(8,128)(2,1)S(1)}, s16[400,768]{1,0:T(8,128)(2,1)S(1)}, u32[]{:S(2)}, u32[]{:S(2)}) collective-permute-start(s16[400,768]{1,0:T(8,128)(2,1)S(1)} %get-tuple-element.67), channel_id=1, source_target_pairs={{0,3},{1,2},{2,1},{3,0},{4,7},{5,6},{6,5},{7,4},{8,11},{9,10},{10,... | collective-permute-start | bytes 1843208 | tf_op jit(solution)/shard_map/ppermute | solution.py:23
  82.6 9.1 %collective-permute-start.21 = (bf16[1536,128]{1,0:T(8,128)(2,1)S(1)}, bf16[1536,128]{1,0:T(8,128)(2,1)S(1)}, u32[]{:S(2)}, u32[]{:S(2)}) collective-permute-start(bf16[1536,128]{1,0:T(8,128)(2,1)S(1)} %get-tuple-element.70.own), channel_id=1, source_target_pairs={{0,96},{32,64},{64,32},{96,0},{1,97},{33,65},{65,33},{97,1},{2,98}... | collective-permute-start | bytes 1179656 | tf_op jit(solution)/shard_map/ppermute | solution.py:23
  83.9 7.8 %collective-permute-start.20 = (bf16[1536,128]{1,0:T(8,128)(2,1)S(1)}, bf16[1536,128]{1,0:T(8,128)(2,1)S(1)}, u32[]{:S(2)}, u32[]{:S(2)}) collective-permute-start(bf16[1536,128]{1,0:T(8,128)(2,1)S(1)} %get-tuple-element.70.own), channel_id=1, source_target_pairs={{0,32},{32,0},{64,96},{96,64},{1,33},{33,1},{65,97},{97,65},{2,34}... | collective-permute-start | bytes 1179656 | tf_op jit(solution)/shard_map/ppermute | solution.py:23
  84.8 11.4 %collective-permute-start.29 = (bf16[3072,128]{1,0:T(8,128)(2,1)S(1)}, bf16[3072,128]{1,0:T(8,128)(2,1)S(1)}, u32[]{:S(2)}, u32[]{:S(2)}) collective-permute-start(bf16[3072,128]{1,0:T(8,128)(2,1)S(1)} %get-tuple-element.72.rights), channel_id=1, source_target_pairs={{0,128},{128,0},{1,129},{129,1},{2,130},{130,2},{3,131},{131,3},{4... | collective-permute-start | bytes 2359304 | tf_op jit(solution)/shard_map/ppermute | solution.py:23
  86.3 18.1 %collective-permute-start.26 = (s16[400,768]{1,0:T(8,128)(2,1)S(1)}, s16[400,768]{1,0:T(8,128)(2,1)S(1)}, u32[]{:S(2)}, u32[]{:S(2)}) collective-permute-start(s16[400,768]{1,0:T(8,128)(2,1)S(1)} %get-tuple-element.74), channel_id=1, source_target_pairs={{0,3},{1,2},{2,1},{3,0},{4,7},{5,6},{6,5},{7,4},{8,11},{9,10},{10,... | collective-permute-start | bytes 1843208 | tf_op jit(solution)/shard_map/ppermute | solution.py:23
  92.4 13.9 %collective-permute-start.25 = (s16[400,768]{1,0:T(8,128)(2,1)S(1)}, s16[400,768]{1,0:T(8,128)(2,1)S(1)}, u32[]{:S(2)}, u32[]{:S(2)}) collective-permute-start(s16[400,768]{1,0:T(8,128)(2,1)S(1)} %get-tuple-element.80), channel_id=1, source_target_pairs={{0,1},{1,0},{2,3},{3,2},{4,5},{5,4},{6,7},{7,6},{8,9},{9,8},{10,11... | collective-permute-start | bytes 1843208 | tf_op jit(solution)/shard_map/ppermute | solution.py:23
  (9 other events, 80.9 us)

commit v4 on v3

--- a/solution.py
+++ b/solution.py
@@ -361,12 +361,13 @@
         )
 
     (give_1,) = corner(corner_give_kernel, lambda at: 3 - at[3], [], panel)
-    (give_0,) = corner(corner_give_kernel, lambda at: 1 - at[2], [], after(panel, give_1))
     step_1 = swapped(give_1, "depth", 3)
+
+    pivot_pair = pivot + after(swapped(pivot, "depth", 1), give_1)
+    pivots = [pivot_pair, *ring_gather(pivot_pair, "col")]
+    (give_0,) = corner(corner_give_kernel, lambda at: 1 - at[2], [], after(panel, pivot_pair))
     step_0 = swapped(give_0, "depth", 1)
-
-    pivot_pair = pivot + after(swapped(pivot, "depth", 1), give_0)
-    pivots = [pivot_pair, *ring_gather(pivot_pair, "col")]
+    pivots = lax.optimization_barrier((pivots, give_0))[0]
     pivots_across = swapped(jnp.concatenate(pivots, axis=0), "row", 1)
 
     both_mine, below_mine = call(

time: 112 us -> 110 us (0.982)
  waiting for transfers between devices: 28.6 us -> 25.3 us
    ppermute x30, waiting for transfers between devices: 28.6 us -> 25.3 us  [swapped(): return lax.ppermute(block, axis, route)]
where the time goes in v4:
time: 110 us; the launch traced here: 109 us
  starting transfers between devices  40.2 us (37%)
  Pallas kernels  35.4 us (32%)
  waiting for transfers between devices  25.3 us (23%)
  blocking collectives  4.47 us (4%)
  local copies, waits for them, and re-layouts  1.94 us (2%)
    ppermute x30, starting transfers between devices, swapped(): return lax.ppermute(block, axis, route)  40.2 us
    pallas_call x17, Pallas kernels, call(): pl.pallas_call(kernel, out_shape=list(outs), compiler_params=pltpu.Compil...  35.4 us
    ppermute x30, waiting for transfers between devices, swapped(): return lax.ppermute(block, axis, route)  25.3 us
    all_gather x1, blocking collectives, body(): far_all = lax.all_gather(upper_grand[0], 'row', axis=0, tiled=True)  2.36 us
  transfers between devices with their start and end apart: 30, of which 13 were waited for; matrix products, arithmetic and copies ran while one was open for 2% of the time, Pallas kernels for 24%

profile of v4, /device:TPU:96, one launch (start us, length us, event | category | flops | bytes accessed | tf_op | source)
XLA Modules:
  0.0 109.2 jit_solution(17518039011174372431)
XLA Ops:
  4.4 2.2 %collective-permute-start.4 = (bf16[896,128]{1,0:T(8,128)(2,1)S(1)}, bf16[896,128]{1,0:T(8,128)(2,1)S(1)}, u32[]{:S(2)}, u32[]{:S(2)}) collective-permute-start(bf16[896,128]{1,0:T(8,128)(2,1)S(1)} %pad_maximum_fusion.1.refs_6_), channel_id=1, source_target_pairs={{0,96},{32,64},{64,32},{96,0},{1,97},{33,65},{65,33},{97,1},{2,98}... | collective-permute-start | bytes 688136 | tf_op jit(solution)/shard_map/ppermute | solution.py:23
  10.6 2.1 %collective-permute-start.2 = (bf16[896,128]{1,0:T(8,128)(2,1)S(1)}, bf16[896,128]{1,0:T(8,128)(2,1)S(1)}, u32[]{:S(2)}, u32[]{:S(2)}) collective-permute-start(bf16[896,128]{1,0:T(8,128)(2,1)S(1)} %collective-permute-done.refs_3_), channel_id=1, source_target_pairs={{0,96},{32,64},{64,32},{96,0},{1,97},{33,65},{65,33},{97,1},{2,98}... | collective-permute-start | bytes 688136 | tf_op jit(solution)/shard_map/ppermute | solution.py:23
  14.2 2.4 %all-gather.1 = bf16[1,512,768]{2,1,0:T(8,128)(2,1)S(1)} all-gather(bf16[1,256,768]{2,1,0:T(8,128)(2,1)S(1)} %copy-done.2), channel_id=3, replica_groups=mesh['row'=2,'col'=4,'depth'=32] {'row'}, dimensions={1}, use_global_device_ids=true | all-gather | bytes 1179648 | tf_op jit(solution)/shard_map/all_gather | solution.py:302
  16.6 2.3 %shard_map.127 = (bf16[512,512]{1,0:T(8,128)(2,1)S(1)}, bf16[512,896]{1,0:T(8,128)(2,1)S(1)}) custom-call(s32[4]{0:T(128)S(1)} %pad_add_fusion.at.refs_0_, s32[1]{0:T(128)S(6)} %copy.14.live, s32[1,24]{1,0:T(1,128)S(1)} %copy-done, s32[1,512]{1,0:T(1,128)S(1)} %copy-done.1, bf16[512,512]{1,0:T(8,128)(2,1)} %bitcast.28, bf16[512,512]{1,0:T(8,128)(2,1)} %bitcast.29, ...), custom_call_target="tpu_custom_call" | custom-call | flops 738197504 | bytes 3410036 | tf_op jit(solution)/shard_map/pallas_call | solution.py:57
  19.1 3.4 %collective-permute-done.2.refs_5_ = bf16[896,128]{1,0:T(8,128)(2,1)S(1)} collective-permute-done((bf16[896,128]{1,0:T(8,128)(2,1)S(1)}, bf16[896,128]{1,0:T(8,128)(2,1)S(1)}, u32[]{:S(2)}, u32[]{:S(2)}) %collective-permute-start.2) | collective-permute-done | bytes 229408 | tf_op jit(solution)/shard_map/ppermute | solution.py:23
  22.6 3.5 %shard_map.128 = (bf16[1536,512]{1,0:T(8,128)(2,1)S(1)}, f32[256,768]{1,0:T(8,128)S(1)}, f32[256,128]{1,0:T(8,128)S(1)}, f32[1536,128]{1,0:T(8,128)S(1)}, s16[3184,128]{1,0:T(8,128)(2,1)S(1)}) custom-call(s32[4]{0:T(128)S(1)} %pad_add_fusion.at.refs_0_, s32[1,24]{1,0:T(1,128)S(1)} %copy-done, bf16[896,128]{1,0:T(8,128)(2,1)S(1)} %slice_bitcast_fusion.refs_2_, ...), custom_call_target="tpu_custom_call" | custom-call | flops 1174405120 | bytes 9072752 | tf_op jit(solution)/shard_map/pallas_call | solution.py:57
  28.2 3.3 %shard_map.129 = s16[400,768]{1,0:T(8,128)(2,1)S(1)} custom-call(s32[4]{0:T(128)S(1)} %pad_add_fusion.at.refs_0_, bf16[1536,512]{1,0:T(8,128)(2,1)S(1)} %get-tuple-element.70.panel, bf16[512,896]{1,0:T(8,128)(2,1)S(1)} %get-tuple-element.50.refs_11_.far, f32[1536,768]{1,0:T(8,128)} %bitcast.20), custom_call_target="tpu_custom_call" | custom-call | flops 301989888 | bytes 7823376 | tf_op jit(solution)/shard_map/pallas_call | solution.py:57
  36.2 3.0 %collective-permute-start.6 = (s16[400,768]{1,0:T(8,128)(2,1)S(1)}, s16[400,768]{1,0:T(8,128)(2,1)S(1)}, u32[]{:S(2)}, u32[]{:S(2)}) collective-permute-start(s16[400,768]{1,0:T(8,128)(2,1)S(1)} %shard_map.129), channel_id=1, source_target_pairs={{0,3},{1,2},{2,1},{3,0},{4,7},{5,6},{6,5},{7,4},{8,11},{9,10},{10,... | collective-permute-start | bytes 1843208 | tf_op jit(solution)/shard_map/ppermute | solution.py:23
  39.2 3.3 %shard_map.130 = s16[400,768]{1,0:T(8,128)(2,1)S(1)} custom-call(s32[4]{0:T(128)S(1)} %pad_add_fusion.at.refs_0_, bf16[1536,512]{1,0:T(8,128)(2,1)S(1)} %get-tuple-element.70.panel, bf16[512,896]{1,0:T(8,128)(2,1)S(1)} %get-tuple-element.50.refs_11_.far, f32[1536,768]{1,0:T(8,128)} %bitcast.21), custom_call_target="tpu_custom_call" | custom-call | flops 301989888 | bytes 7823376 | tf_op jit(solution)/shard_map/pallas_call | solution.py:57
  43.0 6.5 %collective-permute-done.6.came = s16[400,768]{1,0:T(8,128)(2,1)S(1)} collective-permute-done((s16[400,768]{1,0:T(8,128)(2,1)S(1)}, s16[400,768]{1,0:T(8,128)(2,1)S(1)}, u32[]{:S(2)}, u32[]{:S(2)}) %collective-permute-start.6) | collective-permute-done | bytes 614432 | tf_op jit(solution)/shard_map/ppermute | solution.py:23
  49.7 2.4 %collective-permute-start.14 = (bf16[1536,128]{1,0:T(8,128)(2,1)S(1)}, bf16[1536,128]{1,0:T(8,128)(2,1)S(1)}, u32[]{:S(2)}, u32[]{:S(2)}) collective-permute-start(bf16[1536,128]{1,0:T(8,128)(2,1)S(1)} %get-tuple-element.63.own), channel_id=1, source_target_pairs={{0,96},{32,64},{64,32},{96,0},{1,97},{33,65},{65,33},{97,1},{2,98}... | collective-permute-start | bytes 1179656 | tf_op jit(solution)/shard_map/ppermute | solution.py:23
  52.6 3.1 %collective-permute-start.16 = (bf16[3072,128]{1,0:T(8,128)(2,1)S(1)}, bf16[3072,128]{1,0:T(8,128)(2,1)S(1)}, u32[]{:S(2)}, u32[]{:S(2)}) collective-permute-start(bf16[3072,128]{1,0:T(8,128)(2,1)S(1)} %get-tuple-element.72.mine), channel_id=1, source_target_pairs={{0,3},{1,2},{2,1},{3,0},{4,7},{5,6},{6,5},{7,4},{8,11},{9,10},{10,... | collective-permute-start | bytes 2359304 | tf_op jit(solution)/shard_map/ppermute | solution.py:23
  55.7 4.5 %shard_map.132 = (bf16[512,512]{1,0:T(8,128)(2,1)S(1)}, bf16[256,512]{1,0:T(8,128)(2,1)S(1)}) custom-call(s32[4]{0:T(128)S(1)} %pad_add_fusion.at.refs_0_, f32[256,128]{1,0:T(8,128)S(1)} %add.3.block_0, f32[256,128]{1,0:T(8,128)S(1)} %collective-permute-done.8.block_1, f32[256,128]{1,0:T(8,128)S(1)} %collective-permute-done.9.block_3, ...), custom_call_target="tpu_custom_call" | custom-call | flops 3221225472 | bytes 1835024 | tf_op jit(solution)/shard_map/pallas_call | solution.py:57
  60.3 3.4 %shard_map.133 = (f32[384,768]{1,0:T(8,128)S(1)}, s16[400,768]{1,0:T(8,128)(2,1)S(1)}) custom-call(s32[4]{0:T(128)S(1)} %pad_add_fusion.at.refs_0_, bf16[1536,512]{1,0:T(8,128)(2,1)S(1)} %get-tuple-element.70.panel, bf16[512,896]{1,0:T(8,128)(2,1)S(1)} %get-tuple-element.50.refs_11_.far, f32[1536,768]{1,0:T(8,128)} %bitcast.22, ...), custom_call_target="tpu_custom_call" | custom-call | flops 301989888 | bytes 9617424 | tf_op jit(solution)/shard_map/pallas_call | solution.py:57
  63.9 2.1 %collective-permute-start.19 = (bf16[768,128]{1,0:T(8,128)(2,1)S(1)}, bf16[768,128]{1,0:T(8,128)(2,1)S(1)}, u32[]{:S(2)}, u32[]{:S(2)}) collective-permute-start(bf16[768,128]{1,0:T(8,128)(2,1)S(1)} %get-tuple-element.74), channel_id=1, source_target_pairs={{0,32},{32,0},{64,96},{96,64},{1,33},{33,1},{65,97},{97,65},{2,34}... | collective-permute-start | bytes 589832 | tf_op jit(solution)/shard_map/ppermute | solution.py:23
  68.3 3.4 %shard_map.135 = (f32[384,768]{1,0:T(8,128)S(1)}, s16[400,768]{1,0:T(8,128)(2,1)S(1)}) custom-call(s32[4]{0:T(128)S(1)} %pad_add_fusion.at.refs_0_, bf16[1536,512]{1,0:T(8,128)(2,1)S(1)} %get-tuple-element.70.panel, bf16[512,896]{1,0:T(8,128)(2,1)S(1)} %get-tuple-element.50.refs_11_.far, f32[1536,768]{1,0:T(8,128)} %bitcast.23, ...), custom_call_target="tpu_custom_call" | custom-call | flops 301989888 | bytes 9617424 | tf_op jit(solution)/shard_map/pallas_call | solution.py:57
  71.7 2.3 %collective-permute-start.24 = (s16[400,768]{1,0:T(8,128)(2,1)S(1)}, s16[400,768]{1,0:T(8,128)(2,1)S(1)}, u32[]{:S(2)}, u32[]{:S(2)}) collective-permute-start(s16[400,768]{1,0:T(8,128)(2,1)S(1)} %get-tuple-element.75), channel_id=1, source_target_pairs={{0,3},{1,2},{2,1},{3,0},{4,7},{5,6},{6,5},{7,4},{8,11},{9,10},{10,... | collective-permute-start | bytes 1843208 | tf_op jit(solution)/shard_map/ppermute | solution.py:23
  75.7 3.3 %collective-permute-done.17.rest_0_ = bf16[256,512]{1,0:T(8,128)(2,1)S(1)} collective-permute-done((bf16[256,512]{1,0:T(8,128)(2,1)S(1)}, bf16[256,512]{1,0:T(8,128)(2,1)S(1)}, u32[]{:S(2)}, u32[]{:S(2)}) %collective-permute-start.17) | collective-permute-done | bytes 262176 | tf_op jit(solution)/shard_map/ppermute | solution.py:23
  83.6 3.7 %collective-permute-start.26 = (s16[400,768]{1,0:T(8,128)(2,1)S(1)}, s16[400,768]{1,0:T(8,128)(2,1)S(1)}, u32[]{:S(2)}, u32[]{:S(2)}) collective-permute-start(s16[400,768]{1,0:T(8,128)(2,1)S(1)} %get-tuple-element.82), channel_id=1, source_target_pairs={{0,3},{1,2},{2,1},{3,0},{4,7},{5,6},{6,5},{7,4},{8,11},{9,10},{10,... | collective-permute-start | bytes 1843208 | tf_op jit(solution)/shard_map/ppermute | solution.py:23
  89.2 3.2 %collective-permute-start.28 = (bf16[768,128]{1,0:T(8,128)(2,1)S(1)}, bf16[768,128]{1,0:T(8,128)(2,1)S(1)}, u32[]{:S(2)}, u32[]{:S(2)}) collective-permute-start(bf16[768,128]{1,0:T(8,128)(2,1)S(1)} %get-tuple-element.90), channel_id=1, source_target_pairs={{0,32},{32,0},{64,96},{96,64},{1,33},{33,1},{65,97},{97,65},{2,34}... | collective-permute-start | bytes 589832 | tf_op jit(solution)/shard_map/ppermute | solution.py:23
  93.9 2.1 %collective-permute-done.28.across_1 = bf16[768,128]{1,0:T(8,128)(2,1)S(1)} collective-permute-done((bf16[768,128]{1,0:T(8,128)(2,1)S(1)}, bf16[768,128]{1,0:T(8,128)(2,1)S(1)}, u32[]{:S(2)}, u32[]{:S(2)}) %collective-permute-start.28) | collective-permute-done | bytes 196640 | tf_op jit(solution)/shard_map/ppermute | solution.py:23
  96.1 3.2 %collective-permute-done.27.across_0 = bf16[768,128]{1,0:T(8,128)(2,1)S(1)} collective-permute-done((bf16[768,128]{1,0:T(8,128)(2,1)S(1)}, bf16[768,128]{1,0:T(8,128)(2,1)S(1)}, u32[]{:S(2)}, u32[]{:S(2)}) %collective-permute-start.27) | collective-permute-done | bytes 196640 | tf_op jit(solution)/shard_map/ppermute | solution.py:23
  101.4 2.3 %collective-permute-done.25.came_0 = s16[400,768]{1,0:T(8,128)(2,1)S(1)} collective-permute-done((s16[400,768]{1,0:T(8,128)(2,1)S(1)}, s16[400,768]{1,0:T(8,128)(2,1)S(1)}, u32[]{:S(2)}, u32[]{:S(2)}) %collective-permute-start.25) | collective-permute-done | bytes 614432 | tf_op jit(solution)/shard_map/ppermute | solution.py:23
  103.7 5.5 %shard_map.143 = f32[1536,768]{1,0:T(8,128)} custom-call(s32[4]{0:T(128)S(1)} %pad_add_fusion.at.refs_0_, f32[384,768]{1,0:T(8,128)S(1)} %get-tuple-element.87.own_0, s16[400,768]{1,0:T(8,128)(2,1)S(1)} %collective-permute-done.25.came_0, f32[384,768]{1,0:T(8,128)S(1)} %get-tuple-element.89.own_1, s16[400,768]{1,0:T(8,128)(2,1)S(1)} %collective-permute-done.26.came_1, ...), custom_call_target="tpu_custom_call" | custom-call | flops 2415919104 | bytes 13025296 | tf_op jit(solution)/shard_map/pallas_call | solution.py:57
  (67 shorter events, 31.8 us)
Async XLA Ops:
  1.0 9.5 %collective-permute-start = (bf16[896,128]{1,0:T(8,128)(2,1)S(1)}, bf16[896,128]{1,0:T(8,128)(2,1)S(1)}, u32[]{:S(2)}, u32[]{:S(2)}) collective-permute-start(bf16[896,128]{1,0:T(8,128)(2,1)S(1)} %slice_bitcast_fusion.refs_2_), channel_id=1, source_target_pairs={{0,32},{32,0},{64,96},{96,64},{1,33},{33,1},{65,97},{97,65},{2,34}... | collective-permute-start | bytes 688136 | tf_op jit(solution)/shard_map/ppermute | solution.py:23
  4.4 9.8 %collective-permute-start.4 = (bf16[896,128]{1,0:T(8,128)(2,1)S(1)}, bf16[896,128]{1,0:T(8,128)(2,1)S(1)}, u32[]{:S(2)}, u32[]{:S(2)}) collective-permute-start(bf16[896,128]{1,0:T(8,128)(2,1)S(1)} %pad_maximum_fusion.1.refs_6_), channel_id=1, source_target_pairs={{0,96},{32,64},{64,32},{96,0},{1,97},{33,65},{65,33},{97,1},{2,98}... | collective-permute-start | bytes 688136 | tf_op jit(solution)/shard_map/ppermute | solution.py:23
  6.6 12.6 %collective-permute-start.1 = (bf16[896,128]{1,0:T(8,128)(2,1)S(1)}, bf16[896,128]{1,0:T(8,128)(2,1)S(1)}, u32[]{:S(2)}, u32[]{:S(2)}) collective-permute-start(bf16[896,128]{1,0:T(8,128)(2,1)S(1)} %slice_bitcast_fusion.refs_2_), channel_id=1, source_target_pairs={{0,96},{32,64},{64,32},{96,0},{1,97},{33,65},{65,33},{97,1},{2,98}... | collective-permute-start | bytes 688136 | tf_op jit(solution)/shard_map/ppermute | solution.py:23
  7.7 11.4 %collective-permute-start.3 = (bf16[896,128]{1,0:T(8,128)(2,1)S(1)}, bf16[896,128]{1,0:T(8,128)(2,1)S(1)}, u32[]{:S(2)}, u32[]{:S(2)}) collective-permute-start(bf16[896,128]{1,0:T(8,128)(2,1)S(1)} %pad_maximum_fusion.1.refs_6_), channel_id=1, source_target_pairs={{0,32},{32,0},{64,96},{96,64},{1,33},{33,1},{65,97},{97,65},{2,34}... | collective-permute-start | bytes 688136 | tf_op jit(solution)/shard_map/ppermute | solution.py:23
  10.6 12.0 %collective-permute-start.2 = (bf16[896,128]{1,0:T(8,128)(2,1)S(1)}, bf16[896,128]{1,0:T(8,128)(2,1)S(1)}, u32[]{:S(2)}, u32[]{:S(2)}) collective-permute-start(bf16[896,128]{1,0:T(8,128)(2,1)S(1)} %collective-permute-done.refs_3_), channel_id=1, source_target_pairs={{0,96},{32,64},{64,32},{96,0},{1,97},{33,65},{65,33},{97,1},{2,98}... | collective-permute-start | bytes 688136 | tf_op jit(solution)/shard_map/ppermute | solution.py:23
  14.2 8.4 %collective-permute-start.5 = (bf16[896,128]{1,0:T(8,128)(2,1)S(1)}, bf16[896,128]{1,0:T(8,128)(2,1)S(1)}, u32[]{:S(2)}, u32[]{:S(2)}) collective-permute-start(bf16[896,128]{1,0:T(8,128)(2,1)S(1)} %collective-permute-done.4.refs_8_), channel_id=1, source_target_pairs={{0,32},{32,0},{64,96},{96,64},{1,33},{33,1},{65,97},{97,65},{2,34}... | collective-permute-start | bytes 688136 | tf_op jit(solution)/shard_map/ppermute | solution.py:23
  27.7 21.7 %collective-permute-start.12 = (s16[3184,128]{1,0:T(8,128)(2,1)S(1)}, s16[3184,128]{1,0:T(8,128)(2,1)S(1)}, u32[]{:S(2)}, u32[]{:S(2)}) collective-permute-start(s16[3184,128]{1,0:T(8,128)(2,1)S(1)} %get-tuple-element.62), channel_id=1, source_target_pairs={{0,1},{1,0},{2,3},{3,2},{4,5},{5,4},{6,7},{7,6},{8,9},{9,8},{10,11... | collective-permute-start | bytes 2445320 | tf_op jit(solution)/shard_map/ppermute | solution.py:23
  32.6 9.9 %collective-permute-start.10 = (f32[256,128]{1,0:T(8,128)S(1)}, f32[256,128]{1,0:T(8,128)S(1)}, u32[]{:S(2)}, u32[]{:S(2)}) collective-permute-start(f32[256,128]{1,0:T(8,128)S(1)} %add.3.block_0), channel_id=1, source_target_pairs={{0,64},{32,96},{64,0},{96,32},{1,65},{33,97},{65,1},{97,33},{2,66}... | collective-permute-start | bytes 393224 | tf_op jit(solution)/shard_map/ppermute | solution.py:23
  34.2 8.3 %collective-permute-start.9 = (f32[256,128]{1,0:T(8,128)S(1)}, f32[256,128]{1,0:T(8,128)S(1)}, u32[]{:S(2)}, u32[]{:S(2)}) collective-permute-start(f32[256,128]{1,0:T(8,128)S(1)} %add.3.block_0), channel_id=1, source_target_pairs={{0,96},{32,64},{64,32},{96,0},{1,97},{33,65},{65,33},{97,1},{2,98}... | collective-permute-start | bytes 393224 | tf_op jit(solution)/shard_map/ppermute | solution.py:23
  36.2 13.2 %collective-permute-start.6 = (s16[400,768]{1,0:T(8,128)(2,1)S(1)}, s16[400,768]{1,0:T(8,128)(2,1)S(1)}, u32[]{:S(2)}, u32[]{:S(2)}) collective-permute-start(s16[400,768]{1,0:T(8,128)(2,1)S(1)} %shard_map.129), channel_id=1, source_target_pairs={{0,3},{1,2},{2,1},{3,0},{4,7},{5,6},{6,5},{7,4},{8,11},{9,10},{10,... | collective-permute-start | bytes 1843208 | tf_op jit(solution)/shard_map/ppermute | solution.py:23
  42.7 24.5 %collective-permute-start.15 = (s16[400,768]{1,0:T(8,128)(2,1)S(1)}, s16[400,768]{1,0:T(8,128)(2,1)S(1)}, u32[]{:S(2)}, u32[]{:S(2)}) collective-permute-start(s16[400,768]{1,0:T(8,128)(2,1)S(1)} %shard_map.130), channel_id=1, source_target_pairs={{0,1},{1,0},{2,3},{3,2},{4,5},{5,4},{6,7},{7,6},{8,9},{9,8},{10,11... | collective-permute-start | bytes 1843208 | tf_op jit(solution)/shard_map/ppermute | solution.py:23
  49.7 14.2 %collective-permute-start.14 = (bf16[1536,128]{1,0:T(8,128)(2,1)S(1)}, bf16[1536,128]{1,0:T(8,128)(2,1)S(1)}, u32[]{:S(2)}, u32[]{:S(2)}) collective-permute-start(bf16[1536,128]{1,0:T(8,128)(2,1)S(1)} %get-tuple-element.63.own), channel_id=1, source_target_pairs={{0,96},{32,64},{64,32},{96,0},{1,97},{33,65},{65,33},{97,1},{2,98}... | collective-permute-start | bytes 1179656 | tf_op jit(solution)/shard_map/ppermute | solution.py:23
  52.1 11.8 %collective-permute-start.13 = (bf16[1536,128]{1,0:T(8,128)(2,1)S(1)}, bf16[1536,128]{1,0:T(8,128)(2,1)S(1)}, u32[]{:S(2)}, u32[]{:S(2)}) collective-permute-start(bf16[1536,128]{1,0:T(8,128)(2,1)S(1)} %get-tuple-element.63.own), channel_id=1, source_target_pairs={{0,32},{32,0},{64,96},{96,64},{1,33},{33,1},{65,97},{97,65},{2,34}... | collective-permute-start | bytes 1179656 | tf_op jit(solution)/shard_map/ppermute | solution.py:23
  52.6 26.4 %collective-permute-start.16 = (bf16[3072,128]{1,0:T(8,128)(2,1)S(1)}, bf16[3072,128]{1,0:T(8,128)(2,1)S(1)}, u32[]{:S(2)}, u32[]{:S(2)}) collective-permute-start(bf16[3072,128]{1,0:T(8,128)(2,1)S(1)} %get-tuple-element.72.mine), channel_id=1, source_target_pairs={{0,3},{1,2},{2,1},{3,0},{4,7},{5,6},{6,5},{7,4},{8,11},{9,10},{10,... | collective-permute-start | bytes 2359304 | tf_op jit(solution)/shard_map/ppermute | solution.py:23
  63.7 18.4 %collective-permute-start.22 = (s16[400,768]{1,0:T(8,128)(2,1)S(1)}, s16[400,768]{1,0:T(8,128)(2,1)S(1)}, u32[]{:S(2)}, u32[]{:S(2)}) collective-permute-start(s16[400,768]{1,0:T(8,128)(2,1)S(1)} %get-tuple-element.67), channel_id=1, source_target_pairs={{0,1},{1,0},{2,3},{3,2},{4,5},{5,4},{6,7},{7,6},{8,9},{9,8},{10,11... | collective-permute-start | bytes 1843208 | tf_op jit(solution)/shard_map/ppermute | solution.py:23
  63.9 7.7 %collective-permute-start.19 = (bf16[768,128]{1,0:T(8,128)(2,1)S(1)}, bf16[768,128]{1,0:T(8,128)(2,1)S(1)}, u32[]{:S(2)}, u32[]{:S(2)}) collective-permute-start(bf16[768,128]{1,0:T(8,128)(2,1)S(1)} %get-tuple-element.74), channel_id=1, source_target_pairs={{0,32},{32,0},{64,96},{96,64},{1,33},{33,1},{65,97},{97,65},{2,34}... | collective-permute-start | bytes 589832 | tf_op jit(solution)/shard_map/ppermute | solution.py:23
  66.1 7.9 %collective-permute-start.18 = (bf16[768,128]{1,0:T(8,128)(2,1)S(1)}, bf16[768,128]{1,0:T(8,128)(2,1)S(1)}, u32[]{:S(2)}, u32[]{:S(2)}) collective-permute-start(bf16[768,128]{1,0:T(8,128)(2,1)S(1)} %get-tuple-element.69), channel_id=1, source_target_pairs={{0,96},{32,64},{64,32},{96,0},{1,97},{33,65},{65,33},{97,1},{2,98}... | collective-permute-start | bytes 589832 | tf_op jit(solution)/shard_map/ppermute | solution.py:23
  67.2 11.8 %collective-permute-start.17 = (bf16[256,512]{1,0:T(8,128)(2,1)S(1)}, bf16[256,512]{1,0:T(8,128)(2,1)S(1)}, u32[]{:S(2)}, u32[]{:S(2)}) collective-permute-start(bf16[256,512]{1,0:T(8,128)(2,1)S(1)} %get-tuple-element.73), channel_id=1, source_target_pairs={{0,3},{1,2},{2,1},{3,0},{4,7},{5,6},{6,5},{7,4},{8,11},{9,10},{10,... | collective-permute-start | bytes 786440 | tf_op jit(solution)/shard_map/ppermute | solution.py:23
  71.7 16.5 %collective-permute-start.24 = (s16[400,768]{1,0:T(8,128)(2,1)S(1)}, s16[400,768]{1,0:T(8,128)(2,1)S(1)}, u32[]{:S(2)}, u32[]{:S(2)}) collective-permute-start(s16[400,768]{1,0:T(8,128)(2,1)S(1)} %get-tuple-element.75), channel_id=1, source_target_pairs={{0,3},{1,2},{2,1},{3,0},{4,7},{5,6},{6,5},{7,4},{8,11},{9,10},{10,... | collective-permute-start | bytes 1843208 | tf_op jit(solution)/shard_map/ppermute | solution.py:23
  79.1 9.1 %collective-permute-start.21 = (bf16[1536,128]{1,0:T(8,128)(2,1)S(1)}, bf16[1536,128]{1,0:T(8,128)(2,1)S(1)}, u32[]{:S(2)}, u32[]{:S(2)}) collective-permute-start(bf16[1536,128]{1,0:T(8,128)(2,1)S(1)} %get-tuple-element.78.own), channel_id=1, source_target_pairs={{0,96},{32,64},{64,32},{96,0},{1,97},{33,65},{65,33},{97,1},{2,98}... | collective-permute-start | bytes 1179656 | tf_op jit(solution)/shard_map/ppermute | solution.py:23
  79.9 8.2 %collective-permute-start.20 = (bf16[1536,128]{1,0:T(8,128)(2,1)S(1)}, bf16[1536,128]{1,0:T(8,128)(2,1)S(1)}, u32[]{:S(2)}, u32[]{:S(2)}) collective-permute-start(bf16[1536,128]{1,0:T(8,128)(2,1)S(1)} %get-tuple-element.78.own), channel_id=1, source_target_pairs={{0,32},{32,0},{64,96},{96,64},{1,33},{33,1},{65,97},{97,65},{2,34}... | collective-permute-start | bytes 1179656 | tf_op jit(solution)/shard_map/ppermute | solution.py:23
  82.1 11.0 %collective-permute-start.29 = (bf16[3072,128]{1,0:T(8,128)(2,1)S(1)}, bf16[3072,128]{1,0:T(8,128)(2,1)S(1)}, u32[]{:S(2)}, u32[]{:S(2)}) collective-permute-start(bf16[3072,128]{1,0:T(8,128)(2,1)S(1)} %get-tuple-element.80.rights), channel_id=1, source_target_pairs={{0,128},{128,0},{1,129},{129,1},{2,130},{130,2},{3,131},{131,3},{4... | collective-permute-start | bytes 2359304 | tf_op jit(solution)/shard_map/ppermute | solution.py:23
  83.6 17.8 %collective-permute-start.26 = (s16[400,768]{1,0:T(8,128)(2,1)S(1)}, s16[400,768]{1,0:T(8,128)(2,1)S(1)}, u32[]{:S(2)}, u32[]{:S(2)}) collective-permute-start(s16[400,768]{1,0:T(8,128)(2,1)S(1)} %get-tuple-element.82), channel_id=1, source_target_pairs={{0,3},{1,2},{2,1},{3,0},{4,7},{5,6},{6,5},{7,4},{8,11},{9,10},{10,... | collective-permute-start | bytes 1843208 | tf_op jit(solution)/shard_map/ppermute | solution.py:23
  88.9 14.8 %collective-permute-start.25 = (s16[400,768]{1,0:T(8,128)(2,1)S(1)}, s16[400,768]{1,0:T(8,128)(2,1)S(1)}, u32[]{:S(2)}, u32[]{:S(2)}) collective-permute-start(s16[400,768]{1,0:T(8,128)(2,1)S(1)} %get-tuple-element.88), channel_id=1, source_target_pairs={{0,1},{1,0},{2,3},{3,2},{4,5},{5,4},{6,7},{7,6},{8,9},{9,8},{10,11... | collective-permute-start | bytes 1843208 | tf_op jit(solution)/shard_map/ppermute | solution.py:23
  (9 other events, 83.4 us)
